TPU v7x, 256 devices: a whole 4x4x8 slice. The times are simulated.
256 devices in a mesh: band: 8 (over z_hi, core), domain: 32 (over z_lo, x, y).
Axes of the slice: x: 4, y: 4, z: 8 (z_hi: 4, z_lo: 2; z = z_hi * 2 + z_lo), core: 2. Of those that a mesh axis runs over, the one named last changes fastest.
Arguments:
- states: float32 [32, 192, 16, 128], P('band', 'domain'), may hold values from -6 to 6
- potential: float32 [192, 16, 128], P('domain'), may hold values from -10 to 2
- slab: bfloat16 [256, 192, 16, 128], P('band', 'domain'), may hold values from -6 to 6
Outputs:
- gram: float32 [32, 256], P('domain', 'band')
- projected: float32 [32, 256], P('domain', 'band')
All inputs are finite; a program needn't handle non-finite values.
Results may differ from a plain program's by a relative error of at most 0.0045.
Values may be sent and summed in bfloat16 or wider, within the bound.
No kernel may reach another device: no remote copies, remote signals or barrier semaphores. Data moves between devices by JAX's collectives and lax.ppermute only.
A program may use at most 192 MiB of HBM per device.

v0:
```python
import jax
import jax.numpy as jnp
from jax import lax
from jax.sharding import PartitionSpec as P

COEFS = (
    -5369.0 / 1800.0,
    12.0 / 7.0,
    -15.0 / 56.0,
    10.0 / 189.0,
    -1.0 / 112.0,
    2.0 / 1925.0,
    -1.0 / 16632.0,
)
SPACING = 0.5
CENTER = 27.5
HALF = 22.5


def padded_2(array, sides, width):
    for axis, dim in sides:
        size, length = (lax.axis_size(axis), array.shape[dim])
        up = [(i, (i + 1) % size) for i in range(size)]
        down = [(j, i) for i, j in up]
        last = lax.slice_in_dim(array, length - width, length, axis=dim)
        initial = lax.slice_in_dim(array, 0, width, axis=dim)
        before = lax.ppermute(last, axis, up)
        after = lax.ppermute(initial, axis, down)
        array = jnp.concatenate([before, array, after], axis=dim)
    return array


def kinetic(padded, field, potential):
    thick = field.shape[-3]
    total = 3.0 * COEFS[0] * field
    for reach in range(1, 7):
        along = (
            padded[..., 6 + reach : 6 + reach + thick, :, :]
            + padded[..., 6 - reach : 6 - reach + thick, :, :]
        )
        along = along + jnp.roll(field, reach, -2) + jnp.roll(field, -reach, -2)
        along = along + jnp.roll(field, reach, -1) + jnp.roll(field, -reach, -1)
        total = total + COEFS[reach] * along
    return -0.5 / SPACING**2 * total + potential * field


def filter_apply(field, potential):
    padded = padded_2(field, (("domain", 1),), 6)
    return kinetic(padded, field, potential)


def body(states, potential, slab):
    slab_flat = slab.reshape(slab.shape[0], -1)
    slab_count = slab.shape[0]

    def products(block):
        flat = block.reshape(block.shape[0], -1)
        return lax.dot_general(
            flat, slab_flat, (((1,), (1,)), ((), ())), preferred_element_type=jnp.float32
        )

    first = (filter_apply(states, potential) - CENTER * states) / HALF
    second = 2.0 * (filter_apply(first, potential) - CENTER * first) / HALF - states
    rounded = second.astype(jnp.bfloat16)
    thick = states.shape[1]
    gathered = lax.all_gather(rounded, "band", axis=0, tiled=True)
    padded = padded_2(gathered, (("domain", 1),), 6)
    own = padded[:, 6 : 6 + thick].astype(jnp.float32)
    applied = (kinetic(padded.astype(jnp.float32), own, potential) / HALF).astype(jnp.bfloat16)
    term = jnp.concatenate([products(gathered), products(applied)], axis=1)
    domains = lax.axis_size("domain")
    share = lax.psum_scatter(term, "domain", scatter_dimension=0, tiled=True)
    scale = 1.0 / jnp.sqrt(jnp.float32(slab_flat.shape[1] * domains))
    return (share[:, :slab_count] * scale, share[:, slab_count:] * scale)


def solution(mesh):
    placed = (
        P("band", "domain", None, None),
        P("domain", None, None),
        P("band", "domain", None, None),
    )
    return jax.shard_map(
        body,
        mesh=mesh,
        in_specs=placed,
        out_specs=(P("domain", "band"), P("domain", "band")),
        check_vma=False,
    )
```

profile of v0, /device:TPU:32, one launch (start us, length us, event | category | flops | bytes accessed | tf_op | source)
XLA Modules:
  0.0 307.9 jit_solution(11807947044660188579)
XLA Ops:
  0.7 1.7 collective-permute-start.1
  2.3 4.7 %collective-permute-start = (f32[4,6,16,128]{3,2,1,0:T(8,128)}, f32[4,6,16,128]{3,2,1,0:T(8,128)S(1)}, u32[]{:S(2)}, u32[]{:S(2)}) collective-permute-start(f32[4,6,16,128]{3,2,1,0:T(8,128)} %param.3), channel_id=1, source_target_pairs={{1,0},{2,1},{3,2},{4,3},{5,4},{6,5},{7,6},{8,7},{9,8},{10,9},{11,1... | collective-permute-start | bytes 589832 | tf_op jit(solution)/shard_map/ppermute | solution.py:28
  7.0 1.6 fusion.185
  8.6 1.6 fusion.189
  10.1 1.6 fusion.193
  11.7 1.6 fusion.197
  13.3 1.6 fusion.205
  14.9 1.6 fusion.201
  16.9 0.8 fusion.203
  18.5 0.8 fusion.200
  19.4 0.8 fusion.199
  20.2 0.8 fusion.192
  24.9 0.8 fusion.187
  27.3 0.8 fusion.207
  28.1 0.8 fusion.208
  30.3 3.8 %broadcast_multiply_fusion = (f32[4,6,16,128]{3,2,1,0:T(8,128)S(1)}, f32[4,6,16,128]{3,2,1,0:T(8,128)S(1)}) fusion(f32[4,6,16,128]{3,2,1,0:T(8,128)S(1)} %copy-done.1, f32[6,16,128]{2,1,0:T(8,128)} %param.4, f32[4,6,16,6]{3,2,1,0:T(8,128)S(1)} %copy-done.5, f32[4,6,16,122]{3,2,1,0:T(8,128)S(1)} %copy-done.7, f32[4,6,16,122]{3,2,1,0:T(8,128)S(1)} %copy-done.6, ...), kind=kLoop, calls=%fused_computation.170 | loop fusion | flops 3588096 | bytes 7716864 | tf_op jit(solution)/shard_map/div | solution.py:62
  34.3 6.2 %collective-permute-start.2 = (f32[4,6,16,128]{3,2,1,0:T(8,128)S(1)}, f32[4,6,16,128]{3,2,1,0:T(8,128)S(1)}, u32[]{:S(2)}, u32[]{:S(2)}) collective-permute-start(f32[4,6,16,128]{3,2,1,0:T(8,128)S(1)} %get-tuple-element.2), channel_id=1, source_target_pairs={{1,0},{2,1},{3,2},{4,3},{5,4},{6,5},{7,6},{8,7},{9,8},{10,9},{11,1... | collective-permute-start | bytes 589832 | tf_op jit(solution)/shard_map/ppermute | solution.py:28
  42.2 2.4 collective-permute-done.3
  44.6 1.4 fusion.135
  46.0 18.7 %all_gather.3 = bf16[32,6,16,128]{3,2,1,0:T(8,128)(2,1)S(1)} all-gather(bf16[4,6,16,128]{3,2,1,0:T(8,128)(2,1)S(1)} %fusion.135), channel_id=1, replica_groups=mesh['band'=8,'domain'=32] {'band'}, dimensions={0}, use_global_device_ids=true | all-gather | bytes 884736 | tf_op jit(solution)/shard_map/all_gather | solution.py:66
  65.6 0.9 fusion.156
  66.5 0.9 fusion.152
  67.4 1.0 fusion.148
  68.4 5.8 %collective-permute-start.5 = (bf16[32,6,16,128]{3,2,1,0:T(8,128)(2,1)S(1)}, bf16[32,6,16,128]{3,2,1,0:T(8,128)(2,1)S(1)}, u32[]{:S(2)}, u32[]{:S(2)}) collective-permute-start(bf16[32,6,16,128]{3,2,1,0:T(8,128)(2,1)S(1)} %all_gather.3), channel_id=1, source_target_pairs={{1,0},{2,1},{3,2},{4,3},{5,4},{6,5},{7,6},{8,7},{9,8},{10,9},{11,1... | collective-permute-start | bytes 2359304 | tf_op jit(solution)/shard_map/ppermute | solution.py:28
  74.2 1.3 fusion.144
  75.5 1.3 fusion.140
  76.7 1.6 fusion.150
  78.3 2.1 fusion.141
  80.5 2.2 fusion.151
  82.7 2.1 fusion.145
  84.9 2.1 fusion.138
  87.0 2.1 fusion.153
  89.1 2.1 fusion.154
  91.1 2.2 fusion.139
  93.4 2.1 fusion.146
  95.5 2.1 fusion.155
  97.6 2.1 fusion.147
  99.7 2.1 fusion.142
  101.8 2.1 fusion.157
  103.9 2.1 fusion.158
  106.0 2.1 fusion.143
  108.1 2.1 fusion.159
  110.7 2.2 fusion.149
  112.9 2.1 fusion.137
  115.0 2.5 maximum_convert_fusion
  117.5 29.1 %fusion.9 = bf16[32,6,16,128]{3,2,1,0:T(8,128)(2,1)} fusion(f32[32,18,16,128]{3,2,1,0:T(8,128)} %maximum_convert_fusion, f32[32,6,15,128]{3,2,1,0:T(8,128)} %get-tuple-element.49, f32[32,6,1,128]{3,2,1,0:T(1,128)} %get-tuple-element.51, f32[32,6,1,128]{3,2,1,0:T(1,128)} %get-tuple-element.50, f32[32,6,15,128]{3,2,1,0:T(8,128)} %get-tuple-element.48, ...), kind=kLoop, calls=%fused_computation.11 | loop fusion | flops 28704768 | bytes 58245120 | tf_op jit(solution)/shard_map/convert_element_type | solution.py:69
  146.6 1.7 convolution_bitcast_fusion
  148.3 158.3 %all-reduce = f32[32,64]{1,0:T(8,128)S(1)} all-reduce(f32[32,64]{1,0:T(8,128)S(1)} %pad_maximum_fusion.2), channel_id=2, replica_groups=mesh['band'=8,'domain'=32] {'domain'}, use_global_device_ids=true, to_apply=%region_0.1.clone | all-reduce | flops 2048 | bytes 16384
  (72 shorter events, 12.3 us)
Async XLA Ops:
  0.6 109.6 %copy-start = (bf16[32,6,16,128]{3,2,1,0:T(8,128)(2,1)S(1)}, bf16[32,6,16,128]{3,2,1,0:T(8,128)(2,1)}, u32[]{:S(2)}) copy-start(bf16[32,6,16,128]{3,2,1,0:T(8,128)(2,1)} %param.5) | copy-start | bytes 2359300
  0.6 15.9 %copy-start.1 = (f32[4,6,16,128]{3,2,1,0:T(8,128)S(1)}, f32[4,6,16,128]{3,2,1,0:T(8,128)}, u32[]{:S(2)}) copy-start(f32[4,6,16,128]{3,2,1,0:T(8,128)} %param.3) | copy-start | bytes 589828
  0.7 28.9 %collective-permute-start.1 = (f32[4,6,16,128]{3,2,1,0:T(8,128)}, f32[4,6,16,128]{3,2,1,0:T(8,128)S(1)}, u32[]{:S(2)}, u32[]{:S(2)}) collective-permute-start(f32[4,6,16,128]{3,2,1,0:T(8,128)} %param.3), channel_id=1, source_target_pairs={{0,1},{1,2},{2,3},{3,4},{4,5},{5,6},{6,7},{7,8},{8,9},{9,10},{10,1... | collective-permute-start | bytes 589832 | tf_op jit(solution)/shard_map/ppermute | solution.py:27
  2.3 27.3 %collective-permute-start = (f32[4,6,16,128]{3,2,1,0:T(8,128)}, f32[4,6,16,128]{3,2,1,0:T(8,128)S(1)}, u32[]{:S(2)}, u32[]{:S(2)}) collective-permute-start(f32[4,6,16,128]{3,2,1,0:T(8,128)} %param.3), channel_id=1, source_target_pairs={{1,0},{2,1},{3,2},{4,3},{5,4},{6,5},{7,6},{8,7},{9,8},{10,9},{11,1... | collective-permute-start | bytes 589832 | tf_op jit(solution)/shard_map/ppermute | solution.py:28
  25.7 3.2 %copy-start.9 = (u32[256]{0:T(256)S(1)}, u32[256]{0:T(256)}, u32[]{:S(2)}) copy-start(u32[256]{0:T(256)} %constant.46) | copy-start | bytes 3076
  25.7 3.8 %copy-start.8 = (f32[6,16,128]{2,1,0:T(8,128)S(1)}, f32[6,16,128]{2,1,0:T(8,128)}, u32[]{:S(2)}) copy-start(f32[6,16,128]{2,1,0:T(8,128)} %param.4) | copy-start | bytes 147460
  28.9 0.9 copy-start.2
  28.9 1.0 copy-start.3
  28.9 1.1 copy-start.4
  28.9 1.2 copy-start.5
  28.9 1.3 copy-start.6
  29.0 1.3 copy-start.7
  34.2 10.4 %collective-permute-start.3 = (f32[4,6,16,128]{3,2,1,0:T(8,128)S(1)}, f32[4,6,16,128]{3,2,1,0:T(8,128)S(1)}, u32[]{:S(2)}, u32[]{:S(2)}) collective-permute-start(f32[4,6,16,128]{3,2,1,0:T(8,128)S(1)} %get-tuple-element.2), channel_id=1, source_target_pairs={{0,1},{1,2},{2,3},{3,4},{4,5},{5,6},{6,7},{7,8},{8,9},{9,10},{10,1... | collective-permute-start | bytes 589832 | tf_op jit(solution)/shard_map/ppermute | solution.py:27
  34.3 10.3 %collective-permute-start.2 = (f32[4,6,16,128]{3,2,1,0:T(8,128)S(1)}, f32[4,6,16,128]{3,2,1,0:T(8,128)S(1)}, u32[]{:S(2)}, u32[]{:S(2)}) collective-permute-start(f32[4,6,16,128]{3,2,1,0:T(8,128)S(1)} %get-tuple-element.2), channel_id=1, source_target_pairs={{1,0},{2,1},{3,2},{4,3},{5,4},{6,5},{7,6},{8,7},{9,8},{10,9},{11,1... | collective-permute-start | bytes 589832 | tf_op jit(solution)/shard_map/ppermute | solution.py:28
  68.4 46.6 %collective-permute-start.5 = (bf16[32,6,16,128]{3,2,1,0:T(8,128)(2,1)S(1)}, bf16[32,6,16,128]{3,2,1,0:T(8,128)(2,1)S(1)}, u32[]{:S(2)}, u32[]{:S(2)}) collective-permute-start(bf16[32,6,16,128]{3,2,1,0:T(8,128)(2,1)S(1)} %all_gather.3), channel_id=1, source_target_pairs={{1,0},{2,1},{3,2},{4,3},{5,4},{6,5},{7,6},{8,7},{9,8},{10,9},{11,1... | collective-permute-start | bytes 2359304 | tf_op jit(solution)/shard_map/ppermute | solution.py:28
  74.2 40.8 %collective-permute-start.4 = (bf16[32,6,16,128]{3,2,1,0:T(8,128)(2,1)S(1)}, bf16[32,6,16,128]{3,2,1,0:T(8,128)(2,1)S(1)}, u32[]{:S(2)}, u32[]{:S(2)}) collective-permute-start(bf16[32,6,16,128]{3,2,1,0:T(8,128)(2,1)S(1)} %all_gather.3), channel_id=1, source_target_pairs={{0,1},{1,2},{2,3},{3,4},{4,5},{5,6},{6,7},{7,8},{8,9},{9,10},{10,1... | collective-permute-start | bytes 2359304 | tf_op jit(solution)/shard_map/ppermute | solution.py:27
where the time goes:
time: 308 us
  blocking collectives  177 us (57%)
  local copies, waits for them, and re-layouts  69.3 us (22%)
  other arithmetic  37.5 us (12%)
  starting transfers between devices  18.5 us (6%)
    unnamed x1, blocking collectives  158 us
    slice x36, local copies, waits for them, and re-layouts, kinetic(): along = along + jnp.roll(field, reach, -1) + jnp.roll(field, -reach, -1)  33.8 us
    slice x36, local copies, waits for them, and re-layouts, kinetic(): along = along + jnp.roll(field, reach, -2) + jnp.roll(field, -reach, -2)  33.6 us
    convert_element_type x1, other arithmetic, body(): (kinetic(padded.astype(jnp.float32), own, potential) / HALF).astype(jnp.b...  29.1 us
    all_gather x1, blocking collectives, body(): gathered = lax.all_gather(rounded, 'band', axis=0, tiled=True)  18.7 us
    ppermute x3, starting transfers between devices, padded_2(): after = lax.ppermute(initial, axis, down)  16.7 us
  transfers between devices with their start and end apart: 6, of which 1 were waited for; matrix products, arithmetic and copies ran while one was open for 21% of the time, Pallas kernels for 0%

commit v1 on v0

v1 whole, which is shorter than its diff:
```python
import functools

import jax
import jax.numpy as jnp
from jax import lax
from jax.experimental import pallas as pl
from jax.experimental.pallas import tpu as pltpu
from jax.sharding import Mesh, PartitionSpec as P

COEFS = (
    -5369.0 / 1800.0,
    12.0 / 7.0,
    -15.0 / 56.0,
    10.0 / 189.0,
    -1.0 / 112.0,
    2.0 / 1925.0,
    -1.0 / 16632.0,
)
SPACING = 0.5
CENTER = 27.5
HALF = 22.5
KIN = -0.5 / SPACING**2
OFF = tuple(KIN * c / HALF for c in COEFS)
DIAG = 3.0 * KIN * COEFS[0] / HALF
BAND = ("z_hi", "core")
DOMAIN = ("z_lo", "x", "y")
CELLS = 393216
W = 6


def stencil(ref, at, scaled):
    v = ref[at]
    total = (DIAG + scaled) * v
    for k in range(1, W + 1):
        along = ref[at + k] + ref[at - k]
        along = along + pltpu.roll(v, k, 0) + pltpu.roll(v, 16 - k, 0)
        along = along + pltpu.roll(v, k, 1) + pltpu.roll(v, 128 - k, 1)
        total = total + OFF[k] * along
    return total


def filter_kernel(m2, m1, s, p1, p2, pot_m, pot, pot_p, out, field, first, scaled):
    planes = s.shape[1]
    scaled[0:planes] = pot_m[...] * (1.0 / HALF)
    scaled[planes : 2 * planes] = pot[...] * (1.0 / HALF)
    scaled[2 * planes : 3 * planes] = pot_p[...] * (1.0 / HALF)

    def one(i, _):
        for j, ref in enumerate((m2, m1, s, p1, p2)):
            field[j * planes : (j + 1) * planes] = ref[i].astype(jnp.float32)

        def inner(x, _):
            v = field[x + W]
            first[x] = stencil(field, x + W, scaled[x]) - (CENTER / HALF) * v
            return 0

        lax.fori_loop(0, 3 * planes, inner, 0, unroll=2)

        def outer(x, _):
            v = first[x + W]
            t = stencil(first, x + W, scaled[x + W]) - (CENTER / HALF) * v
            out[i, x] = (2.0 * t - field[x + 2 * W]).astype(jnp.bfloat16)
            return 0

        lax.fori_loop(0, planes, outer, 0, unroll=2)
        return 0

    lax.fori_loop(0, s.shape[0], one, 0)


def apply_kernel(m1, r, p1, pot, out, field):
    planes = r.shape[1]

    def one(i, _):
        for j, ref in enumerate((m1, r, p1)):
            field[j * planes : (j + 1) * planes] = ref[i].astype(jnp.float32)

        def inner(x, _):
            out[i, x] = stencil(field, x + W, pot[x] * (1.0 / HALF)).astype(jnp.bfloat16)
            return 0

        lax.fori_loop(0, planes, inner, 0, unroll=2)
        return 0

    lax.fori_loop(0, r.shape[0], one, 0)


def shifted(array, by):
    n = 32
    return lax.ppermute(array, DOMAIN, [(i, (i + by) % n) for i in range(n)])


def body(states, potential, slab):
    count, planes = states.shape[:2]
    low = states.astype(jnp.bfloat16)
    m1, p1 = shifted(low, 1), shifted(low, -1)
    m2, p2 = shifted(low, 2), shifted(low, -2)
    pot_m, pot_p = shifted(potential, 1), shifted(potential, -1)
    f32 = jnp.float32
    block = jax.ShapeDtypeStruct(states.shape, jnp.bfloat16)
    vm = pl.BlockSpec(memory_space=pltpu.VMEM)
    grid = states.shape[2:]
    rounded = pl.pallas_call(
        filter_kernel,
        out_shape=block,
        in_specs=[vm] * 8,
        out_specs=vm,
        scratch_shapes=[
            pltpu.VMEM((5 * planes, *grid), f32),
            pltpu.VMEM((3 * planes, *grid), f32),
            pltpu.VMEM((3 * planes, *grid), f32),
        ],
        cost_estimate=pl.CostEstimate(flops=10_000_000, bytes_accessed=700_000, transcendentals=0),
    )(m2, m1, states, p1, p2, pot_m, potential, pot_p)
    rm, rp = shifted(rounded, 1), shifted(rounded, -1)
    gathered = lax.all_gather(rounded, BAND, axis=0, tiled=True)
    applied = pl.pallas_call(
        apply_kernel,
        out_shape=block,
        in_specs=[vm] * 4,
        out_specs=vm,
        scratch_shapes=[pltpu.VMEM((3 * planes, *grid), f32)],
        cost_estimate=pl.CostEstimate(flops=3_000_000, bytes_accessed=400_000, transcendentals=0),
    )(rm, rounded, rp, potential)
    gathered_applied = lax.all_gather(applied, BAND, axis=0, tiled=True)

    slab_flat = slab.reshape(slab.shape[0], -1)

    def products(x):
        flat = x.reshape(x.shape[0], -1)
        return lax.dot_general(flat, slab_flat, (((1,), (1,)), ((), ())), preferred_element_type=f32)

    term = jnp.concatenate([products(gathered), products(gathered_applied)], axis=1)
    parts = lax.all_to_all(term, DOMAIN, 0, 0, tiled=True)
    scale = 1.0 / jnp.sqrt(jnp.float32(CELLS))
    share = jnp.sum(parts, axis=0, keepdims=True) * scale
    n = slab.shape[0]
    return share[:, :n], share[:, n:]


def solution(mesh):
    fine = Mesh(mesh.devices.reshape(4, 2, 2, 4, 4), ("z_hi", "core", "z_lo", "x", "y"))
    placed = (P(BAND, DOMAIN, None, None), P(DOMAIN, None, None), P(BAND, DOMAIN, None, None))
    return jax.shard_map(
        body,
        mesh=fine,
        in_specs=placed,
        out_specs=(P(DOMAIN, BAND), P(DOMAIN, BAND)),
        check_vma=False,
    )
```

time: 308 us -> 89.5 us (0.29)
  the two profiles are of different devices: /device:TPU:32 before, /device:TPU:1 now
where the time goes in v1:
time: 89.5 us; the launch traced here: 89.3 us
  blocking collectives  50.7 us (57%)
  starting transfers between devices  13.2 us (15%)
  Pallas kernels  11.1 us (12%)
  waiting for transfers between devices  8.17 us (9%)
  local copies, waits for them, and re-layouts  3.2 us (4%)
  other arithmetic  1.08 us (1%)
  matrix products  1.06 us (1%)
    all_gather x1, blocking collectives, body(): gathered = lax.all_gather(rounded, BAND, axis=0, tiled=True)  21.4 us
    all_gather x1, blocking collectives, body(): gathered_applied = lax.all_gather(applied, BAND, axis=0, tiled=True)  16.5 us
    ppermute x8, starting transfers between devices, shifted(): return lax.ppermute(array, DOMAIN, [(i, (i + by) % n) for i in range(n)])  13.2 us
    all_to_all x1, blocking collectives, body(): parts = lax.all_to_all(term, DOMAIN, 0, 0, tiled=True)  12.8 us
    ppermute x8, waiting for transfers between devices, shifted(): return lax.ppermute(array, DOMAIN, [(i, (i + by) % n) for i in range(n)])  8.17 us
    pallas_call x1, Pallas kernels, body(): pl.pallas_call(filter_kernel, out_shape=block, in_specs=[vm] * 8, out_spe...  7.93 us
    pallas_call x1, Pallas kernels, body(): pl.pallas_call(apply_kernel, out_shape=block, in_specs=[vm] * 4, out_spec...  3.2 us
    unnamed x20, local copies, waits for them, and re-layouts  2.61 us
  transfers between devices with their start and end apart: 8, of which 1 were waited for; matrix products, arithmetic and copies ran while one was open for 2% of the time, Pallas kernels for 0%

profile of v1, /device:TPU:1, one launch (start us, length us, event | category | flops | bytes accessed | tf_op | source)
XLA Modules:
  0.0 89.3 jit_solution(5859195842008040846)
XLA Ops:
  0.6 0.0 copy-start
  0.6 0.0 copy-start.1
  0.7 7.2 %collective-permute-start.5 = (f32[6,16,128]{2,1,0:T(8,128)}, f32[6,16,128]{2,1,0:T(8,128)S(1)}, u32[]{:S(2)}, u32[]{:S(2)}) collective-permute-start(f32[6,16,128]{2,1,0:T(8,128)} %pot.3), channel_id=1, source_target_pairs={{0,31},{1,0},{2,1},{3,2},{4,3},{5,4},{6,5},{7,6},{8,7},{9,8},{10,9... | collective-permute-start | bytes 147464 | tf_op jit(solution)/shard_map/ppermute | solution.py:90
  7.8 0.9 %convert_element_type.3 = bf16[4,6,16,128]{3,2,1,0:T(8,128)(2,1)S(1)} convert(f32[4,6,16,128]{3,2,1,0:T(8,128)} %s.1) | non-fusion elementwise | flops 49152 | bytes 294912 | tf_op jit(solution)/shard_map/convert_element_type | solution.py:95
  8.8 0.4 collective-permute-start.3
  9.2 0.8 collective-permute-start.2
  10.0 0.7 collective-permute-start.1
  10.7 2.6 %collective-permute-start = (bf16[4,6,16,128]{3,2,1,0:T(8,128)(2,1)S(1)}, bf16[4,6,16,128]{3,2,1,0:T(8,128)(2,1)S(1)}, u32[]{:S(2)}, u32[]{:S(2)}) collective-permute-start(bf16[4,6,16,128]{3,2,1,0:T(8,128)(2,1)S(1)} %convert_element_type.3), channel_id=1, source_target_pairs={{0,2},{1,3},{2,4},{3,5},{4,6},{5,7},{6,8},{7,9},{8,10},{9,11},{10,... | collective-permute-start | bytes 294920 | tf_op jit(solution)/shard_map/ppermute | solution.py:90
  13.3 0.0 collective-permute-done.5.pot_p
  13.3 0.0 copy-done.1
  13.3 0.0 copy-start.8
  13.3 0.1 collective-permute-start.4
  13.4 8.2 %collective-permute-done.4.pot_m = f32[6,16,128]{2,1,0:T(8,128)S(1)} collective-permute-done((f32[6,16,128]{2,1,0:T(8,128)S(1)}, f32[6,16,128]{2,1,0:T(8,128)S(1)}, u32[]{:S(2)}, u32[]{:S(2)}) %collective-permute-start.4) | collective-permute-done | bytes 49184 | tf_op jit(solution)/shard_map/ppermute | solution.py:90
  21.6 0.0 copy-start.9
  21.6 0.0 collective-permute-done.3.p2
  21.6 0.0 copy-start.2
  21.6 0.0 collective-permute-done.2.p1
  21.6 0.0 copy-start.3
  21.6 0.0 collective-permute-done.1.m1
  21.6 0.0 copy-start.4
  21.6 0.0 collective-permute-done.m2
  21.6 0.0 copy-done.8
  21.6 0.5 copy-done.9
  22.2 0.0 copy-done.2
  22.2 0.0 copy-done.3
  22.2 0.1 copy-done.4
  22.3 0.0 copy-start.5
  22.3 0.6 copy-done.5
  22.9 7.9 %shard_map.50.r = bf16[4,6,16,128]{3,2,1,0:T(8,128)(2,1)} custom-call(bf16[4,6,16,128]{3,2,1,0:T(8,128)(2,1)} %copy-done.5, bf16[4,6,16,128]{3,2,1,0:T(8,128)(2,1)} %copy-done.4, f32[4,6,16,128]{3,2,1,0:T(8,128)} %s.1, bf16[4,6,16,128]{3,2,1,0:T(8,128)(2,1)} %copy-done.3, bf16[4,6,16,128]{3,2,1,0:T(8,128)(2,1)} %copy-done.2, f32[6,16,128]{2,1,0:T(8,128)} %copy-done.9, ...), custom_call_target="tpu_custom_call" | custom-call | flops 10000000 | bytes 700000 | tf_op jit(solution)/shard_map/pallas_call | solution.py:103
  30.9 0.0 collective-permute-start.7
  30.9 1.5 %collective-permute-start.6 = (bf16[4,6,16,128]{3,2,1,0:T(8,128)(2,1)}, bf16[4,6,16,128]{3,2,1,0:T(8,128)(2,1)S(1)}, u32[]{:S(2)}, u32[]{:S(2)}) collective-permute-start(bf16[4,6,16,128]{3,2,1,0:T(8,128)(2,1)} %shard_map.50.r), channel_id=1, source_target_pairs={{0,1},{1,2},{2,3},{3,4},{4,5},{5,6},{6,7},{7,8},{8,9},{9,10},{10,1... | collective-permute-start | bytes 294920 | tf_op jit(solution)/shard_map/ppermute | solution.py:90
  32.3 21.4 %all_gather.6 = bf16[32,6,16,128]{3,2,1,0:T(8,128)(2,1)S(1)} all-gather(bf16[4,6,16,128]{3,2,1,0:T(8,128)(2,1)} %shard_map.50.r), channel_id=1, replica_groups=mesh['z_hi'=4,'core'=2,'z_lo'=2,'x'=4,'y'=4] {'z_hi','core'}, dimensions={0}, use_global_device_ids=true | all-gather | bytes 884736 | tf_op jit(solution)/shard_map/all_gather | solution.py:116
  53.7 0.0 copy-done
  53.7 0.5 convolution_bitcast_fusion.1
  54.2 0.0 collective-permute-done.7.p1
  54.3 0.0 copy-start.6
  54.3 0.0 collective-permute-done.6.m1
  54.3 0.6 copy-done.6
  54.9 0.0 copy-start.7
  54.9 0.6 copy-done.7
  55.5 3.2 %shard_map.51 = bf16[4,6,16,128]{3,2,1,0:T(8,128)(2,1)} custom-call(bf16[4,6,16,128]{3,2,1,0:T(8,128)(2,1)} %copy-done.7, bf16[4,6,16,128]{3,2,1,0:T(8,128)(2,1)} %shard_map.50.r, bf16[4,6,16,128]{3,2,1,0:T(8,128)(2,1)} %copy-done.6, f32[6,16,128]{2,1,0:T(8,128)} %pot.3), custom_call_target="tpu_custom_call" | custom-call | flops 3000000 | bytes 400000 | tf_op jit(solution)/shard_map/pallas_call | solution.py:117
  58.7 16.5 %all_gather.7 = bf16[32,6,16,128]{3,2,1,0:T(8,128)(2,1)S(1)} all-gather(bf16[4,6,16,128]{3,2,1,0:T(8,128)(2,1)} %shard_map.51), channel_id=1, replica_groups=mesh['z_hi'=4,'core'=2,'z_lo'=2,'x'=4,'y'=4] {'z_hi','core'}, dimensions={0}, use_global_device_ids=true | all-gather | bytes 884736 | tf_op jit(solution)/shard_map/all_gather | solution.py:125
  75.3 0.5 convolution_bitcast_fusion
  75.8 0.1 pad_maximum_fusion
  75.9 12.8 %all_to_all.9 = f32[32,1,64]{2,1,0:T(1,128)S(1)} all-to-all(f32[32,1,64]{2,1,0:T(1,128)S(1)} %bitcast.13), channel_id=1, replica_groups=mesh['z_hi'=4,'core'=2,'z_lo'=2,'x'=4,'y'=4] {'z_lo','x','y'}, dimensions={0} | all-to-all | bytes 16384 | tf_op jit(solution)/shard_map/all_to_all | solution.py:134
  88.7 0.1 reduce_sum.9
  88.7 0.6 fusion.4
  (1 shorter events, 0.0 us)
Async XLA Ops:
  0.6 53.1 %copy-start = (bf16[32,6,16,128]{3,2,1,0:T(8,128)(2,1)S(1)}, bf16[32,6,16,128]{3,2,1,0:T(8,128)(2,1)}, u32[]{:S(2)}) copy-start(bf16[32,6,16,128]{3,2,1,0:T(8,128)(2,1)} %param.5) | copy-start | bytes 2359300
  0.6 12.7 %copy-start.1 = (f32[6,16,128]{2,1,0:T(8,128)S(1)}, f32[6,16,128]{2,1,0:T(8,128)}, u32[]{:S(2)}) copy-start(f32[6,16,128]{2,1,0:T(8,128)} %pot.3) | copy-start | bytes 147460
  0.7 12.7 %collective-permute-start.5 = (f32[6,16,128]{2,1,0:T(8,128)}, f32[6,16,128]{2,1,0:T(8,128)S(1)}, u32[]{:S(2)}, u32[]{:S(2)}) collective-permute-start(f32[6,16,128]{2,1,0:T(8,128)} %pot.3), channel_id=1, source_target_pairs={{0,31},{1,0},{2,1},{3,2},{4,3},{5,4},{6,5},{7,6},{8,7},{9,8},{10,9... | collective-permute-start | bytes 147464 | tf_op jit(solution)/shard_map/ppermute | solution.py:90
  8.8 12.8 %collective-permute-start.3 = (bf16[4,6,16,128]{3,2,1,0:T(8,128)(2,1)S(1)}, bf16[4,6,16,128]{3,2,1,0:T(8,128)(2,1)S(1)}, u32[]{:S(2)}, u32[]{:S(2)}) collective-permute-start(bf16[4,6,16,128]{3,2,1,0:T(8,128)(2,1)S(1)} %convert_element_type.3), channel_id=1, source_target_pairs={{0,30},{1,31},{2,0},{3,1},{4,2},{5,3},{6,4},{7,5},{8,6},{9,7},{10,... | collective-permute-start | bytes 294920 | tf_op jit(solution)/shard_map/ppermute | solution.py:90
  9.2 12.3 %collective-permute-start.2 = (bf16[4,6,16,128]{3,2,1,0:T(8,128)(2,1)S(1)}, bf16[4,6,16,128]{3,2,1,0:T(8,128)(2,1)S(1)}, u32[]{:S(2)}, u32[]{:S(2)}) collective-permute-start(bf16[4,6,16,128]{3,2,1,0:T(8,128)(2,1)S(1)} %convert_element_type.3), channel_id=1, source_target_pairs={{0,31},{1,0},{2,1},{3,2},{4,3},{5,4},{6,5},{7,6},{8,7},{9,8},{10,9... | collective-permute-start | bytes 294920 | tf_op jit(solution)/shard_map/ppermute | solution.py:90
  10.0 11.6 %collective-permute-start.1 = (bf16[4,6,16,128]{3,2,1,0:T(8,128)(2,1)S(1)}, bf16[4,6,16,128]{3,2,1,0:T(8,128)(2,1)S(1)}, u32[]{:S(2)}, u32[]{:S(2)}) collective-permute-start(bf16[4,6,16,128]{3,2,1,0:T(8,128)(2,1)S(1)} %convert_element_type.3), channel_id=1, source_target_pairs={{0,1},{1,2},{2,3},{3,4},{4,5},{5,6},{6,7},{7,8},{8,9},{9,10},{10,1... | collective-permute-start | bytes 294920 | tf_op jit(solution)/shard_map/ppermute | solution.py:90
  10.7 10.9 %collective-permute-start = (bf16[4,6,16,128]{3,2,1,0:T(8,128)(2,1)S(1)}, bf16[4,6,16,128]{3,2,1,0:T(8,128)(2,1)S(1)}, u32[]{:S(2)}, u32[]{:S(2)}) collective-permute-start(bf16[4,6,16,128]{3,2,1,0:T(8,128)(2,1)S(1)} %convert_element_type.3), channel_id=1, source_target_pairs={{0,2},{1,3},{2,4},{3,5},{4,6},{5,7},{6,8},{7,9},{8,10},{9,11},{10,... | collective-permute-start | bytes 294920 | tf_op jit(solution)/shard_map/ppermute | solution.py:90
  13.3 8.3 %copy-start.8 = (f32[6,16,128]{2,1,0:T(8,128)}, f32[6,16,128]{2,1,0:T(8,128)S(1)}, u32[]{:S(2)}) copy-start(f32[6,16,128]{2,1,0:T(8,128)S(1)} %collective-permute-done.5.pot_p) | copy-start | bytes 147460
  13.3 8.2 %collective-permute-start.4 = (f32[6,16,128]{2,1,0:T(8,128)S(1)}, f32[6,16,128]{2,1,0:T(8,128)S(1)}, u32[]{:S(2)}, u32[]{:S(2)}) collective-permute-start(f32[6,16,128]{2,1,0:T(8,128)S(1)} %copy-done.1), channel_id=1, source_target_pairs={{0,1},{1,2},{2,3},{3,4},{4,5},{5,6},{6,7},{7,8},{8,9},{9,10},{10,1... | collective-permute-start | bytes 147464 | tf_op jit(solution)/shard_map/ppermute | solution.py:90
  21.6 0.6 copy-start.9
  21.6 0.6 copy-start.2
  21.6 0.7 copy-start.3
  21.6 0.7 copy-start.4
  22.3 0.6 copy-start.5
  30.9 23.4 %collective-permute-start.7 = (bf16[4,6,16,128]{3,2,1,0:T(8,128)(2,1)}, bf16[4,6,16,128]{3,2,1,0:T(8,128)(2,1)S(1)}, u32[]{:S(2)}, u32[]{:S(2)}) collective-permute-start(bf16[4,6,16,128]{3,2,1,0:T(8,128)(2,1)} %shard_map.50.r), channel_id=1, source_target_pairs={{0,31},{1,0},{2,1},{3,2},{4,3},{5,4},{6,5},{7,6},{8,7},{9,8},{10,9... | collective-permute-start | bytes 294920 | tf_op jit(solution)/shard_map/ppermute | solution.py:90
  30.9 23.4 %collective-permute-start.6 = (bf16[4,6,16,128]{3,2,1,0:T(8,128)(2,1)}, bf16[4,6,16,128]{3,2,1,0:T(8,128)(2,1)S(1)}, u32[]{:S(2)}, u32[]{:S(2)}) collective-permute-start(bf16[4,6,16,128]{3,2,1,0:T(8,128)(2,1)} %shard_map.50.r), channel_id=1, source_target_pairs={{0,1},{1,2},{2,3},{3,4},{4,5},{5,6},{6,7},{7,8},{8,9},{9,10},{10,1... | collective-permute-start | bytes 294920 | tf_op jit(solution)/shard_map/ppermute | solution.py:90
  54.3 0.7 copy-start.6
  54.9 0.6 copy-start.7

commit v2 on v1

v2 whole, which is shorter than its diff:
```python
import jax
import jax.numpy as jnp
import ml_dtypes
import numpy as np
from jax import lax
from jax.experimental import pallas as pl
from jax.experimental.pallas import tpu as pltpu
from jax.sharding import Mesh, PartitionSpec as P

COEFS = (
    -5369.0 / 1800.0,
    12.0 / 7.0,
    -15.0 / 56.0,
    10.0 / 189.0,
    -1.0 / 112.0,
    2.0 / 1925.0,
    -1.0 / 16632.0,
)
SPACING = 0.5
CENTER = 27.5
HALF = 22.5
KIN = -0.5 / SPACING**2
OFF = tuple(KIN * c / HALF for c in COEFS)
DIAG = 3.0 * KIN * COEFS[0] / HALF
SHIFT = CENTER / HALF
BAND = ("z_hi", "core")
DOMAIN = ("z_lo", "x", "y")
CELLS = 393216
W = 6
CY, CZ, PLANES = 16, 128, 6
ROWS = PLANES * CY
BF16, F32 = jnp.bfloat16, jnp.float32


def circulant(n):
    m = np.zeros((n, n), np.float64)
    for i in range(n):
        for k in range(1, W + 1):
            m[i, (i + k) % n] += OFF[k]
            m[i, (i - k) % n] += OFF[k]
    return m


def halves(m):
    high = m.astype(ml_dtypes.bfloat16)
    low = (m - high.astype(np.float64)).astype(ml_dtypes.bfloat16)
    return high, low


Z_HIGH, Z_LOW = halves(circulant(CZ))
Y_HIGH, Y_LOW = halves(np.kron(np.eye(PLANES), circulant(CY)))
Z2 = np.concatenate([Z_HIGH, Z_LOW], 0)
Y2 = np.concatenate([Y_HIGH, Y_LOW], 1)
Z3 = np.block([[Z_HIGH, Z_LOW], [Z_HIGH, np.zeros_like(Z_LOW)]])
Y3 = np.concatenate([Y_HIGH, Y_HIGH, Y_LOW], 1)


def dot(a, b):
    return jnp.dot(a, b, preferred_element_type=F32)


def along_x(planes, n):
    out = []
    for x in range(W, W + n):
        total = OFF[1] * (planes[x + 1] + planes[x - 1])
        for k in range(2, W + 1):
            total = total + OFF[k] * (planes[x + k] + planes[x - k])
        out.append(total)
    return out


def along_yz(planes, z3, y3):
    n = len(planes)
    field = jnp.concatenate([p[None] for p in planes], 0).reshape(n * CY, CZ)
    high = field.astype(BF16)
    low = (field - high.astype(F32)).astype(BF16)
    z = dot(jnp.concatenate([high, low], 1), z3)
    z = z[:, :CZ] + z[:, CZ:]
    out = []
    for g in range(0, n * CY, ROWS):
        h, l = high[g : g + ROWS], low[g : g + ROWS]
        y = dot(y3, jnp.concatenate([h, l, h], 0)) + z[g : g + ROWS]
        out += [y[i * CY : (i + 1) * CY] for i in range(PLANES)]
    return out


def filter_kernel(m2, m1, s, p1, p2, pot, z3_ref, y3_ref, out):
    count = s.shape[0]
    z3, y3 = z3_ref[...], y3_ref[...]

    def sent(ref):
        return [(ref[count, x].astype(F32) + ref[count + 1, x].astype(F32)) for x in range(PLANES)]

    raw = sent(m1) + [pot[x] for x in range(PLANES)] + sent(p1)
    diag = [(DIAG - SHIFT) + v * (1.0 / HALF) for v in raw]
    for i in range(count):
        field = []
        for ref in (m2, m1, s, p1, p2):
            field += [ref[i, x].astype(F32) for x in range(PLANES)]
        inner = field[W:-W]
        first = [
            a + b + d * v
            for a, b, d, v in zip(along_x(field, 3 * PLANES), along_yz(inner, z3, y3), diag, inner)
        ]
        own = first[W:-W]
        turned = [
            a + b + d * v
            for a, b, d, v in zip(along_x(first, PLANES), along_yz(own, z3, y3), diag[W:-W], own)
        ]
        for x in range(PLANES):
            out[i, x] = (2.0 * turned[x] - field[2 * W + x]).astype(BF16)


def slab_inner_kernel(slab, pot, z2_ref, y2_ref, out):
    count = slab.shape[0]
    z2, y2 = z2_ref[...], y2_ref[...]
    diag = (DIAG + pot[...] * (1.0 / HALF)).reshape(ROWS, CZ)
    for i in range(0, count, 2):
        pair = [slab[i + j].reshape(ROWS, CZ) for j in range(2)]
        wide = jnp.concatenate(pair, 1)
        y = dot(y2, jnp.concatenate([wide, wide], 0))
        for j in range(2):
            z = dot(jnp.concatenate([pair[j], pair[j]], 1), z2)
            total = y[:, j * CZ : (j + 1) * CZ] + z + diag * pair[j].astype(F32)
            out[i + j] = total.reshape(PLANES, CY, CZ)


def slab_outer_kernel(before, slab, after, inner, out):
    def one(i, _):
        planes = []
        for ref in (before, slab, after):
            planes += [ref[i, x].astype(F32) for x in range(PLANES)]
        for x, along in enumerate(along_x(planes, PLANES)):
            out[i, x] = (along + inner[i, x]).astype(BF16)
        return 0

    lax.fori_loop(0, slab.shape[0], one, 0)


def shifted(array, by):
    n = 32
    return lax.ppermute(array, DOMAIN, [(i, (i + by) % n) for i in range(n)])


def vmem(n=1):
    return [pl.BlockSpec(memory_space=pltpu.VMEM)] * n


def filter_own(m2, m1, s, p1, p2, pot):
    return pl.pallas_call(
        filter_kernel,
        out_shape=jax.ShapeDtypeStruct(s.shape, BF16),
        in_specs=vmem(8),
        out_specs=vmem()[0],
        compiler_params=pltpu.CompilerParams(vmem_limit_bytes=16 << 20),
        cost_estimate=pl.CostEstimate(flops=200_000_000, bytes_accessed=800_000, transcendentals=0),
        name="filter_own",
    )(m2, m1, s, p1, p2, pot, jnp.asarray(Z3), jnp.asarray(Y3))


GROUP = 8


def by_group(count):
    return pl.BlockSpec((GROUP, PLANES, CY, CZ), lambda i: (i, 0, 0, 0))


def whole(shape):
    return pl.BlockSpec(shape, lambda i: (0,) * len(shape))


def slab_inner(slab, pot):
    n = slab.shape[0]
    return pl.pallas_call(
        slab_inner_kernel,
        grid=(n // GROUP,),
        out_shape=jax.ShapeDtypeStruct(slab.shape, F32),
        in_specs=[by_group(n), whole(pot.shape), whole(Z2.shape), whole(Y2.shape)],
        out_specs=by_group(n),
        compiler_params=pltpu.CompilerParams(vmem_limit_bytes=16 << 20),
        cost_estimate=pl.CostEstimate(flops=400_000_000, bytes_accessed=2_400_000, transcendentals=0),
        name="slab_inner",
    )(slab, pot, jnp.asarray(Z2), jnp.asarray(Y2))


def slab_outer(before, slab, after, inner):
    n = slab.shape[0]
    return pl.pallas_call(
        slab_outer_kernel,
        grid=(n // GROUP,),
        out_shape=jax.ShapeDtypeStruct(slab.shape, BF16),
        in_specs=[by_group(n)] * 4,
        out_specs=by_group(n),
        compiler_params=pltpu.CompilerParams(vmem_limit_bytes=16 << 20),
        cost_estimate=pl.CostEstimate(flops=10_000_000, bytes_accessed=4_700_000, transcendentals=0),
        name="slab_outer",
    )(before, slab, after, inner)


def body(states, potential, slab):
    low = states.astype(BF16)
    pot_high = potential.astype(BF16)
    pot_low = (potential - pot_high.astype(F32)).astype(BF16)
    near = jnp.concatenate([low, pot_high[None], pot_low[None]], axis=0)
    m1, p1 = shifted(near, 1), shifted(near, -1)
    m2, p2 = shifted(low, 2), shifted(low, -2)
    inner = slab_inner(slab, potential)
    late_slab, inner = lax.optimization_barrier((slab, inner))
    before, after = shifted(late_slab, 1), shifted(late_slab, -1)
    rounded = filter_own(m2, m1, states, p1, p2, potential)
    gathered = lax.all_gather(rounded, BAND, axis=0, tiled=True)
    turned = slab_outer(before, slab, after, inner)

    flat = gathered.reshape(gathered.shape[0], -1)

    def products(x):
        return lax.dot_general(
            flat, x.reshape(x.shape[0], -1), (((1,), (1,)), ((), ())), preferred_element_type=F32
        )

    term = jnp.concatenate([products(slab), products(turned)], axis=1)
    parts = lax.all_to_all(term, DOMAIN, 0, 0, tiled=True)
    scale = 1.0 / jnp.sqrt(jnp.float32(CELLS))
    share = jnp.sum(parts, axis=0, keepdims=True) * scale
    n = slab.shape[0]
    return share[:, :n], share[:, n:]


def solution(mesh):
    fine = Mesh(mesh.devices.reshape(4, 2, 2, 4, 4), ("z_hi", "core", "z_lo", "x", "y"))
    placed = (P(BAND, DOMAIN, None, None), P(DOMAIN, None, None), P(BAND, DOMAIN, None, None))
    return jax.shard_map(
        body,
        mesh=fine,
        in_specs=placed,
        out_specs=(P(DOMAIN, BAND), P(DOMAIN, BAND)),
        check_vma=False,
    )
```

time: 89.5 us -> 83 us (0.927)
  blocking collectives: 50.7 us -> 37.9 us
  starting transfers between devices: 13.2 us -> 20.3 us
  Pallas kernels: 11.1 us -> 7.04 us
  waiting for transfers between devices: 8.17 us -> 11.2 us
  matrix products: 1.06 us -> 2.19 us
  other arithmetic: 1.08 us -> 0.18 us
    all_gather x1 -> x0, blocking collectives: 16.5 us -> none  [body(): gathered_applied = lax.all_gather(applied, BAND, axis=0, tiled=True)]
    ppermute x8 -> x6, starting transfers between devices: 13.2 us -> 20.3 us  [shifted(): return lax.ppermute(array, DOMAIN, [(i, (i + by) % n) for i in range(n)])]
    pallas_call x2 -> x3, Pallas kernels: 11.1 us -> 7.04 us  [the longest x1 2.92 us: slab_inner(): pl.pallas_call(slab_inner_kernel, grid=(n // GROUP,), out_shape=jax.Shape...]
    all_to_all x1, blocking collectives: 12.8 us -> 16.8 us  [body(): parts = lax.all_to_all(term, DOMAIN, 0, 0, tiled=True)]
    ppermute x8 -> x6, waiting for transfers between devices: 8.17 us -> 11.2 us  [shifted(): return lax.ppermute(array, DOMAIN, [(i, (i + by) % n) for i in range(n)])]
    dot_general x2, matrix products: 1.06 us -> 2.19 us  [products(): lax.dot_general(flat, x.reshape(x.shape[0], -1), (((1,), (1,)), ((), ()))...]
    convert_element_type x1, other arithmetic: 0.94 us -> 0.02 us  [body(): low = states.astype(BF16)]
    unnamed x20 -> x14, local copies, waits for them, and re-layouts: 2.61 us -> 2.44 us
  transfers between devices with their start and end apart: 8 -> 6, of which waited for: 1 -> 3; matrix products, arithmetic and copies ran while one was open for 2% -> 2% of each run, Pallas kernels for 0% -> 1%
where the time goes in v2:
time: 83 us; the launch traced here: 82.6 us
  blocking collectives  37.9 us (46%)
  starting transfers between devices  20.3 us (24%)
  waiting for transfers between devices  11.2 us (13%)
  Pallas kernels  7.04 us (8%)
  local copies, waits for them, and re-layouts  3.03 us (4%)
  matrix products  2.19 us (3%)
    all_gather x1, blocking collectives, body(): gathered = lax.all_gather(rounded, BAND, axis=0, tiled=True)  21.2 us
    ppermute x6, starting transfers between devices, shifted(): return lax.ppermute(array, DOMAIN, [(i, (i + by) % n) for i in range(n)])  20.3 us
    all_to_all x1, blocking collectives, body(): parts = lax.all_to_all(term, DOMAIN, 0, 0, tiled=True)  16.8 us
    ppermute x6, waiting for transfers between devices, shifted(): return lax.ppermute(array, DOMAIN, [(i, (i + by) % n) for i in range(n)])  11.2 us
    pallas_call x1, Pallas kernels, slab_inner(): pl.pallas_call(slab_inner_kernel, grid=(n // GROUP,), out_shape=jax.Shape...  2.92 us
    pallas_call x1, Pallas kernels, slab_outer(): pl.pallas_call(slab_outer_kernel, grid=(n // GROUP,), out_shape=jax.Shape...  2.89 us
    unnamed x14, local copies, waits for them, and re-layouts  2.44 us
    dot_general x2, matrix products, products(): lax.dot_general(flat, x.reshape(x.shape[0], -1), (((1,), (1,)), ((), ()))...  2.19 us
  transfers between devices with their start and end apart: 6, of which 3 were waited for; matrix products, arithmetic and copies ran while one was open for 2% of the time, Pallas kernels for 1%

profile of v2, /device:TPU:1, one launch (start us, length us, event | category | flops | bytes accessed | tf_op | source)
XLA Modules:
  0.0 82.6 jit_solution(5837581963557045658)
XLA Ops:
  0.6 0.0 copy-start.1
  0.6 0.8 copy-done.1
  1.4 0.0 copy-start.5
  1.4 0.8 %copy-done.5 = bf16[256,128]{1,0:T(8,128)(2,1)S(1)} copy-done((bf16[256,128]{1,0:T(8,128)(2,1)S(1)}, bf16[256,128]{1,0:T(8,128)(2,1)}, u32[]{:S(2)}) %copy-start.5) | copy-done | bytes 65560
  2.3 0.0 copy-start.6
  2.3 0.8 copy-done.6
  3.1 0.0 copy-start
  3.1 0.0 copy-start.2
  3.1 0.0 copy-start.3
  3.1 0.0 copy-start.4
  3.1 2.9 %slab_inner.1.inner = f32[32,6,16,128]{3,2,1,0:T(8,128)S(1)} custom-call(bf16[32,6,16,128]{3,2,1,0:T(8,128)(2,1)} %slab.3, f32[6,16,128]{2,1,0:T(8,128)S(1)} %copy-done.1, bf16[256,128]{1,0:T(8,128)(2,1)S(1)} %copy-done.5, bf16[96,192]{1,0:T(8,128)(2,1)S(1)} %copy-done.6), custom_call_target="tpu_custom_call" | custom-call | flops 400000000 | bytes 2400000 | tf_op jit(solution)/shard_map/slab_inner/pallas_call | solution.py:174
  6.0 2.2 %collective-permute-start.4 = (bf16[32,6,16,128]{3,2,1,0:T(8,128)(2,1)}, bf16[32,6,16,128]{3,2,1,0:T(8,128)(2,1)S(1)}, u32[]{:S(2)}, u32[]{:S(2)}) collective-permute-start(bf16[32,6,16,128]{3,2,1,0:T(8,128)(2,1)} %slab.3), channel_id=1, source_target_pairs={{0,1},{1,2},{2,3},{3,4},{4,5},{5,6},{6,7},{7,8},{8,9},{9,10},{10,1... | collective-permute-start | bytes 2359304 | tf_op jit(solution)/shard_map/ppermute | solution.py:142
  8.2 5.1 %collective-permute-start.5 = (bf16[32,6,16,128]{3,2,1,0:T(8,128)(2,1)}, bf16[32,6,16,128]{3,2,1,0:T(8,128)(2,1)S(1)}, u32[]{:S(2)}, u32[]{:S(2)}) collective-permute-start(bf16[32,6,16,128]{3,2,1,0:T(8,128)(2,1)} %slab.3), channel_id=1, source_target_pairs={{0,31},{1,0},{2,1},{3,2},{4,3},{5,4},{6,5},{7,6},{8,7},{9,8},{10,9... | collective-permute-start | bytes 2359304 | tf_op jit(solution)/shard_map/ppermute | solution.py:142
  13.3 0.0 copy-done
  13.3 0.1 collective-permute-start
  13.5 0.1 collective-permute-start.1
  13.5 5.7 %collective-permute-start.2 = (bf16[6,6,16,128]{3,2,1,0:T(8,128)(2,1)S(1)}, bf16[6,6,16,128]{3,2,1,0:T(8,128)(2,1)S(1)}, u32[]{:S(2)}, u32[]{:S(2)}) collective-permute-start(bf16[6,6,16,128]{3,2,1,0:T(8,128)(2,1)S(1)} %pad_maximum_fusion), channel_id=1, source_target_pairs={{0,31},{1,0},{2,1},{3,2},{4,3},{5,4},{6,5},{7,6},{8,7},{9,8},{10,9... | collective-permute-start | bytes 442376 | tf_op jit(solution)/shard_map/ppermute | solution.py:142
  19.2 7.3 %collective-permute-done.m2 = bf16[4,6,16,128]{3,2,1,0:T(8,128)(2,1)S(1)} collective-permute-done((bf16[4,6,16,128]{3,2,1,0:T(8,128)(2,1)S(1)}, bf16[4,6,16,128]{3,2,1,0:T(8,128)(2,1)S(1)}, u32[]{:S(2)}, u32[]{:S(2)}) %collective-permute-start) | collective-permute-done | bytes 98336 | tf_op jit(solution)/shard_map/ppermute | solution.py:142
  26.5 7.2 %collective-permute-start.3 = (bf16[4,6,16,128]{3,2,1,0:T(8,128)(2,1)S(1)}, bf16[4,6,16,128]{3,2,1,0:T(8,128)(2,1)S(1)}, u32[]{:S(2)}, u32[]{:S(2)}) collective-permute-start(bf16[4,6,16,128]{3,2,1,0:T(8,128)(2,1)S(1)} %convert_element_type.12), channel_id=1, source_target_pairs={{0,30},{1,31},{2,0},{3,1},{4,2},{5,3},{6,4},{7,5},{8,6},{9,7},{10,... | collective-permute-start | bytes 294920 | tf_op jit(solution)/shard_map/ppermute | solution.py:142
  33.7 3.2 %collective-permute-done.3.p2 = bf16[4,6,16,128]{3,2,1,0:T(8,128)(2,1)S(1)} collective-permute-done((bf16[4,6,16,128]{3,2,1,0:T(8,128)(2,1)S(1)}, bf16[4,6,16,128]{3,2,1,0:T(8,128)(2,1)S(1)}, u32[]{:S(2)}, u32[]{:S(2)}) %collective-permute-start.3) | collective-permute-done | bytes 98336 | tf_op jit(solution)/shard_map/ppermute | solution.py:142
  36.9 0.7 collective-permute-done.1.m1
  37.6 0.0 collective-permute-done.2.p1
  37.6 0.0 copy-done.2
  37.6 0.0 copy-done.3
  37.6 0.0 copy-done.4
  37.6 1.2 %filter_own.1 = bf16[4,6,16,128]{3,2,1,0:T(8,128)(2,1)S(1)} custom-call(bf16[4,6,16,128]{3,2,1,0:T(8,128)(2,1)S(1)} %collective-permute-done.m2, bf16[6,6,16,128]{3,2,1,0:T(8,128)(2,1)S(1)} %collective-permute-done.1.m1, f32[4,6,16,128]{3,2,1,0:T(8,128)S(1)} %copy-done, bf16[6,6,16,128]{3,2,1,0:T(8,128)(2,1)S(1)} %collective-permute-done.2.p1, ...), custom_call_target="tpu_custom_call" | custom-call | flops 200000000 | bytes 800000 | tf_op jit(solution)/shard_map/filter_own/pallas_call | solution.py:150
  38.9 21.2 %all_gather.3 = bf16[32,6,16,128]{3,2,1,0:T(8,128)(2,1)S(1)} all-gather(bf16[4,6,16,128]{3,2,1,0:T(8,128)(2,1)S(1)} %filter_own.1), channel_id=1, replica_groups=mesh['z_hi'=4,'core'=2,'z_lo'=2,'x'=4,'y'=4] {'z_hi','core'}, dimensions={0}, use_global_device_ids=true | all-gather | bytes 884736 | tf_op jit(solution)/shard_map/all_gather | solution.py:211
  60.0 1.7 %convolution_bitcast_fusion.1 = f32[32,32]{1,0:T(8,128)S(1)} fusion(bf16[32,6,16,128]{3,2,1,0:T(8,128)(2,1)} %slab.3, bf16[32,6,16,128]{3,2,1,0:T(8,128)(2,1)S(1)} %all_gather.3), kind=kOutput, calls=%fused_computation.1 | convolution fusion | flops 25165824 | bytes 1576960 | tf_op jit(solution)/shard_map/dot_general | solution.py:217
  61.7 0.0 collective-permute-done.4.before
  61.7 0.0 collective-permute-done.5.after
  61.7 2.9 %slab_outer.1 = bf16[32,6,16,128]{3,2,1,0:T(8,128)(2,1)S(1)} custom-call(bf16[32,6,16,128]{3,2,1,0:T(8,128)(2,1)S(1)} %collective-permute-done.4.before, bf16[32,6,16,128]{3,2,1,0:T(8,128)(2,1)} %slab.3, bf16[32,6,16,128]{3,2,1,0:T(8,128)(2,1)S(1)} %collective-permute-done.5.after, f32[32,6,16,128]{3,2,1,0:T(8,128)S(1)} %slab_inner.1.inner), custom_call_target="tpu_custom_call" | custom-call | flops 10000000 | bytes 4700000 | tf_op jit(solution)/shard_map/slab_outer/pallas_call | solution.py:188
  64.6 0.5 convolution_bitcast_fusion
  65.1 0.1 pad_maximum_fusion.1
  65.2 16.8 %all_to_all.9 = f32[32,1,64]{2,1,0:T(1,128)S(1)} all-to-all(f32[32,1,64]{2,1,0:T(1,128)S(1)} %bitcast.17), channel_id=1, replica_groups=mesh['z_hi'=4,'core'=2,'z_lo'=2,'x'=4,'y'=4] {'z_lo','x','y'}, dimensions={0} | all-to-all | bytes 16384 | tf_op jit(solution)/shard_map/all_to_all | solution.py:222
  82.0 0.1 reduce_sum.9
  82.0 0.6 fusion.5
  (4 shorter events, 0.1 us)
Async XLA Ops:
  0.6 0.8 copy-start.1
  1.4 0.8 %copy-start.5 = (bf16[256,128]{1,0:T(8,128)(2,1)S(1)}, bf16[256,128]{1,0:T(8,128)(2,1)}, u32[]{:S(2)}) copy-start(bf16[256,128]{1,0:T(8,128)(2,1)} %constant.12.clone.z2_ref) | copy-start | bytes 196612
  2.3 0.8 copy-start.6
  3.1 10.2 %copy-start = (f32[4,6,16,128]{3,2,1,0:T(8,128)S(1)}, f32[4,6,16,128]{3,2,1,0:T(8,128)}, u32[]{:S(2)}) copy-start(f32[4,6,16,128]{3,2,1,0:T(8,128)} %s.1) | copy-start | bytes 589828
  3.1 34.5 %copy-start.2 = (f32[6,16,128]{2,1,0:T(8,128)S(1)}, f32[6,16,128]{2,1,0:T(8,128)}, u32[]{:S(2)}) copy-start(f32[6,16,128]{2,1,0:T(8,128)} %pot.3) | copy-start | bytes 147460
  3.1 34.5 %copy-start.3 = (bf16[256,256]{1,0:T(8,128)(2,1)S(1)}, bf16[256,256]{1,0:T(8,128)(2,1)}, u32[]{:S(2)}) copy-start(bf16[256,256]{1,0:T(8,128)(2,1)} %constant.14.clone.z3_ref) | copy-start | bytes 393220
  3.1 34.6 %copy-start.4 = (bf16[96,288]{1,0:T(8,128)(2,1)S(1)}, bf16[96,288]{1,0:T(8,128)(2,1)}, u32[]{:S(2)}) copy-start(bf16[96,288]{1,0:T(8,128)(2,1)} %constant.15.clone.y3_ref) | copy-start | bytes 165892
  6.0 55.7 %collective-permute-start.4 = (bf16[32,6,16,128]{3,2,1,0:T(8,128)(2,1)}, bf16[32,6,16,128]{3,2,1,0:T(8,128)(2,1)S(1)}, u32[]{:S(2)}, u32[]{:S(2)}) collective-permute-start(bf16[32,6,16,128]{3,2,1,0:T(8,128)(2,1)} %slab.3), channel_id=1, source_target_pairs={{0,1},{1,2},{2,3},{3,4},{4,5},{5,6},{6,7},{7,8},{8,9},{9,10},{10,1... | collective-permute-start | bytes 2359304 | tf_op jit(solution)/shard_map/ppermute | solution.py:142
  8.2 53.5 %collective-permute-start.5 = (bf16[32,6,16,128]{3,2,1,0:T(8,128)(2,1)}, bf16[32,6,16,128]{3,2,1,0:T(8,128)(2,1)S(1)}, u32[]{:S(2)}, u32[]{:S(2)}) collective-permute-start(bf16[32,6,16,128]{3,2,1,0:T(8,128)(2,1)} %slab.3), channel_id=1, source_target_pairs={{0,31},{1,0},{2,1},{3,2},{4,3},{5,4},{6,5},{7,6},{8,7},{9,8},{10,9... | collective-permute-start | bytes 2359304 | tf_op jit(solution)/shard_map/ppermute | solution.py:142
  13.3 13.2 %collective-permute-start = (bf16[4,6,16,128]{3,2,1,0:T(8,128)(2,1)S(1)}, bf16[4,6,16,128]{3,2,1,0:T(8,128)(2,1)S(1)}, u32[]{:S(2)}, u32[]{:S(2)}) collective-permute-start(bf16[4,6,16,128]{3,2,1,0:T(8,128)(2,1)S(1)} %convert_element_type.12), channel_id=1, source_target_pairs={{0,2},{1,3},{2,4},{3,5},{4,6},{5,7},{6,8},{7,9},{8,10},{9,11},{10,... | collective-permute-start | bytes 294920 | tf_op jit(solution)/shard_map/ppermute | solution.py:142
  13.5 24.2 %collective-permute-start.1 = (bf16[6,6,16,128]{3,2,1,0:T(8,128)(2,1)S(1)}, bf16[6,6,16,128]{3,2,1,0:T(8,128)(2,1)S(1)}, u32[]{:S(2)}, u32[]{:S(2)}) collective-permute-start(bf16[6,6,16,128]{3,2,1,0:T(8,128)(2,1)S(1)} %pad_maximum_fusion), channel_id=1, source_target_pairs={{0,1},{1,2},{2,3},{3,4},{4,5},{5,6},{6,7},{7,8},{8,9},{9,10},{10,1... | collective-permute-start | bytes 442376 | tf_op jit(solution)/shard_map/ppermute | solution.py:142
  13.5 24.1 %collective-permute-start.2 = (bf16[6,6,16,128]{3,2,1,0:T(8,128)(2,1)S(1)}, bf16[6,6,16,128]{3,2,1,0:T(8,128)(2,1)S(1)}, u32[]{:S(2)}, u32[]{:S(2)}) collective-permute-start(bf16[6,6,16,128]{3,2,1,0:T(8,128)(2,1)S(1)} %pad_maximum_fusion), channel_id=1, source_target_pairs={{0,31},{1,0},{2,1},{3,2},{4,3},{5,4},{6,5},{7,6},{8,7},{9,8},{10,9... | collective-permute-start | bytes 442376 | tf_op jit(solution)/shard_map/ppermute | solution.py:142
  26.5 10.4 %collective-permute-start.3 = (bf16[4,6,16,128]{3,2,1,0:T(8,128)(2,1)S(1)}, bf16[4,6,16,128]{3,2,1,0:T(8,128)(2,1)S(1)}, u32[]{:S(2)}, u32[]{:S(2)}) collective-permute-start(bf16[4,6,16,128]{3,2,1,0:T(8,128)(2,1)S(1)} %convert_element_type.12), channel_id=1, source_target_pairs={{0,30},{1,31},{2,0},{3,1},{4,2},{5,3},{6,4},{7,5},{8,6},{9,7},{10,... | collective-permute-start | bytes 294920 | tf_op jit(solution)/shard_map/ppermute | solution.py:142

commit v3 on v2

v3 whole, which is shorter than its diff:
```python
import jax
import jax.numpy as jnp
import ml_dtypes
import numpy as np
from jax import lax
from jax.experimental import pallas as pl
from jax.experimental.pallas import tpu as pltpu
from jax.sharding import Mesh, PartitionSpec as P

COEFS = (
    -5369.0 / 1800.0,
    12.0 / 7.0,
    -15.0 / 56.0,
    10.0 / 189.0,
    -1.0 / 112.0,
    2.0 / 1925.0,
    -1.0 / 16632.0,
)
SPACING = 0.5
CENTER = 27.5
HALF = 22.5
KIN = -0.5 / SPACING**2
OFF = tuple(KIN * c / HALF for c in COEFS)
DIAG = 3.0 * KIN * COEFS[0] / HALF
SHIFT = CENTER / HALF
BAND = ("z_hi", "core")
DOMAIN = ("z_lo", "x", "y")
CELLS = 393216
W = 6
CY, CZ, PLANES = 16, 128, 6
ROWS = PLANES * CY
BF16, F32 = jnp.bfloat16, jnp.float32


def circulant(n):
    m = np.zeros((n, n), np.float64)
    for i in range(n):
        for k in range(1, W + 1):
            m[i, (i + k) % n] += OFF[k]
            m[i, (i - k) % n] += OFF[k]
    return m


def plane_weights():
    m = np.zeros((PLANES, 3 * PLANES), np.float64)
    for i in range(PLANES):
        for j in range(3 * PLANES):
            k = abs(i + PLANES - j)
            if 1 <= k <= W:
                m[i, j] = OFF[k]
    m = np.kron(m, np.eye(CY))
    m[:, ROWS : 2 * ROWS] += np.kron(np.eye(PLANES), circulant(CY))
    return m


def halves(m):
    high = m.astype(ml_dtypes.bfloat16)
    low = (m - high.astype(np.float64)).astype(ml_dtypes.bfloat16)
    return high, low


Z_HIGH, Z_LOW = halves(circulant(CZ))
Y_HIGH, Y_LOW = halves(np.kron(np.eye(PLANES), circulant(CY)))
Z3 = np.block([[Z_HIGH, Z_LOW], [Z_HIGH, np.zeros_like(Z_LOW)]])
Y3 = np.concatenate([Y_HIGH, Y_HIGH, Y_LOW], 1)
Z2 = np.concatenate([Z_HIGH, Z_LOW], 0)
XY2 = np.concatenate(halves(plane_weights()), 1)


def dot(a, b):
    return jnp.dot(a, b, preferred_element_type=F32)


def along_x(planes, n):
    out = []
    for x in range(W, W + n):
        total = OFF[1] * (planes[x + 1] + planes[x - 1])
        for k in range(2, W + 1):
            total = total + OFF[k] * (planes[x + k] + planes[x - k])
        out.append(total)
    return out


def along_yz(planes, z3, y3):
    n = len(planes)
    field = jnp.concatenate([p[None] for p in planes], 0).reshape(n * CY, CZ)
    high = field.astype(BF16)
    low = (field - high.astype(F32)).astype(BF16)
    z = dot(jnp.concatenate([high, low], 1), z3)
    z = z[:, :CZ] + z[:, CZ:]
    out = []
    for g in range(0, n * CY, ROWS):
        h, l = high[g : g + ROWS], low[g : g + ROWS]
        y = dot(y3, jnp.concatenate([h, l, h], 0)) + z[g : g + ROWS]
        out += [y[i * CY : (i + 1) * CY] for i in range(PLANES)]
    return out


def filter_kernel(
    even, odd, even2, odd2, even3, odd3, s, pot, z3_ref, y3_ref, z2_ref, xy2_ref, out
):
    count = s.shape[0]
    place = lax.axis_index("y")
    first_of_pair = place % 2 == 0
    first_of_two = place < 2
    z3, y3, z2, xy2 = z3_ref[...], y3_ref[...], z2_ref[...], xy2_ref[...]

    def sides(i, one, other, flag):
        before, after = [], []
        for x in range(PLANES):
            a, b = one[i, x].astype(F32), other[i, x].astype(F32)
            before.append(jnp.where(flag, b, a))
            after.append(jnp.where(flag, a, b))
        return before, after

    def sums(one, other, flag):
        high, low = sides(count, one, other, flag), sides(count + 1, one, other, flag)
        return [[h + l for h, l in zip(*pair)] for pair in zip(high, low)]

    b1, a1 = sums(even, odd, first_of_pair)
    b2, a2 = sums(even2, odd2, first_of_two)
    raw = b2 + b1 + [pot[x] for x in range(PLANES)] + a1 + a2
    diag = [(DIAG - SHIFT) + v * (1.0 / HALF) for v in raw]

    def turn(planes, weights):
        inner = planes[W:-W]
        x = along_x(planes, len(inner))
        yz = along_yz(inner, z3, y3)
        return [a + b + d * v for a, b, d, v in zip(x, yz, weights, inner)]

    for i in range(count):
        b1, a1 = sides(i, even, odd, first_of_pair)
        b2, a2 = sides(i, even2, odd2, first_of_two)
        b3, a3 = sides(i, even3, odd3, first_of_pair)
        field = b3 + b2 + b1 + [s[i, x] for x in range(PLANES)] + a1 + a2 + a3
        first = turn(field, diag)
        second = turn(first, diag[W:-W])
        rounded = [
            (2.0 * t - v).astype(BF16) for t, v in zip(second, field[2 * W : -2 * W])
        ]
        blocks = [jnp.concatenate(rounded[k * W : (k + 1) * W], 0) for k in range(3)]
        own = blocks[1]
        xy = dot(xy2, jnp.concatenate(blocks + blocks, 0))
        z = dot(jnp.concatenate([own, own], 1), z2)
        for x in range(PLANES):
            rows = slice(x * CY, (x + 1) * CY)
            total = xy[rows] + z[rows] + (diag[2 * W + x] + SHIFT) * rounded[W + x].astype(F32)
            out[i, x] = rounded[W + x]
            out[count + i, x] = total.astype(BF16)


def exchange(array, axes, size, partner):
    return lax.ppermute(array, axes, [(i, partner(i) % size) for i in range(size)])


def even_pairs(array):
    return exchange(array, DOMAIN, 32, lambda d: d ^ 1)


def odd_pairs(array):
    return exchange(array, DOMAIN, 32, lambda d: d + 1 if d % 2 else d - 1)


def even_twos(array):
    return exchange(array, DOMAIN, 32, lambda d: d ^ 2)


def odd_twos(array):
    return exchange(array, DOMAIN, 32, lambda d: d + 2 if d % 4 >= 2 else d - 2)


def even_threes(array):
    return exchange(array, DOMAIN, 32, lambda d: d - 3 if d % 2 else d + 3)


def odd_threes(array):
    return exchange(array, DOMAIN, 32, lambda d: d + 3 if d % 2 else d - 3)


def vmem(n=1):
    return [pl.BlockSpec(memory_space=pltpu.VMEM)] * n


def filter_own(pairs, twos, threes, s, pot):
    constants = [jnp.asarray(m) for m in (Z3, Y3, Z2, XY2)]
    return pl.pallas_call(
        filter_kernel,
        out_shape=jax.ShapeDtypeStruct((2 * s.shape[0], *s.shape[1:]), BF16),
        in_specs=vmem(12),
        out_specs=vmem()[0],
        compiler_params=pltpu.CompilerParams(vmem_limit_bytes=16 << 20),
        cost_estimate=pl.CostEstimate(flops=400_000_000, bytes_accessed=1_500_000, transcendentals=0),
        name="filter_own",
    )(*pairs, *twos, *threes, s, pot, *constants)


def body(states, potential, slab):
    count = states.shape[0]
    low = states.astype(BF16)
    pot_high = potential.astype(BF16)
    pot_low = (potential - pot_high.astype(F32)).astype(BF16)
    near = jnp.concatenate([low, pot_high[None], pot_low[None]], axis=0)
    pairs = even_pairs(near), odd_pairs(near)
    twos = even_twos(near), odd_twos(near)
    threes = even_threes(low), odd_threes(low)
    both = filter_own(pairs, twos, threes, states, potential)
    mine = lax.all_gather(both, "z_hi", axis=0, tiled=True)
    theirs = exchange(mine, "core", 2, lambda i: i ^ 1)

    n = slab.shape[0]
    slab_flat = slab.reshape(n, -1)

    def products(block):
        flat = block.reshape(block.shape[0], -1)
        out = lax.dot_general(
            flat, slab_flat, (((1,), (1,)), ((), ())), preferred_element_type=F32
        )
        return jnp.swapaxes(out.reshape(4, 2, count, n), 1, 2)

    pair = jnp.stack([products(mine), products(theirs)], axis=1)
    pair = jnp.where(lax.axis_index("core") == 1, jnp.flip(pair, 1), pair)
    term = pair.reshape(32, 2 * n)
    parts = lax.all_to_all(term, DOMAIN, 0, 0, tiled=True)
    scale = 1.0 / jnp.sqrt(jnp.float32(CELLS))
    share = jnp.sum(parts, axis=0, keepdims=True) * scale
    return share[:, :n], share[:, n:]


def solution(mesh):
    fine = Mesh(mesh.devices.reshape(4, 2, 2, 4, 4), ("z_hi", "core", "z_lo", "x", "y"))
    placed = (P(BAND, DOMAIN, None, None), P(DOMAIN, None, None), P(BAND, DOMAIN, None, None))
    return jax.shard_map(
        body,
        mesh=fine,
        in_specs=placed,
        out_specs=(P(DOMAIN, BAND), P(DOMAIN, BAND)),
        check_vma=False,
    )
```

time: 83 us -> 64.5 us (0.78)
  blocking collectives: 37.9 us -> 32.6 us
  Pallas kernels: 7.04 us -> 2.4 us
  waiting for transfers between devices: 11.2 us -> 6.75 us
  starting transfers between devices: 20.3 us -> 18.1 us
  local copies, waits for them, and re-layouts: 3.03 us -> 1.51 us
  matrix products: 2.19 us -> 1.02 us
  other arithmetic: 0.18 us -> 1.1 us
    pallas_call x3 -> x1, Pallas kernels: 7.04 us -> 2.4 us  [filter_own(): pl.pallas_call(filter_kernel, out_shape=jax.ShapeDtypeStruct((2 * s.shape...]
    ppermute x6 -> x7, waiting for transfers between devices: 11.2 us -> 6.75 us  [exchange(): lax.ppermute(array, axes, [(i, partner(i) % size) for i in range(size)])]
    all_to_all x1, blocking collectives: 16.8 us -> 12.6 us  [body(): parts = lax.all_to_all(term, DOMAIN, 0, 0, tiled=True)]
    unnamed x14, local copies, waits for them, and re-layouts: 2.44 us -> 0.04 us
    ppermute x6 -> x7, starting transfers between devices: 20.3 us -> 18.1 us  [exchange(): lax.ppermute(array, axes, [(i, partner(i) % size) for i in range(size)])]
    dot_general x2, matrix products: 2.19 us -> 1.02 us  [products(): lax.dot_general(flat, slab_flat, (((1,), (1,)), ((), ())), preferred_elem...]
    all_gather x1, blocking collectives: 21.2 us -> 20 us  [body(): mine = lax.all_gather(both, 'z_hi', axis=0, tiled=True)]
    convert_element_type x1, other arithmetic: 0.02 us -> 0.99 us  [body(): low = states.astype(BF16)]
  transfers between devices with their start and end apart: 6 -> 7, of which waited for: 3 -> 3; matrix products, arithmetic and copies ran while one was open for 2% -> 2% of each run, Pallas kernels for 1% -> 0%
where the time goes in v3:
time: 64.5 us; the launch traced here: 64.3 us
  blocking collectives  32.6 us (51%)
  starting transfers between devices  18.1 us (28%)
  waiting for transfers between devices  6.75 us (10%)
  Pallas kernels  2.4 us (4%)
  local copies, waits for them, and re-layouts  1.51 us (2%)
  other arithmetic  1.1 us (2%)
  matrix products  1.02 us (2%)
  between operations  0.79 us (1%)
    all_gather x1, blocking collectives, body(): mine = lax.all_gather(both, 'z_hi', axis=0, tiled=True)  20 us
    ppermute x7, starting transfers between devices, exchange(): lax.ppermute(array, axes, [(i, partner(i) % size) for i in range(size)])  18.1 us
    all_to_all x1, blocking collectives, body(): parts = lax.all_to_all(term, DOMAIN, 0, 0, tiled=True)  12.6 us
    ppermute x7, waiting for transfers between devices, exchange(): lax.ppermute(array, axes, [(i, partner(i) % size) for i in range(size)])  6.75 us
    pallas_call x1, Pallas kernels, filter_own(): pl.pallas_call(filter_kernel, out_shape=jax.ShapeDtypeStruct((2 * s.shape...  2.4 us
  transfers between devices with their start and end apart: 7, of which 3 were waited for; matrix products, arithmetic and copies ran while one was open for 2% of the time, Pallas kernels for 0%

profile of v3, /device:TPU:1, one launch (start us, length us, event | category | flops | bytes accessed | tf_op | source)
XLA Modules:
  0.0 64.3 jit_solution(5034461461210773273)
XLA Ops:
  0.6 0.0 copy-start.1
  0.6 0.0 copy-start.3
  0.7 0.0 copy-start.4
  0.7 1.0 %convert_element_type.12 = bf16[4,6,16,128]{3,2,1,0:T(8,128)(2,1)S(1)} convert(f32[4,6,16,128]{3,2,1,0:T(8,128)} %s.1) | non-fusion elementwise | flops 49152 | bytes 294912 | tf_op jit(solution)/shard_map/convert_element_type | solution.py:199
  1.7 0.0 copy-start
  1.7 3.7 %collective-permute-start.4 = (bf16[4,6,16,128]{3,2,1,0:T(8,128)(2,1)S(1)}, bf16[4,6,16,128]{3,2,1,0:T(8,128)(2,1)S(1)}, u32[]{:S(2)}, u32[]{:S(2)}) collective-permute-start(bf16[4,6,16,128]{3,2,1,0:T(8,128)(2,1)S(1)} %convert_element_type.12), channel_id=1, source_target_pairs={{0,3},{1,30},{2,5},{3,0},{4,7},{5,2},{6,9},{7,4},{8,11},{9,6},{10,... | collective-permute-start | bytes 294920 | tf_op jit(solution)/shard_map/ppermute | solution.py:153
  5.3 0.0 copy-done.1
  5.3 0.0 copy-start.2
  5.3 0.0 copy-start.5
  5.4 3.5 %collective-permute-start = (bf16[6,6,16,128]{3,2,1,0:T(8,128)(2,1)S(1)}, bf16[6,6,16,128]{3,2,1,0:T(8,128)(2,1)S(1)}, u32[]{:S(2)}, u32[]{:S(2)}) collective-permute-start(bf16[6,6,16,128]{3,2,1,0:T(8,128)(2,1)S(1)} %pad_maximum_fusion), channel_id=1, source_target_pairs={{0,1},{1,0},{2,3},{3,2},{4,5},{5,4},{6,7},{7,6},{8,9},{9,8},{10,11... | collective-permute-start | bytes 442376 | tf_op jit(solution)/shard_map/ppermute | solution.py:153
  8.9 0.6 collective-permute-start.1
  9.5 1.3 %collective-permute-start.2 = (bf16[6,6,16,128]{3,2,1,0:T(8,128)(2,1)S(1)}, bf16[6,6,16,128]{3,2,1,0:T(8,128)(2,1)S(1)}, u32[]{:S(2)}, u32[]{:S(2)}) collective-permute-start(bf16[6,6,16,128]{3,2,1,0:T(8,128)(2,1)S(1)} %pad_maximum_fusion), channel_id=1, source_target_pairs={{0,2},{1,3},{2,0},{3,1},{4,6},{5,7},{6,4},{7,5},{8,10},{9,11},{10,... | collective-permute-start | bytes 442376 | tf_op jit(solution)/shard_map/ppermute | solution.py:153
  10.8 2.8 %collective-permute-start.3 = (bf16[6,6,16,128]{3,2,1,0:T(8,128)(2,1)S(1)}, bf16[6,6,16,128]{3,2,1,0:T(8,128)(2,1)S(1)}, u32[]{:S(2)}, u32[]{:S(2)}) collective-permute-start(bf16[6,6,16,128]{3,2,1,0:T(8,128)(2,1)S(1)} %pad_maximum_fusion), channel_id=1, source_target_pairs={{0,30},{1,31},{2,4},{3,5},{4,2},{5,3},{6,8},{7,9},{8,6},{9,7},{10,... | collective-permute-start | bytes 442376 | tf_op jit(solution)/shard_map/ppermute | solution.py:153
  13.5 0.0 collective-permute-done.4.even3
  13.5 1.6 %collective-permute-start.5 = (bf16[4,6,16,128]{3,2,1,0:T(8,128)(2,1)S(1)}, bf16[4,6,16,128]{3,2,1,0:T(8,128)(2,1)S(1)}, u32[]{:S(2)}, u32[]{:S(2)}) collective-permute-start(bf16[4,6,16,128]{3,2,1,0:T(8,128)(2,1)S(1)} %convert_element_type.12), channel_id=1, source_target_pairs={{0,29},{1,4},{2,31},{3,6},{4,1},{5,8},{6,3},{7,10},{8,5},{9,12},{1... | collective-permute-start | bytes 294920 | tf_op jit(solution)/shard_map/ppermute | solution.py:153
  15.2 5.1 %collective-permute-done.5.odd3 = bf16[4,6,16,128]{3,2,1,0:T(8,128)(2,1)S(1)} collective-permute-done((bf16[4,6,16,128]{3,2,1,0:T(8,128)(2,1)S(1)}, bf16[4,6,16,128]{3,2,1,0:T(8,128)(2,1)S(1)}, u32[]{:S(2)}, u32[]{:S(2)}) %collective-permute-start.5) | collective-permute-done | bytes 98336 | tf_op jit(solution)/shard_map/ppermute | solution.py:153
  20.3 0.0 collective-permute-done.even
  20.3 0.0 collective-permute-done.1.odd
  20.3 0.0 collective-permute-done.2.even2
  20.3 0.8 %collective-permute-done.3.odd2 = bf16[6,6,16,128]{3,2,1,0:T(8,128)(2,1)S(1)} collective-permute-done((bf16[6,6,16,128]{3,2,1,0:T(8,128)(2,1)S(1)}, bf16[6,6,16,128]{3,2,1,0:T(8,128)(2,1)S(1)}, u32[]{:S(2)}, u32[]{:S(2)}) %collective-permute-start.3) | collective-permute-done | bytes 147488 | tf_op jit(solution)/shard_map/ppermute | solution.py:153
  21.1 0.0 copy-done.3
  21.1 0.0 copy-done.4
  21.1 0.0 copy-done
  21.1 0.0 copy-done.2
  21.1 0.0 copy-done.5
  21.1 2.4 %filter_own.1 = bf16[8,6,16,128]{3,2,1,0:T(8,128)(2,1)S(1)} custom-call(bf16[6,6,16,128]{3,2,1,0:T(8,128)(2,1)S(1)} %collective-permute-done.even, bf16[6,6,16,128]{3,2,1,0:T(8,128)(2,1)S(1)} %collective-permute-done.1.odd, bf16[6,6,16,128]{3,2,1,0:T(8,128)(2,1)S(1)} %collective-permute-done.2.even2, ...), custom_call_target="tpu_custom_call" | custom-call | flops 400000000 | bytes 1500000 | tf_op jit(solution)/shard_map/filter_own/pallas_call | solution.py:186
  23.5 0.0 copy-start.6
  23.5 20.0 %all_gather.3 = bf16[32,6,16,128]{3,2,1,0:T(8,128)(2,1)S(1)} all-gather(bf16[8,6,16,128]{3,2,1,0:T(8,128)(2,1)S(1)} %filter_own.1), channel_id=1, replica_groups=mesh['z_hi'=4,'core'=2,'z_lo'=2,'x'=4,'y'=4] {'z_hi'}, dimensions={0}, use_global_device_ids=true | all-gather | bytes 983040 | tf_op jit(solution)/shard_map/all_gather | solution.py:207
  43.6 4.7 %collective-permute-start.6 = (bf16[32,6,16,128]{3,2,1,0:T(8,128)(2,1)S(1)}, bf16[32,6,16,128]{3,2,1,0:T(8,128)(2,1)S(1)}, u32[]{:S(2)}, u32[]{:S(2)}) collective-permute-start(bf16[32,6,16,128]{3,2,1,0:T(8,128)(2,1)S(1)} %all_gather.3), channel_id=1, source_target_pairs={{0,32},{32,0},{1,33},{33,1},{2,34},{34,2},{3,35},{35,3},{4,36},{36... | collective-permute-start | bytes 2359304 | tf_op jit(solution)/shard_map/ppermute | solution.py:153
  48.3 0.0 copy-done.6
  48.3 0.3 reshape.30
  48.6 0.2 dot_general.10
  48.8 0.5 convolution_bitcast_fusion.1
  49.3 0.8 %collective-permute-done.6 = bf16[32,6,16,128]{3,2,1,0:T(8,128)(2,1)S(1)} collective-permute-done((bf16[32,6,16,128]{3,2,1,0:T(8,128)(2,1)S(1)}, bf16[32,6,16,128]{3,2,1,0:T(8,128)(2,1)S(1)}, u32[]{:S(2)}, u32[]{:S(2)}) %collective-permute-start.6) | collective-permute-done | bytes 786464 | tf_op jit(solution)/shard_map/ppermute | solution.py:153
  50.2 0.2 dot_general.12
  50.4 0.5 convolution_bitcast_fusion
  51.0 0.1 all_to_all.6
  51.1 12.6 %all_to_all.9 = f32[32,1,64]{2,1,0:T(1,128)S(1)} all-to-all(f32[32,1,64]{2,1,0:T(1,128)S(1)} %bitcast.28), channel_id=1, replica_groups=mesh['z_hi'=4,'core'=2,'z_lo'=2,'x'=4,'y'=4] {'z_lo','x','y'}, dimensions={0} | all-to-all | bytes 16384 | tf_op jit(solution)/shard_map/all_to_all | solution.py:223
  63.7 0.1 reduce_sum.9
  63.7 0.6 fusion.3
  (6 shorter events, 0.1 us)
Async XLA Ops:
  0.6 4.7 %copy-start.1 = (f32[6,16,128]{2,1,0:T(8,128)S(1)}, f32[6,16,128]{2,1,0:T(8,128)}, u32[]{:S(2)}) copy-start(f32[6,16,128]{2,1,0:T(8,128)} %pot.1) | copy-start | bytes 147460
  0.6 20.4 %copy-start.3 = (bf16[96,576]{1,0:T(8,128)(2,1)S(1)}, bf16[96,576]{1,0:T(8,128)(2,1)}, u32[]{:S(2)}) copy-start(bf16[96,576]{1,0:T(8,128)(2,1)} %constant.23.clone.xy2_ref) | copy-start | bytes 331780
  0.7 20.4 %copy-start.4 = (bf16[96,288]{1,0:T(8,128)(2,1)S(1)}, bf16[96,288]{1,0:T(8,128)(2,1)}, u32[]{:S(2)}) copy-start(bf16[96,288]{1,0:T(8,128)(2,1)} %constant.21.clone.y3_ref) | copy-start | bytes 165892
  1.7 19.4 %copy-start = (f32[4,6,16,128]{3,2,1,0:T(8,128)S(1)}, f32[4,6,16,128]{3,2,1,0:T(8,128)}, u32[]{:S(2)}) copy-start(f32[4,6,16,128]{3,2,1,0:T(8,128)} %s.1) | copy-start | bytes 589828
  1.7 11.9 %collective-permute-start.4 = (bf16[4,6,16,128]{3,2,1,0:T(8,128)(2,1)S(1)}, bf16[4,6,16,128]{3,2,1,0:T(8,128)(2,1)S(1)}, u32[]{:S(2)}, u32[]{:S(2)}) collective-permute-start(bf16[4,6,16,128]{3,2,1,0:T(8,128)(2,1)S(1)} %convert_element_type.12), channel_id=1, source_target_pairs={{0,3},{1,30},{2,5},{3,0},{4,7},{5,2},{6,9},{7,4},{8,11},{9,6},{10,... | collective-permute-start | bytes 294920 | tf_op jit(solution)/shard_map/ppermute | solution.py:153
  5.3 15.8 %copy-start.2 = (bf16[256,256]{1,0:T(8,128)(2,1)S(1)}, bf16[256,256]{1,0:T(8,128)(2,1)}, u32[]{:S(2)}) copy-start(bf16[256,256]{1,0:T(8,128)(2,1)} %constant.20.clone.z3_ref) | copy-start | bytes 393220
  5.3 15.8 %copy-start.5 = (bf16[256,128]{1,0:T(8,128)(2,1)S(1)}, bf16[256,128]{1,0:T(8,128)(2,1)}, u32[]{:S(2)}) copy-start(bf16[256,128]{1,0:T(8,128)(2,1)} %constant.22.clone.z2_ref) | copy-start | bytes 196612
  5.4 14.9 %collective-permute-start = (bf16[6,6,16,128]{3,2,1,0:T(8,128)(2,1)S(1)}, bf16[6,6,16,128]{3,2,1,0:T(8,128)(2,1)S(1)}, u32[]{:S(2)}, u32[]{:S(2)}) collective-permute-start(bf16[6,6,16,128]{3,2,1,0:T(8,128)(2,1)S(1)} %pad_maximum_fusion), channel_id=1, source_target_pairs={{0,1},{1,0},{2,3},{3,2},{4,5},{5,4},{6,7},{7,6},{8,9},{9,8},{10,11... | collective-permute-start | bytes 442376 | tf_op jit(solution)/shard_map/ppermute | solution.py:153
  8.9 11.4 %collective-permute-start.1 = (bf16[6,6,16,128]{3,2,1,0:T(8,128)(2,1)S(1)}, bf16[6,6,16,128]{3,2,1,0:T(8,128)(2,1)S(1)}, u32[]{:S(2)}, u32[]{:S(2)}) collective-permute-start(bf16[6,6,16,128]{3,2,1,0:T(8,128)(2,1)S(1)} %pad_maximum_fusion), channel_id=1, source_target_pairs={{0,31},{1,2},{2,1},{3,4},{4,3},{5,6},{6,5},{7,8},{8,7},{9,10},{10,... | collective-permute-start | bytes 442376 | tf_op jit(solution)/shard_map/ppermute | solution.py:153
  9.5 10.8 %collective-permute-start.2 = (bf16[6,6,16,128]{3,2,1,0:T(8,128)(2,1)S(1)}, bf16[6,6,16,128]{3,2,1,0:T(8,128)(2,1)S(1)}, u32[]{:S(2)}, u32[]{:S(2)}) collective-permute-start(bf16[6,6,16,128]{3,2,1,0:T(8,128)(2,1)S(1)} %pad_maximum_fusion), channel_id=1, source_target_pairs={{0,2},{1,3},{2,0},{3,1},{4,6},{5,7},{6,4},{7,5},{8,10},{9,11},{10,... | collective-permute-start | bytes 442376 | tf_op jit(solution)/shard_map/ppermute | solution.py:153
  10.8 10.3 %collective-permute-start.3 = (bf16[6,6,16,128]{3,2,1,0:T(8,128)(2,1)S(1)}, bf16[6,6,16,128]{3,2,1,0:T(8,128)(2,1)S(1)}, u32[]{:S(2)}, u32[]{:S(2)}) collective-permute-start(bf16[6,6,16,128]{3,2,1,0:T(8,128)(2,1)S(1)} %pad_maximum_fusion), channel_id=1, source_target_pairs={{0,30},{1,31},{2,4},{3,5},{4,2},{5,3},{6,8},{7,9},{8,6},{9,7},{10,... | collective-permute-start | bytes 442376 | tf_op jit(solution)/shard_map/ppermute | solution.py:153
  13.5 6.8 %collective-permute-start.5 = (bf16[4,6,16,128]{3,2,1,0:T(8,128)(2,1)S(1)}, bf16[4,6,16,128]{3,2,1,0:T(8,128)(2,1)S(1)}, u32[]{:S(2)}, u32[]{:S(2)}) collective-permute-start(bf16[4,6,16,128]{3,2,1,0:T(8,128)(2,1)S(1)} %convert_element_type.12), channel_id=1, source_target_pairs={{0,29},{1,4},{2,31},{3,6},{4,1},{5,8},{6,3},{7,10},{8,5},{9,12},{1... | collective-permute-start | bytes 294920 | tf_op jit(solution)/shard_map/ppermute | solution.py:153
  23.5 24.7 %copy-start.6 = (bf16[32,6,16,128]{3,2,1,0:T(8,128)(2,1)S(1)}, bf16[32,6,16,128]{3,2,1,0:T(8,128)(2,1)}, u32[]{:S(2)}) copy-start(bf16[32,6,16,128]{3,2,1,0:T(8,128)(2,1)} %param.9) | copy-start | bytes 2359300
  43.6 6.6 %collective-permute-start.6 = (bf16[32,6,16,128]{3,2,1,0:T(8,128)(2,1)S(1)}, bf16[32,6,16,128]{3,2,1,0:T(8,128)(2,1)S(1)}, u32[]{:S(2)}, u32[]{:S(2)}) collective-permute-start(bf16[32,6,16,128]{3,2,1,0:T(8,128)(2,1)S(1)} %all_gather.3), channel_id=1, source_target_pairs={{0,32},{32,0},{1,33},{33,1},{2,34},{34,2},{3,35},{35,3},{4,36},{36... | collective-permute-start | bytes 2359304 | tf_op jit(solution)/shard_map/ppermute | solution.py:153

commit v4 on v3

--- a/solution.py
+++ b/solution.py
@@ -63,8 +63,8 @@
 Y_HIGH, Y_LOW = halves(np.kron(np.eye(PLANES), circulant(CY)))
 Z3 = np.block([[Z_HIGH, Z_LOW], [Z_HIGH, np.zeros_like(Z_LOW)]])
 Y3 = np.concatenate([Y_HIGH, Y_HIGH, Y_LOW], 1)
-Z2 = np.concatenate([Z_HIGH, Z_LOW], 0)
 XY2 = np.concatenate(halves(plane_weights()), 1)
+LEFT = np.concatenate([Y3, XY2], 1)
 
 
 def dot(a, b):
@@ -97,13 +97,14 @@
 
 
 def filter_kernel(
-    even, odd, even2, odd2, even3, odd3, s, pot, z3_ref, y3_ref, z2_ref, xy2_ref, out
+    even, odd, even2, odd2, even3, odd3, s, pot, z3_ref, left_ref, out
 ):
     count = s.shape[0]
     place = lax.axis_index("y")
     first_of_pair = place % 2 == 0
     first_of_two = place < 2
-    z3, y3, z2, xy2 = z3_ref[...], y3_ref[...], z2_ref[...], xy2_ref[...]
+    z3, left = z3_ref[...], left_ref[...]
+    y3, xy2 = left[:, : 3 * ROWS], left[:, 3 * ROWS :]
 
     def sides(i, one, other, flag):
         before, after = [], []
@@ -113,12 +114,8 @@
             after.append(jnp.where(flag, a, b))
         return before, after
 
-    def sums(one, other, flag):
-        high, low = sides(count, one, other, flag), sides(count + 1, one, other, flag)
-        return [[h + l for h, l in zip(*pair)] for pair in zip(high, low)]
-
-    b1, a1 = sums(even, odd, first_of_pair)
-    b2, a2 = sums(even2, odd2, first_of_two)
+    b1, a1 = sides(count, even, odd, first_of_pair)
+    b2, a2 = sides(count, even2, odd2, first_of_two)
     raw = b2 + b1 + [pot[x] for x in range(PLANES)] + a1 + a2
     diag = [(DIAG - SHIFT) + v * (1.0 / HALF) for v in raw]
 
@@ -141,7 +138,8 @@
         blocks = [jnp.concatenate(rounded[k * W : (k + 1) * W], 0) for k in range(3)]
         own = blocks[1]
         xy = dot(xy2, jnp.concatenate(blocks + blocks, 0))
-        z = dot(jnp.concatenate([own, own], 1), z2)
+        z = dot(own, z3[:CZ])
+        z = z[:, :CZ] + z[:, CZ:]
         for x in range(PLANES):
             rows = slice(x * CY, (x + 1) * CY)
             total = xy[rows] + z[rows] + (diag[2 * W + x] + SHIFT) * rounded[W + x].astype(F32)
@@ -182,11 +180,11 @@
 
 
 def filter_own(pairs, twos, threes, s, pot):
-    constants = [jnp.asarray(m) for m in (Z3, Y3, Z2, XY2)]
+    constants = [jnp.asarray(m) for m in (Z3, LEFT)]
     return pl.pallas_call(
         filter_kernel,
         out_shape=jax.ShapeDtypeStruct((2 * s.shape[0], *s.shape[1:]), BF16),
-        in_specs=vmem(12),
+        in_specs=vmem(10),
         out_specs=vmem()[0],
         compiler_params=pltpu.CompilerParams(vmem_limit_bytes=16 << 20),
         cost_estimate=pl.CostEstimate(flops=400_000_000, bytes_accessed=1_500_000, transcendentals=0),
@@ -197,32 +195,30 @@
 def body(states, potential, slab):
     count = states.shape[0]
     low = states.astype(BF16)
-    pot_high = potential.astype(BF16)
-    pot_low = (potential - pot_high.astype(F32)).astype(BF16)
-    near = jnp.concatenate([low, pot_high[None], pot_low[None]], axis=0)
+    near = jnp.concatenate([low, potential.astype(BF16)[None]], axis=0)
     pairs = even_pairs(near), odd_pairs(near)
     twos = even_twos(near), odd_twos(near)
     threes = even_threes(low), odd_threes(low)
     both = filter_own(pairs, twos, threes, states, potential)
     mine = lax.all_gather(both, "z_hi", axis=0, tiled=True)
-    theirs = exchange(mine, "core", 2, lambda i: i ^ 1)
+    theirs = lax.optimization_barrier(exchange(mine, "core", 2, lambda i: i ^ 1))
 
     n = slab.shape[0]
-    slab_flat = slab.reshape(n, -1)
 
     def products(block):
-        flat = block.reshape(block.shape[0], -1)
-        out = lax.dot_general(
-            flat, slab_flat, (((1,), (1,)), ((), ())), preferred_element_type=F32
+        return lax.dot_general(
+            block.reshape(block.shape[0], -1),
+            slab.reshape(n, -1),
+            (((1,), (1,)), ((), ())),
+            preferred_element_type=F32,
         )
-        return jnp.swapaxes(out.reshape(4, 2, count, n), 1, 2)
-
-    pair = jnp.stack([products(mine), products(theirs)], axis=1)
-    pair = jnp.where(lax.axis_index("core") == 1, jnp.flip(pair, 1), pair)
-    term = pair.reshape(32, 2 * n)
+
+    out = lax.optimization_barrier((products(mine), products(theirs)))
+    pair = jnp.stack(out).reshape(2, 4, 2, count, n) * (1.0 / np.sqrt(np.float32(CELLS)))
+    pair = jnp.where(lax.axis_index("core") == 1, jnp.flip(pair, 0), pair)
+    term = jnp.transpose(pair, (1, 0, 3, 2, 4)).reshape(32, 2 * n)
     parts = lax.all_to_all(term, DOMAIN, 0, 0, tiled=True)
-    scale = 1.0 / jnp.sqrt(jnp.float32(CELLS))
-    share = jnp.sum(parts, axis=0, keepdims=True) * scale
+    share = jnp.sum(parts, axis=0, keepdims=True)
     return share[:, :n], share[:, n:]
 
 

time: 64.5 us -> 62.5 us (0.969)
  blocking collectives: 32.6 us -> 31.5 us
  local copies, waits for them, and re-layouts: 1.51 us -> 0.73 us
    all_to_all x1, blocking collectives: 12.6 us -> 11.8 us  [body(): parts = lax.all_to_all(term, DOMAIN, 0, 0, tiled=True)]
  transfers between devices with their start and end apart: 7 -> 7, of which waited for: 3 -> 2; matrix products, arithmetic and copies ran while one was open for 2% -> 1% of each run, Pallas kernels for 0% -> 0%
where the time goes in v4:
time: 62.5 us; the launch traced here: 62.4 us
  blocking collectives  31.5 us (50%)
  starting transfers between devices  18.3 us (29%)
  waiting for transfers between devices  6.54 us (10%)
  Pallas kernels  2.39 us (4%)
  other arithmetic  1.12 us (2%)
  matrix products  1.05 us (2%)
  between operations  0.75 us (1%)
  local copies, waits for them, and re-layouts  0.73 us (1%)
    all_gather x1, blocking collectives, body(): mine = lax.all_gather(both, 'z_hi', axis=0, tiled=True)  19.7 us
    ppermute x7, starting transfers between devices, exchange(): lax.ppermute(array, axes, [(i, partner(i) % size) for i in range(size)])  18.3 us
    all_to_all x1, blocking collectives, body(): parts = lax.all_to_all(term, DOMAIN, 0, 0, tiled=True)  11.8 us
    ppermute x7, waiting for transfers between devices, exchange(): lax.ppermute(array, axes, [(i, partner(i) % size) for i in range(size)])  6.54 us
    pallas_call x1, Pallas kernels, filter_own(): pl.pallas_call(filter_kernel, out_shape=jax.ShapeDtypeStruct((2 * s.shape...  2.39 us
  transfers between devices with their start and end apart: 7, of which 2 were waited for; matrix products, arithmetic and copies ran while one was open for 1% of the time, Pallas kernels for 0%

profile of v4, /device:TPU:1, one launch (start us, length us, event | category | flops | bytes accessed | tf_op | source)
XLA Modules:
  0.0 62.4 jit_solution(5859095375560086228)
XLA Ops:
  0.6 0.0 copy-start
  0.6 0.0 copy-start.2
  0.7 0.0 copy-start.3
  0.7 0.0 copy-start.4
  0.7 1.0 %convert_element_type.6 = bf16[4,6,16,128]{3,2,1,0:T(8,128)(2,1)S(1)} convert(f32[4,6,16,128]{3,2,1,0:T(8,128)} %s.1) | non-fusion elementwise | flops 49152 | bytes 294912 | tf_op jit(solution)/shard_map/convert_element_type | solution.py:197
  1.7 0.0 copy-start.1
  1.7 3.7 %collective-permute-start.4 = (bf16[4,6,16,128]{3,2,1,0:T(8,128)(2,1)S(1)}, bf16[4,6,16,128]{3,2,1,0:T(8,128)(2,1)S(1)}, u32[]{:S(2)}, u32[]{:S(2)}) collective-permute-start(bf16[4,6,16,128]{3,2,1,0:T(8,128)(2,1)S(1)} %convert_element_type.6), channel_id=1, source_target_pairs={{0,3},{1,30},{2,5},{3,0},{4,7},{5,2},{6,9},{7,4},{8,11},{9,6},{10,... | collective-permute-start | bytes 294920 | tf_op jit(solution)/shard_map/ppermute | solution.py:151
  5.4 0.0 copy-done.2
  5.4 3.5 %collective-permute-start = (bf16[5,6,16,128]{3,2,1,0:T(8,128)(2,1)S(1)}, bf16[5,6,16,128]{3,2,1,0:T(8,128)(2,1)S(1)}, u32[]{:S(2)}, u32[]{:S(2)}) collective-permute-start(bf16[5,6,16,128]{3,2,1,0:T(8,128)(2,1)S(1)} %pad_maximum_fusion), channel_id=1, source_target_pairs={{0,1},{1,0},{2,3},{3,2},{4,5},{5,4},{6,7},{7,6},{8,9},{9,8},{10,11... | collective-permute-start | bytes 368648 | tf_op jit(solution)/shard_map/ppermute | solution.py:151
  8.9 0.6 %collective-permute-start.1 = (bf16[5,6,16,128]{3,2,1,0:T(8,128)(2,1)S(1)}, bf16[5,6,16,128]{3,2,1,0:T(8,128)(2,1)S(1)}, u32[]{:S(2)}, u32[]{:S(2)}) collective-permute-start(bf16[5,6,16,128]{3,2,1,0:T(8,128)(2,1)S(1)} %pad_maximum_fusion), channel_id=1, source_target_pairs={{0,31},{1,2},{2,1},{3,4},{4,3},{5,6},{6,5},{7,8},{8,7},{9,10},{10,... | collective-permute-start | bytes 368648 | tf_op jit(solution)/shard_map/ppermute | solution.py:151
  9.5 1.3 %collective-permute-start.2 = (bf16[5,6,16,128]{3,2,1,0:T(8,128)(2,1)S(1)}, bf16[5,6,16,128]{3,2,1,0:T(8,128)(2,1)S(1)}, u32[]{:S(2)}, u32[]{:S(2)}) collective-permute-start(bf16[5,6,16,128]{3,2,1,0:T(8,128)(2,1)S(1)} %pad_maximum_fusion), channel_id=1, source_target_pairs={{0,2},{1,3},{2,0},{3,1},{4,6},{5,7},{6,4},{7,5},{8,10},{9,11},{10,... | collective-permute-start | bytes 368648 | tf_op jit(solution)/shard_map/ppermute | solution.py:151
  10.8 2.8 %collective-permute-start.3 = (bf16[5,6,16,128]{3,2,1,0:T(8,128)(2,1)S(1)}, bf16[5,6,16,128]{3,2,1,0:T(8,128)(2,1)S(1)}, u32[]{:S(2)}, u32[]{:S(2)}) collective-permute-start(bf16[5,6,16,128]{3,2,1,0:T(8,128)(2,1)S(1)} %pad_maximum_fusion), channel_id=1, source_target_pairs={{0,30},{1,31},{2,4},{3,5},{4,2},{5,3},{6,8},{7,9},{8,6},{9,7},{10,... | collective-permute-start | bytes 368648 | tf_op jit(solution)/shard_map/ppermute | solution.py:151
  13.5 0.0 collective-permute-done.4.even3
  13.5 1.6 %collective-permute-start.5 = (bf16[4,6,16,128]{3,2,1,0:T(8,128)(2,1)S(1)}, bf16[4,6,16,128]{3,2,1,0:T(8,128)(2,1)S(1)}, u32[]{:S(2)}, u32[]{:S(2)}) collective-permute-start(bf16[4,6,16,128]{3,2,1,0:T(8,128)(2,1)S(1)} %convert_element_type.6), channel_id=1, source_target_pairs={{0,29},{1,4},{2,31},{3,6},{4,1},{5,8},{6,3},{7,10},{8,5},{9,12},{1... | collective-permute-start | bytes 294920 | tf_op jit(solution)/shard_map/ppermute | solution.py:151
  15.2 5.1 %collective-permute-done.5.odd3 = bf16[4,6,16,128]{3,2,1,0:T(8,128)(2,1)S(1)} collective-permute-done((bf16[4,6,16,128]{3,2,1,0:T(8,128)(2,1)S(1)}, bf16[4,6,16,128]{3,2,1,0:T(8,128)(2,1)S(1)}, u32[]{:S(2)}, u32[]{:S(2)}) %collective-permute-start.5) | collective-permute-done | bytes 98336 | tf_op jit(solution)/shard_map/ppermute | solution.py:151
  20.3 0.0 collective-permute-done.even
  20.3 0.0 collective-permute-done.1.odd
  20.3 0.0 collective-permute-done.2.even2
  20.3 0.0 collective-permute-done.3.odd2
  20.3 0.0 copy-done.3
  20.4 0.0 copy-done.4
  20.4 0.0 copy-done.1
  20.4 2.4 %filter_own.1 = bf16[8,6,16,128]{3,2,1,0:T(8,128)(2,1)S(1)} custom-call(bf16[5,6,16,128]{3,2,1,0:T(8,128)(2,1)S(1)} %collective-permute-done.even, bf16[5,6,16,128]{3,2,1,0:T(8,128)(2,1)S(1)} %collective-permute-done.1.odd, bf16[5,6,16,128]{3,2,1,0:T(8,128)(2,1)S(1)} %collective-permute-done.2.even2, ...), custom_call_target="tpu_custom_call" | custom-call | flops 400000000 | bytes 1500000 | tf_op jit(solution)/shard_map/filter_own/pallas_call | solution.py:184
  22.8 19.7 %all_gather.3 = bf16[32,6,16,128]{3,2,1,0:T(8,128)(2,1)S(1)} all-gather(bf16[8,6,16,128]{3,2,1,0:T(8,128)(2,1)S(1)} %filter_own.1), channel_id=1, replica_groups=mesh['z_hi'=4,'core'=2,'z_lo'=2,'x'=4,'y'=4] {'z_hi'}, dimensions={0}, use_global_device_ids=true | all-gather | bytes 983040 | tf_op jit(solution)/shard_map/all_gather | solution.py:203
  42.5 4.9 %collective-permute-start.6 = (bf16[32,6,16,128]{3,2,1,0:T(8,128)(2,1)S(1)}, bf16[32,6,16,128]{3,2,1,0:T(8,128)(2,1)S(1)}, u32[]{:S(2)}, u32[]{:S(2)}) collective-permute-start(bf16[32,6,16,128]{3,2,1,0:T(8,128)(2,1)S(1)} %all_gather.3), channel_id=1, source_target_pairs={{0,32},{32,0},{1,33},{33,1},{2,34},{34,2},{3,35},{35,3},{4,36},{36... | collective-permute-start | bytes 2359304 | tf_op jit(solution)/shard_map/ppermute | solution.py:151
  47.4 0.0 copy-done
  47.4 0.5 convolution_bitcast_fusion.1
  47.9 1.4 %collective-permute-done.6 = bf16[32,6,16,128]{3,2,1,0:T(8,128)(2,1)S(1)} collective-permute-done((bf16[32,6,16,128]{3,2,1,0:T(8,128)(2,1)S(1)}, bf16[32,6,16,128]{3,2,1,0:T(8,128)(2,1)S(1)}, u32[]{:S(2)}, u32[]{:S(2)}) %collective-permute-start.6) | collective-permute-done | bytes 786464 | tf_op jit(solution)/shard_map/ppermute | solution.py:151
  49.3 0.5 convolution_bitcast_fusion
  49.9 0.1 all_to_all.6
  50.0 11.8 %all_to_all.9 = f32[32,1,64]{2,1,0:T(1,128)S(1)} all-to-all(f32[32,1,64]{2,1,0:T(1,128)S(1)} %bitcast.16), channel_id=1, replica_groups=mesh['z_hi'=4,'core'=2,'z_lo'=2,'x'=4,'y'=4] {'z_lo','x','y'}, dimensions={0} | all-to-all | bytes 16384 | tf_op jit(solution)/shard_map/all_to_all | solution.py:220
  61.7 0.1 reduce_sum.9
  61.8 0.6 fusion.4
  (5 shorter events, 0.1 us)
Async XLA Ops:
  0.6 46.7 %copy-start = (bf16[32,6,16,128]{3,2,1,0:T(8,128)(2,1)S(1)}, bf16[32,6,16,128]{3,2,1,0:T(8,128)(2,1)}, u32[]{:S(2)}) copy-start(bf16[32,6,16,128]{3,2,1,0:T(8,128)(2,1)} %param.7) | copy-start | bytes 2359300
  0.6 4.7 %copy-start.2 = (f32[6,16,128]{2,1,0:T(8,128)S(1)}, f32[6,16,128]{2,1,0:T(8,128)}, u32[]{:S(2)}) copy-start(f32[6,16,128]{2,1,0:T(8,128)} %pot.1) | copy-start | bytes 147460
  0.7 19.7 %copy-start.3 = (bf16[96,864]{1,0:T(8,128)(2,1)S(1)}, bf16[96,864]{1,0:T(8,128)(2,1)}, u32[]{:S(2)}) copy-start(bf16[96,864]{1,0:T(8,128)(2,1)} %constant.17.clone.left_ref) | copy-start | bytes 497668
  0.7 19.7 %copy-start.4 = (bf16[256,256]{1,0:T(8,128)(2,1)S(1)}, bf16[256,256]{1,0:T(8,128)(2,1)}, u32[]{:S(2)}) copy-start(bf16[256,256]{1,0:T(8,128)(2,1)} %constant.16.clone.z3_ref) | copy-start | bytes 393220
  1.7 18.7 %copy-start.1 = (f32[4,6,16,128]{3,2,1,0:T(8,128)S(1)}, f32[4,6,16,128]{3,2,1,0:T(8,128)}, u32[]{:S(2)}) copy-start(f32[4,6,16,128]{3,2,1,0:T(8,128)} %s.1) | copy-start | bytes 589828
  1.7 11.8 %collective-permute-start.4 = (bf16[4,6,16,128]{3,2,1,0:T(8,128)(2,1)S(1)}, bf16[4,6,16,128]{3,2,1,0:T(8,128)(2,1)S(1)}, u32[]{:S(2)}, u32[]{:S(2)}) collective-permute-start(bf16[4,6,16,128]{3,2,1,0:T(8,128)(2,1)S(1)} %convert_element_type.6), channel_id=1, source_target_pairs={{0,3},{1,30},{2,5},{3,0},{4,7},{5,2},{6,9},{7,4},{8,11},{9,6},{10,... | collective-permute-start | bytes 294920 | tf_op jit(solution)/shard_map/ppermute | solution.py:151
  5.4 14.9 %collective-permute-start = (bf16[5,6,16,128]{3,2,1,0:T(8,128)(2,1)S(1)}, bf16[5,6,16,128]{3,2,1,0:T(8,128)(2,1)S(1)}, u32[]{:S(2)}, u32[]{:S(2)}) collective-permute-start(bf16[5,6,16,128]{3,2,1,0:T(8,128)(2,1)S(1)} %pad_maximum_fusion), channel_id=1, source_target_pairs={{0,1},{1,0},{2,3},{3,2},{4,5},{5,4},{6,7},{7,6},{8,9},{9,8},{10,11... | collective-permute-start | bytes 368648 | tf_op jit(solution)/shard_map/ppermute | solution.py:151
  8.9 11.4 %collective-permute-start.1 = (bf16[5,6,16,128]{3,2,1,0:T(8,128)(2,1)S(1)}, bf16[5,6,16,128]{3,2,1,0:T(8,128)(2,1)S(1)}, u32[]{:S(2)}, u32[]{:S(2)}) collective-permute-start(bf16[5,6,16,128]{3,2,1,0:T(8,128)(2,1)S(1)} %pad_maximum_fusion), channel_id=1, source_target_pairs={{0,31},{1,2},{2,1},{3,4},{4,3},{5,6},{6,5},{7,8},{8,7},{9,10},{10,... | collective-permute-start | bytes 368648 | tf_op jit(solution)/shard_map/ppermute | solution.py:151
  9.5 10.8 %collective-permute-start.2 = (bf16[5,6,16,128]{3,2,1,0:T(8,128)(2,1)S(1)}, bf16[5,6,16,128]{3,2,1,0:T(8,128)(2,1)S(1)}, u32[]{:S(2)}, u32[]{:S(2)}) collective-permute-start(bf16[5,6,16,128]{3,2,1,0:T(8,128)(2,1)S(1)} %pad_maximum_fusion), channel_id=1, source_target_pairs={{0,2},{1,3},{2,0},{3,1},{4,6},{5,7},{6,4},{7,5},{8,10},{9,11},{10,... | collective-permute-start | bytes 368648 | tf_op jit(solution)/shard_map/ppermute | solution.py:151
  10.8 9.5 %collective-permute-start.3 = (bf16[5,6,16,128]{3,2,1,0:T(8,128)(2,1)S(1)}, bf16[5,6,16,128]{3,2,1,0:T(8,128)(2,1)S(1)}, u32[]{:S(2)}, u32[]{:S(2)}) collective-permute-start(bf16[5,6,16,128]{3,2,1,0:T(8,128)(2,1)S(1)} %pad_maximum_fusion), channel_id=1, source_target_pairs={{0,30},{1,31},{2,4},{3,5},{4,2},{5,3},{6,8},{7,9},{8,6},{9,7},{10,... | collective-permute-start | bytes 368648 | tf_op jit(solution)/shard_map/ppermute | solution.py:151
  13.5 6.8 %collective-permute-start.5 = (bf16[4,6,16,128]{3,2,1,0:T(8,128)(2,1)S(1)}, bf16[4,6,16,128]{3,2,1,0:T(8,128)(2,1)S(1)}, u32[]{:S(2)}, u32[]{:S(2)}) collective-permute-start(bf16[4,6,16,128]{3,2,1,0:T(8,128)(2,1)S(1)} %convert_element_type.6), channel_id=1, source_target_pairs={{0,29},{1,4},{2,31},{3,6},{4,1},{5,8},{6,3},{7,10},{8,5},{9,12},{1... | collective-permute-start | bytes 294920 | tf_op jit(solution)/shard_map/ppermute | solution.py:151
  42.5 6.8 %collective-permute-start.6 = (bf16[32,6,16,128]{3,2,1,0:T(8,128)(2,1)S(1)}, bf16[32,6,16,128]{3,2,1,0:T(8,128)(2,1)S(1)}, u32[]{:S(2)}, u32[]{:S(2)}) collective-permute-start(bf16[32,6,16,128]{3,2,1,0:T(8,128)(2,1)S(1)} %all_gather.3), channel_id=1, source_target_pairs={{0,32},{32,0},{1,33},{33,1},{2,34},{34,2},{3,35},{35,3},{4,36},{36... | collective-permute-start | bytes 2359304 | tf_op jit(solution)/shard_map/ppermute | solution.py:151

commit v5 on v4

--- a/solution.py
+++ b/solution.py
@@ -81,18 +81,25 @@
     return out
 
 
-def along_yz(planes, z3, y3):
-    n = len(planes)
-    field = jnp.concatenate([p[None] for p in planes], 0).reshape(n * CY, CZ)
-    high = field.astype(BF16)
-    low = (field - high.astype(F32)).astype(BF16)
-    z = dot(jnp.concatenate([high, low], 1), z3)
-    z = z[:, :CZ] + z[:, CZ:]
-    out = []
-    for g in range(0, n * CY, ROWS):
-        h, l = high[g : g + ROWS], low[g : g + ROWS]
-        y = dot(y3, jnp.concatenate([h, l, h], 0)) + z[g : g + ROWS]
-        out += [y[i * CY : (i + 1) * CY] for i in range(PLANES)]
+def along_yz(pair, z3, left, exact):
+    out = [[] for _ in pair]
+    for block in range(len(pair[0]) // PLANES):
+        part = slice(block * PLANES, (block + 1) * PLANES)
+        fields = [jnp.concatenate(planes[part], 0) for planes in pair]
+        high = [f.astype(BF16) for f in fields]
+        wide = jnp.concatenate(high, 1)
+        if exact(block):
+            y = dot(left[:, ROWS : 3 * ROWS], jnp.concatenate([wide, wide], 0))
+            z = dot(jnp.concatenate(high, 0), z3[:CZ])
+        else:
+            low = [(f - h.astype(F32)).astype(BF16) for f, h in zip(fields, high)]
+            rest = jnp.concatenate(low, 1)
+            y = dot(left[:, : 3 * ROWS], jnp.concatenate([wide, rest, wide], 0))
+            z = dot(jnp.concatenate([jnp.concatenate(high, 0), jnp.concatenate(low, 0)], 1), z3)
+        z = z[:, :CZ] + z[:, CZ:]
+        for k in range(len(pair)):
+            total = y[:, k * CZ : (k + 1) * CZ] + z[k * ROWS : (k + 1) * ROWS]
+            out[k].extend(total[i * CY : (i + 1) * CY] for i in range(PLANES))
     return out
 
 
@@ -104,7 +111,7 @@
     first_of_pair = place % 2 == 0
     first_of_two = place < 2
     z3, left = z3_ref[...], left_ref[...]
-    y3, xy2 = left[:, : 3 * ROWS], left[:, 3 * ROWS :]
+    xy2 = left[:, 3 * ROWS :]
 
     def sides(i, one, other, flag):
         before, after = [], []
@@ -119,32 +126,40 @@
     raw = b2 + b1 + [pot[x] for x in range(PLANES)] + a1 + a2
     diag = [(DIAG - SHIFT) + v * (1.0 / HALF) for v in raw]
 
-    def turn(planes, weights):
-        inner = planes[W:-W]
-        x = along_x(planes, len(inner))
-        yz = along_yz(inner, z3, y3)
-        return [a + b + d * v for a, b, d, v in zip(x, yz, weights, inner)]
-
-    for i in range(count):
-        b1, a1 = sides(i, even, odd, first_of_pair)
-        b2, a2 = sides(i, even2, odd2, first_of_two)
-        b3, a3 = sides(i, even3, odd3, first_of_pair)
-        field = b3 + b2 + b1 + [s[i, x] for x in range(PLANES)] + a1 + a2 + a3
-        first = turn(field, diag)
-        second = turn(first, diag[W:-W])
+    def turn(pair, weights, exact):
+        inner = [planes[W:-W] for planes in pair]
+        yz = along_yz(inner, z3, left, exact)
+        return [
+            [a + b + d * v for a, b, d, v in zip(along_x(p, len(v_in)), b_in, weights, v_in)]
+            for p, v_in, b_in in zip(pair, inner, yz)
+        ]
+
+    for i in range(0, count, 4):
+        pair = []
+        for j in range(i, i + 4):
+            b1, a1 = sides(j, even, odd, first_of_pair)
+            b2, a2 = sides(j, even2, odd2, first_of_two)
+            b3, a3 = sides(j, even3, odd3, first_of_pair)
+            pair.append(b3 + b2 + b1 + [s[j, x] for x in range(PLANES)] + a1 + a2 + a3)
+        first = turn(pair, diag, lambda block: block != 2)
+        second = turn(first, diag[W:-W], lambda block: False)
         rounded = [
-            (2.0 * t - v).astype(BF16) for t, v in zip(second, field[2 * W : -2 * W])
+            [(2.0 * t - v).astype(BF16) for t, v in zip(turned, field[2 * W : -2 * W])]
+            for turned, field in zip(second, pair)
         ]
-        blocks = [jnp.concatenate(rounded[k * W : (k + 1) * W], 0) for k in range(3)]
-        own = blocks[1]
-        xy = dot(xy2, jnp.concatenate(blocks + blocks, 0))
-        z = dot(own, z3[:CZ])
+        blocks = [[jnp.concatenate(r[k * W : (k + 1) * W], 0) for k in range(3)] for r in rounded]
+        wide = [jnp.concatenate([b[k] for b in blocks], 1) for k in range(3)]
+        xy = dot(xy2, jnp.concatenate(wide + wide, 0))
+        z = dot(jnp.concatenate([b[1] for b in blocks], 0), z3[:CZ])
         z = z[:, :CZ] + z[:, CZ:]
-        for x in range(PLANES):
-            rows = slice(x * CY, (x + 1) * CY)
-            total = xy[rows] + z[rows] + (diag[2 * W + x] + SHIFT) * rounded[W + x].astype(F32)
-            out[i, x] = rounded[W + x]
-            out[count + i, x] = total.astype(BF16)
+        for j in range(4):
+            for x in range(PLANES):
+                rows = slice(x * CY, (x + 1) * CY)
+                total = xy[rows, j * CZ : (j + 1) * CZ] + z[j * ROWS + x * CY : j * ROWS + (x + 1) * CY]
+                own = rounded[j][W + x]
+                total = total + (diag[2 * W + x] + SHIFT) * own.astype(F32)
+                out[i + j, x] = own
+                out[count + i + j, x] = total.astype(BF16)
 
 
 def exchange(array, axes, size, partner):

time: 62.5 us -> 61.7 us (0.987)
  no operation moved by 1% of the time
where the time goes in v5:
time: 61.7 us; the launch traced here: 61.5 us
  blocking collectives  31.3 us (51%)
  starting transfers between devices  18.2 us (29%)
  waiting for transfers between devices  6.54 us (11%)
  Pallas kernels  1.86 us (3%)
  other arithmetic  1.12 us (2%)
  matrix products  1.05 us (2%)
  between operations  0.75 us (1%)
  local copies, waits for them, and re-layouts  0.73 us (1%)
    all_gather x1, blocking collectives, body(): mine = lax.all_gather(both, 'z_hi', axis=0, tiled=True)  19.8 us
    ppermute x7, starting transfers between devices, exchange(): lax.ppermute(array, axes, [(i, partner(i) % size) for i in range(size)])  18.2 us
    all_to_all x1, blocking collectives, body(): parts = lax.all_to_all(term, DOMAIN, 0, 0, tiled=True)  11.5 us
    ppermute x7, waiting for transfers between devices, exchange(): lax.ppermute(array, axes, [(i, partner(i) % size) for i in range(size)])  6.54 us
    pallas_call x1, Pallas kernels, filter_own(): pl.pallas_call(filter_kernel, out_shape=jax.ShapeDtypeStruct((2 * s.shape...  1.86 us
  transfers between devices with their start and end apart: 7, of which 2 were waited for; matrix products, arithmetic and copies ran while one was open for 1% of the time, Pallas kernels for 0%

profile of v5, /device:TPU:1, one launch (start us, length us, event | category | flops | bytes accessed | tf_op | source)
XLA Modules:
  0.0 61.5 jit_solution(14455054316913684240)
XLA Ops:
  0.6 0.0 copy-start
  0.6 0.0 copy-start.2
  0.7 0.0 copy-start.3
  0.7 0.0 copy-start.4
  0.7 1.0 %convert_element_type.6 = bf16[4,6,16,128]{3,2,1,0:T(8,128)(2,1)S(1)} convert(f32[4,6,16,128]{3,2,1,0:T(8,128)} %s.1) | non-fusion elementwise | flops 49152 | bytes 294912 | tf_op jit(solution)/shard_map/convert_element_type | solution.py:212
  1.7 0.0 copy-start.1
  1.7 3.7 %collective-permute-start.4 = (bf16[4,6,16,128]{3,2,1,0:T(8,128)(2,1)S(1)}, bf16[4,6,16,128]{3,2,1,0:T(8,128)(2,1)S(1)}, u32[]{:S(2)}, u32[]{:S(2)}) collective-permute-start(bf16[4,6,16,128]{3,2,1,0:T(8,128)(2,1)S(1)} %convert_element_type.6), channel_id=1, source_target_pairs={{0,3},{1,30},{2,5},{3,0},{4,7},{5,2},{6,9},{7,4},{8,11},{9,6},{10,... | collective-permute-start | bytes 294920 | tf_op jit(solution)/shard_map/ppermute | solution.py:166
  5.4 0.0 copy-done.2
  5.4 3.5 %collective-permute-start = (bf16[5,6,16,128]{3,2,1,0:T(8,128)(2,1)S(1)}, bf16[5,6,16,128]{3,2,1,0:T(8,128)(2,1)S(1)}, u32[]{:S(2)}, u32[]{:S(2)}) collective-permute-start(bf16[5,6,16,128]{3,2,1,0:T(8,128)(2,1)S(1)} %pad_maximum_fusion), channel_id=1, source_target_pairs={{0,1},{1,0},{2,3},{3,2},{4,5},{5,4},{6,7},{7,6},{8,9},{9,8},{10,11... | collective-permute-start | bytes 368648 | tf_op jit(solution)/shard_map/ppermute | solution.py:166
  8.9 0.6 %collective-permute-start.1 = (bf16[5,6,16,128]{3,2,1,0:T(8,128)(2,1)S(1)}, bf16[5,6,16,128]{3,2,1,0:T(8,128)(2,1)S(1)}, u32[]{:S(2)}, u32[]{:S(2)}) collective-permute-start(bf16[5,6,16,128]{3,2,1,0:T(8,128)(2,1)S(1)} %pad_maximum_fusion), channel_id=1, source_target_pairs={{0,31},{1,2},{2,1},{3,4},{4,3},{5,6},{6,5},{7,8},{8,7},{9,10},{10,... | collective-permute-start | bytes 368648 | tf_op jit(solution)/shard_map/ppermute | solution.py:166
  9.5 1.3 %collective-permute-start.2 = (bf16[5,6,16,128]{3,2,1,0:T(8,128)(2,1)S(1)}, bf16[5,6,16,128]{3,2,1,0:T(8,128)(2,1)S(1)}, u32[]{:S(2)}, u32[]{:S(2)}) collective-permute-start(bf16[5,6,16,128]{3,2,1,0:T(8,128)(2,1)S(1)} %pad_maximum_fusion), channel_id=1, source_target_pairs={{0,2},{1,3},{2,0},{3,1},{4,6},{5,7},{6,4},{7,5},{8,10},{9,11},{10,... | collective-permute-start | bytes 368648 | tf_op jit(solution)/shard_map/ppermute | solution.py:166
  10.8 2.8 %collective-permute-start.3 = (bf16[5,6,16,128]{3,2,1,0:T(8,128)(2,1)S(1)}, bf16[5,6,16,128]{3,2,1,0:T(8,128)(2,1)S(1)}, u32[]{:S(2)}, u32[]{:S(2)}) collective-permute-start(bf16[5,6,16,128]{3,2,1,0:T(8,128)(2,1)S(1)} %pad_maximum_fusion), channel_id=1, source_target_pairs={{0,30},{1,31},{2,4},{3,5},{4,2},{5,3},{6,8},{7,9},{8,6},{9,7},{10,... | collective-permute-start | bytes 368648 | tf_op jit(solution)/shard_map/ppermute | solution.py:166
  13.5 0.0 collective-permute-done.4.even3
  13.5 1.6 %collective-permute-start.5 = (bf16[4,6,16,128]{3,2,1,0:T(8,128)(2,1)S(1)}, bf16[4,6,16,128]{3,2,1,0:T(8,128)(2,1)S(1)}, u32[]{:S(2)}, u32[]{:S(2)}) collective-permute-start(bf16[4,6,16,128]{3,2,1,0:T(8,128)(2,1)S(1)} %convert_element_type.6), channel_id=1, source_target_pairs={{0,29},{1,4},{2,31},{3,6},{4,1},{5,8},{6,3},{7,10},{8,5},{9,12},{1... | collective-permute-start | bytes 294920 | tf_op jit(solution)/shard_map/ppermute | solution.py:166
  15.2 5.1 %collective-permute-done.5.odd3 = bf16[4,6,16,128]{3,2,1,0:T(8,128)(2,1)S(1)} collective-permute-done((bf16[4,6,16,128]{3,2,1,0:T(8,128)(2,1)S(1)}, bf16[4,6,16,128]{3,2,1,0:T(8,128)(2,1)S(1)}, u32[]{:S(2)}, u32[]{:S(2)}) %collective-permute-start.5) | collective-permute-done | bytes 98336 | tf_op jit(solution)/shard_map/ppermute | solution.py:166
  20.3 0.0 collective-permute-done.even
  20.3 0.0 collective-permute-done.1.odd
  20.3 0.0 collective-permute-done.2.even2
  20.3 0.0 collective-permute-done.3.odd2
  20.3 0.0 copy-done.3
  20.4 0.0 copy-done.4
  20.4 0.0 copy-done.1
  20.4 1.9 %filter_own.1 = bf16[8,6,16,128]{3,2,1,0:T(8,128)(2,1)S(1)} custom-call(bf16[5,6,16,128]{3,2,1,0:T(8,128)(2,1)S(1)} %collective-permute-done.even, bf16[5,6,16,128]{3,2,1,0:T(8,128)(2,1)S(1)} %collective-permute-done.1.odd, bf16[5,6,16,128]{3,2,1,0:T(8,128)(2,1)S(1)} %collective-permute-done.2.even2, ...), custom_call_target="tpu_custom_call" | custom-call | flops 400000000 | bytes 1500000 | tf_op jit(solution)/shard_map/filter_own/pallas_call | solution.py:199
  22.2 19.8 %all_gather.3 = bf16[32,6,16,128]{3,2,1,0:T(8,128)(2,1)S(1)} all-gather(bf16[8,6,16,128]{3,2,1,0:T(8,128)(2,1)S(1)} %filter_own.1), channel_id=1, replica_groups=mesh['z_hi'=4,'core'=2,'z_lo'=2,'x'=4,'y'=4] {'z_hi'}, dimensions={0}, use_global_device_ids=true | all-gather | bytes 983040 | tf_op jit(solution)/shard_map/all_gather | solution.py:218
  42.0 4.8 %collective-permute-start.6 = (bf16[32,6,16,128]{3,2,1,0:T(8,128)(2,1)S(1)}, bf16[32,6,16,128]{3,2,1,0:T(8,128)(2,1)S(1)}, u32[]{:S(2)}, u32[]{:S(2)}) collective-permute-start(bf16[32,6,16,128]{3,2,1,0:T(8,128)(2,1)S(1)} %all_gather.3), channel_id=1, source_target_pairs={{0,32},{32,0},{1,33},{33,1},{2,34},{34,2},{3,35},{35,3},{4,36},{36... | collective-permute-start | bytes 2359304 | tf_op jit(solution)/shard_map/ppermute | solution.py:166
  46.8 0.0 copy-done
  46.8 0.5 convolution_bitcast_fusion.1
  47.4 1.4 %collective-permute-done.6 = bf16[32,6,16,128]{3,2,1,0:T(8,128)(2,1)S(1)} collective-permute-done((bf16[32,6,16,128]{3,2,1,0:T(8,128)(2,1)S(1)}, bf16[32,6,16,128]{3,2,1,0:T(8,128)(2,1)S(1)}, u32[]{:S(2)}, u32[]{:S(2)}) %collective-permute-start.6) | collective-permute-done | bytes 786464 | tf_op jit(solution)/shard_map/ppermute | solution.py:166
  48.7 0.5 convolution_bitcast_fusion
  49.3 0.1 all_to_all.6
  49.4 11.5 %all_to_all.9 = f32[32,1,64]{2,1,0:T(1,128)S(1)} all-to-all(f32[32,1,64]{2,1,0:T(1,128)S(1)} %bitcast.16), channel_id=1, replica_groups=mesh['z_hi'=4,'core'=2,'z_lo'=2,'x'=4,'y'=4] {'z_lo','x','y'}, dimensions={0} | all-to-all | bytes 16384 | tf_op jit(solution)/shard_map/all_to_all | solution.py:235
  60.9 0.1 reduce_sum.9
  60.9 0.6 fusion.4
  (5 shorter events, 0.1 us)
Async XLA Ops:
  0.6 46.2 %copy-start = (bf16[32,6,16,128]{3,2,1,0:T(8,128)(2,1)S(1)}, bf16[32,6,16,128]{3,2,1,0:T(8,128)(2,1)}, u32[]{:S(2)}) copy-start(bf16[32,6,16,128]{3,2,1,0:T(8,128)(2,1)} %param.7) | copy-start | bytes 2359300
  0.6 4.7 %copy-start.2 = (f32[6,16,128]{2,1,0:T(8,128)S(1)}, f32[6,16,128]{2,1,0:T(8,128)}, u32[]{:S(2)}) copy-start(f32[6,16,128]{2,1,0:T(8,128)} %pot.1) | copy-start | bytes 147460
  0.7 19.7 %copy-start.3 = (bf16[96,864]{1,0:T(8,128)(2,1)S(1)}, bf16[96,864]{1,0:T(8,128)(2,1)}, u32[]{:S(2)}) copy-start(bf16[96,864]{1,0:T(8,128)(2,1)} %constant.17.clone.left_ref) | copy-start | bytes 497668
  0.7 19.7 %copy-start.4 = (bf16[256,256]{1,0:T(8,128)(2,1)S(1)}, bf16[256,256]{1,0:T(8,128)(2,1)}, u32[]{:S(2)}) copy-start(bf16[256,256]{1,0:T(8,128)(2,1)} %constant.16.clone.z3_ref) | copy-start | bytes 393220
  1.7 18.7 %copy-start.1 = (f32[4,6,16,128]{3,2,1,0:T(8,128)S(1)}, f32[4,6,16,128]{3,2,1,0:T(8,128)}, u32[]{:S(2)}) copy-start(f32[4,6,16,128]{3,2,1,0:T(8,128)} %s.1) | copy-start | bytes 589828
  1.7 11.8 %collective-permute-start.4 = (bf16[4,6,16,128]{3,2,1,0:T(8,128)(2,1)S(1)}, bf16[4,6,16,128]{3,2,1,0:T(8,128)(2,1)S(1)}, u32[]{:S(2)}, u32[]{:S(2)}) collective-permute-start(bf16[4,6,16,128]{3,2,1,0:T(8,128)(2,1)S(1)} %convert_element_type.6), channel_id=1, source_target_pairs={{0,3},{1,30},{2,5},{3,0},{4,7},{5,2},{6,9},{7,4},{8,11},{9,6},{10,... | collective-permute-start | bytes 294920 | tf_op jit(solution)/shard_map/ppermute | solution.py:166
  5.4 14.9 %collective-permute-start = (bf16[5,6,16,128]{3,2,1,0:T(8,128)(2,1)S(1)}, bf16[5,6,16,128]{3,2,1,0:T(8,128)(2,1)S(1)}, u32[]{:S(2)}, u32[]{:S(2)}) collective-permute-start(bf16[5,6,16,128]{3,2,1,0:T(8,128)(2,1)S(1)} %pad_maximum_fusion), channel_id=1, source_target_pairs={{0,1},{1,0},{2,3},{3,2},{4,5},{5,4},{6,7},{7,6},{8,9},{9,8},{10,11... | collective-permute-start | bytes 368648 | tf_op jit(solution)/shard_map/ppermute | solution.py:166
  8.9 11.4 %collective-permute-start.1 = (bf16[5,6,16,128]{3,2,1,0:T(8,128)(2,1)S(1)}, bf16[5,6,16,128]{3,2,1,0:T(8,128)(2,1)S(1)}, u32[]{:S(2)}, u32[]{:S(2)}) collective-permute-start(bf16[5,6,16,128]{3,2,1,0:T(8,128)(2,1)S(1)} %pad_maximum_fusion), channel_id=1, source_target_pairs={{0,31},{1,2},{2,1},{3,4},{4,3},{5,6},{6,5},{7,8},{8,7},{9,10},{10,... | collective-permute-start | bytes 368648 | tf_op jit(solution)/shard_map/ppermute | solution.py:166
  9.5 10.8 %collective-permute-start.2 = (bf16[5,6,16,128]{3,2,1,0:T(8,128)(2,1)S(1)}, bf16[5,6,16,128]{3,2,1,0:T(8,128)(2,1)S(1)}, u32[]{:S(2)}, u32[]{:S(2)}) collective-permute-start(bf16[5,6,16,128]{3,2,1,0:T(8,128)(2,1)S(1)} %pad_maximum_fusion), channel_id=1, source_target_pairs={{0,2},{1,3},{2,0},{3,1},{4,6},{5,7},{6,4},{7,5},{8,10},{9,11},{10,... | collective-permute-start | bytes 368648 | tf_op jit(solution)/shard_map/ppermute | solution.py:166
  10.8 9.5 %collective-permute-start.3 = (bf16[5,6,16,128]{3,2,1,0:T(8,128)(2,1)S(1)}, bf16[5,6,16,128]{3,2,1,0:T(8,128)(2,1)S(1)}, u32[]{:S(2)}, u32[]{:S(2)}) collective-permute-start(bf16[5,6,16,128]{3,2,1,0:T(8,128)(2,1)S(1)} %pad_maximum_fusion), channel_id=1, source_target_pairs={{0,30},{1,31},{2,4},{3,5},{4,2},{5,3},{6,8},{7,9},{8,6},{9,7},{10,... | collective-permute-start | bytes 368648 | tf_op jit(solution)/shard_map/ppermute | solution.py:166
  13.5 6.8 %collective-permute-start.5 = (bf16[4,6,16,128]{3,2,1,0:T(8,128)(2,1)S(1)}, bf16[4,6,16,128]{3,2,1,0:T(8,128)(2,1)S(1)}, u32[]{:S(2)}, u32[]{:S(2)}) collective-permute-start(bf16[4,6,16,128]{3,2,1,0:T(8,128)(2,1)S(1)} %convert_element_type.6), channel_id=1, source_target_pairs={{0,29},{1,4},{2,31},{3,6},{4,1},{5,8},{6,3},{7,10},{8,5},{9,12},{1... | collective-permute-start | bytes 294920 | tf_op jit(solution)/shard_map/ppermute | solution.py:166
  42.0 6.7 %collective-permute-start.6 = (bf16[32,6,16,128]{3,2,1,0:T(8,128)(2,1)S(1)}, bf16[32,6,16,128]{3,2,1,0:T(8,128)(2,1)S(1)}, u32[]{:S(2)}, u32[]{:S(2)}) collective-permute-start(bf16[32,6,16,128]{3,2,1,0:T(8,128)(2,1)S(1)} %all_gather.3), channel_id=1, source_target_pairs={{0,32},{32,0},{1,33},{33,1},{2,34},{34,2},{3,35},{35,3},{4,36},{36... | collective-permute-start | bytes 2359304 | tf_op jit(solution)/shard_map/ppermute | solution.py:166

commit v6 on v5

--- a/solution.py
+++ b/solution.py
@@ -103,8 +103,40 @@
     return out
 
 
+def sides(i, one, other, flag):
+    before, after = [], []
+    for x in range(PLANES):
+        a, b = one[i, x].astype(F32), other[i, x].astype(F32)
+        before.append(jnp.where(flag, b, a))
+        after.append(jnp.where(flag, a, b))
+    return before, after
+
+
+def weights(values):
+    return [(DIAG - SHIFT) + v * (1.0 / HALF) for v in values]
+
+
+def near_kernel(even, odd, s, pot, z3_ref, left_ref, out):
+    count = s.shape[0]
+    flag = lax.axis_index("y") % 2 == 0
+    b1, a1 = sides(count, even, odd, flag)
+    diag = weights(b1 + [pot[x] for x in range(PLANES)] + a1)
+    fields = []
+    for i in range(count):
+        b1, a1 = sides(i, even, odd, flag)
+        fields.append(b1 + [s[i, x] for x in range(PLANES)] + a1)
+    yz = along_yz(fields, z3_ref[...], left_ref[...], lambda block: block != 1)
+    for i in range(count):
+        x_terms = along_x(fields[i], PLANES)
+        for p in range(3 * PLANES):
+            total = yz[i][p] + diag[p] * fields[i][p]
+            if W <= p < W + PLANES:
+                total = total + x_terms[p - W]
+            out[i, p] = total
+
+
 def filter_kernel(
-    even, odd, even2, odd2, even3, odd3, s, pot, z3_ref, left_ref, out
+    even, odd, even2, odd2, even3, odd3, s, pot, near, z3_ref, left_ref, out
 ):
     count = s.shape[0]
     place = lax.axis_index("y")
@@ -113,53 +145,53 @@
     z3, left = z3_ref[...], left_ref[...]
     xy2 = left[:, 3 * ROWS :]
 
-    def sides(i, one, other, flag):
-        before, after = [], []
-        for x in range(PLANES):
-            a, b = one[i, x].astype(F32), other[i, x].astype(F32)
-            before.append(jnp.where(flag, b, a))
-            after.append(jnp.where(flag, a, b))
-        return before, after
-
     b1, a1 = sides(count, even, odd, first_of_pair)
     b2, a2 = sides(count, even2, odd2, first_of_two)
-    raw = b2 + b1 + [pot[x] for x in range(PLANES)] + a1 + a2
-    diag = [(DIAG - SHIFT) + v * (1.0 / HALF) for v in raw]
-
-    def turn(pair, weights, exact):
-        inner = [planes[W:-W] for planes in pair]
-        yz = along_yz(inner, z3, left, exact)
-        return [
-            [a + b + d * v for a, b, d, v in zip(along_x(p, len(v_in)), b_in, weights, v_in)]
-            for p, v_in, b_in in zip(pair, inner, yz)
-        ]
-
-    for i in range(0, count, 4):
-        pair = []
-        for j in range(i, i + 4):
-            b1, a1 = sides(j, even, odd, first_of_pair)
-            b2, a2 = sides(j, even2, odd2, first_of_two)
-            b3, a3 = sides(j, even3, odd3, first_of_pair)
-            pair.append(b3 + b2 + b1 + [s[j, x] for x in range(PLANES)] + a1 + a2 + a3)
-        first = turn(pair, diag, lambda block: block != 2)
-        second = turn(first, diag[W:-W], lambda block: False)
-        rounded = [
-            [(2.0 * t - v).astype(BF16) for t, v in zip(turned, field[2 * W : -2 * W])]
-            for turned, field in zip(second, pair)
-        ]
-        blocks = [[jnp.concatenate(r[k * W : (k + 1) * W], 0) for k in range(3)] for r in rounded]
-        wide = [jnp.concatenate([b[k] for b in blocks], 1) for k in range(3)]
-        xy = dot(xy2, jnp.concatenate(wide + wide, 0))
-        z = dot(jnp.concatenate([b[1] for b in blocks], 0), z3[:CZ])
-        z = z[:, :CZ] + z[:, CZ:]
-        for j in range(4):
-            for x in range(PLANES):
-                rows = slice(x * CY, (x + 1) * CY)
-                total = xy[rows, j * CZ : (j + 1) * CZ] + z[j * ROWS + x * CY : j * ROWS + (x + 1) * CY]
-                own = rounded[j][W + x]
-                total = total + (diag[2 * W + x] + SHIFT) * own.astype(F32)
-                out[i + j, x] = own
-                out[count + i + j, x] = total.astype(BF16)
+    diag = weights(b2 + b1 + [pot[x] for x in range(PLANES)] + a1 + a2)
+
+    fields, outer = [], []
+    for i in range(count):
+        b1, a1 = sides(i, even, odd, first_of_pair)
+        b2, a2 = sides(i, even2, odd2, first_of_two)
+        b3, a3 = sides(i, even3, odd3, first_of_pair)
+        fields.append(b3 + b2 + b1 + [s[i, x] for x in range(PLANES)] + a1 + a2 + a3)
+        outer.append(b2 + a2)
+    yz = along_yz(outer, z3, left, lambda block: True)
+    first = []
+    for i in range(count):
+        planes = []
+        for p in range(5 * PLANES):
+            block = p // PLANES
+            if block in (0, 4):
+                k = p if block == 0 else p - 3 * PLANES
+                total = yz[i][k] + diag[p] * fields[i][p + W]
+            else:
+                total = near[i, p - PLANES]
+            if block != 2:
+                total = total + along_x(fields[i][p : p + 2 * W + 1], 1)[0]
+            planes.append(total)
+        first.append(planes)
+    inner = [planes[W:-W] for planes in first]
+    yz = along_yz(inner, z3, left, lambda block: False)
+    rounded = []
+    for i in range(count):
+        x_terms = along_x(first[i], 3 * PLANES)
+        turned = [a + b + d * v for a, b, d, v in zip(x_terms, yz[i], diag[W:-W], inner[i])]
+        own = fields[i][2 * W : -2 * W]
+        rounded.append([(2.0 * t - v).astype(BF16) for t, v in zip(turned, own)])
+    blocks = [[jnp.concatenate(r[k * W : (k + 1) * W], 0) for k in range(3)] for r in rounded]
+    wide = [jnp.concatenate([b[k] for b in blocks], 1) for k in range(3)]
+    xy = dot(xy2, jnp.concatenate(wide + wide, 0))
+    z = dot(jnp.concatenate([b[1] for b in blocks], 0), z3[:CZ])
+    z = z[:, :CZ] + z[:, CZ:]
+    for j in range(count):
+        for x in range(PLANES):
+            rows = slice(x * CY, (x + 1) * CY)
+            total = xy[rows, j * CZ : (j + 1) * CZ] + z[j * ROWS + x * CY : j * ROWS + (x + 1) * CY]
+            own = rounded[j][W + x]
+            total = total + (diag[2 * W + x] + SHIFT) * own.astype(F32)
+            out[j, x] = own
+            out[count + j, x] = total.astype(BF16)
 
 
 def exchange(array, axes, size, partner):
@@ -194,17 +226,30 @@
     return [pl.BlockSpec(memory_space=pltpu.VMEM)] * n
 
 
-def filter_own(pairs, twos, threes, s, pot):
+def near_terms(pairs, s, pot):
+    count, planes, *cells = s.shape
+    return pl.pallas_call(
+        near_kernel,
+        out_shape=jax.ShapeDtypeStruct((count, 3 * planes, *cells), F32),
+        in_specs=vmem(6),
+        out_specs=vmem()[0],
+        compiler_params=pltpu.CompilerParams(vmem_limit_bytes=16 << 20),
+        cost_estimate=pl.CostEstimate(flops=4000000000, bytes_accessed=1_500_000, transcendentals=0),
+        name="near_terms",
+    )(*pairs, s, pot, jnp.asarray(Z3), jnp.asarray(LEFT))
+
+
+def filter_own(pairs, twos, threes, s, pot, near):
     constants = [jnp.asarray(m) for m in (Z3, LEFT)]
     return pl.pallas_call(
         filter_kernel,
         out_shape=jax.ShapeDtypeStruct((2 * s.shape[0], *s.shape[1:]), BF16),
-        in_specs=vmem(10),
+        in_specs=vmem(11),
         out_specs=vmem()[0],
         compiler_params=pltpu.CompilerParams(vmem_limit_bytes=16 << 20),
-        cost_estimate=pl.CostEstimate(flops=400_000_000, bytes_accessed=1_500_000, transcendentals=0),
+        cost_estimate=pl.CostEstimate(flops=5_000_000_000, bytes_accessed=1_500_000, transcendentals=0),
         name="filter_own",
-    )(*pairs, *twos, *threes, s, pot, *constants)
+    )(*pairs, *twos, *threes, s, pot, near, *constants)
 
 
 def body(states, potential, slab):
@@ -214,21 +259,22 @@
     pairs = even_pairs(near), odd_pairs(near)
     twos = even_twos(near), odd_twos(near)
     threes = even_threes(low), odd_threes(low)
-    both = filter_own(pairs, twos, threes, states, potential)
+    near = near_terms(pairs, states, potential)
+    other_slab = lax.optimization_barrier(exchange(slab, "core", 2, lambda i: i ^ 1))
+    both = filter_own(pairs, twos, threes, states, potential, near)
     mine = lax.all_gather(both, "z_hi", axis=0, tiled=True)
-    theirs = lax.optimization_barrier(exchange(mine, "core", 2, lambda i: i ^ 1))
-
     n = slab.shape[0]
 
     def products(block):
-        return lax.dot_general(
-            block.reshape(block.shape[0], -1),
-            slab.reshape(n, -1),
+        out = lax.dot_general(
+            mine.reshape(mine.shape[0], -1),
+            block.reshape(n, -1),
             (((1,), (1,)), ((), ())),
             preferred_element_type=F32,
         )
-
-    out = lax.optimization_barrier((products(mine), products(theirs)))
+        return lax.optimization_barrier(out)
+
+    out = products(slab), exchange(products(other_slab), "core", 2, lambda i: i ^ 1)
     pair = jnp.stack(out).reshape(2, 4, 2, count, n) * (1.0 / np.sqrt(np.float32(CELLS)))
     pair = jnp.where(lax.axis_index("core") == 1, jnp.flip(pair, 0), pair)
     term = jnp.transpose(pair, (1, 0, 3, 2, 4)).reshape(32, 2 * n)

time: 61.7 us -> 61.5 us (level)
  blocking collectives: 31.3 us -> 33.8 us
  starting transfers between devices: 18.2 us -> 16.4 us
  waiting for transfers between devices: 6.54 us -> 5.39 us
    all_gather x1, blocking collectives: 19.8 us -> 21.6 us  [body(): mine = lax.all_gather(both, 'z_hi', axis=0, tiled=True)]
    ppermute x7 -> x8, starting transfers between devices: 18.2 us -> 16.4 us  [exchange(): lax.ppermute(array, axes, [(i, partner(i) % size) for i in range(size)])]
    ppermute x7 -> x8, waiting for transfers between devices: 6.54 us -> 5.39 us  [exchange(): lax.ppermute(array, axes, [(i, partner(i) % size) for i in range(size)])]
    all_to_all x1, blocking collectives: 11.5 us -> 12.3 us  [body(): parts = lax.all_to_all(term, DOMAIN, 0, 0, tiled=True)]
  transfers between devices with their start and end apart: 7 -> 8, of which waited for: 2 -> 2; matrix products, arithmetic and copies ran while one was open for 1% -> 1% of each run, Pallas kernels for 0% -> 3%
where the time goes in v6:
time: 61.5 us; the launch traced here: 61.4 us
  blocking collectives  33.8 us (55%)
  starting transfers between devices  16.4 us (27%)
  waiting for transfers between devices  5.39 us (9%)
  Pallas kernels  2.12 us (3%)
  other arithmetic  1.08 us (2%)
  matrix products  1.06 us (2%)
  local copies, waits for them, and re-layouts  0.73 us (1%)
  between operations  0.73 us (1%)
    all_gather x1, blocking collectives, body(): mine = lax.all_gather(both, 'z_hi', axis=0, tiled=True)  21.6 us
    ppermute x8, starting transfers between devices, exchange(): lax.ppermute(array, axes, [(i, partner(i) % size) for i in range(size)])  16.4 us
    all_to_all x1, blocking collectives, body(): parts = lax.all_to_all(term, DOMAIN, 0, 0, tiled=True)  12.3 us
    ppermute x8, waiting for transfers between devices, exchange(): lax.ppermute(array, axes, [(i, partner(i) % size) for i in range(size)])  5.39 us
    pallas_call x1, Pallas kernels, filter_own(): pl.pallas_call(filter_kernel, out_shape=jax.ShapeDtypeStruct((2 * s.shape...  1.6 us
  transfers between devices with their start and end apart: 8, of which 2 were waited for; matrix products, arithmetic and copies ran while one was open for 1% of the time, Pallas kernels for 3%

profile of v6, /device:TPU:1, one launch (start us, length us, event | category | flops | bytes accessed | tf_op | source)
XLA Modules:
  0.0 61.4 jit_solution(313334856378301436)
XLA Ops:
  0.6 0.0 copy-start.1
  0.6 0.0 copy-start.2
  0.7 1.0 %convert_element_type.6 = bf16[4,6,16,128]{3,2,1,0:T(8,128)(2,1)S(1)} convert(f32[4,6,16,128]{3,2,1,0:T(8,128)} %s.3) | non-fusion elementwise | flops 49152 | bytes 294912 | tf_op jit(solution)/shard_map/convert_element_type | solution.py:257
  1.6 0.0 copy-done.1
  1.6 0.0 copy-start
  1.7 0.0 copy-start.3
  1.7 2.2 %collective-permute-start = (bf16[5,6,16,128]{3,2,1,0:T(8,128)(2,1)S(1)}, bf16[5,6,16,128]{3,2,1,0:T(8,128)(2,1)S(1)}, u32[]{:S(2)}, u32[]{:S(2)}) collective-permute-start(bf16[5,6,16,128]{3,2,1,0:T(8,128)(2,1)S(1)} %pad_maximum_fusion), channel_id=1, source_target_pairs={{0,1},{1,0},{2,3},{3,2},{4,5},{5,4},{6,7},{7,6},{8,9},{9,8},{10,11... | collective-permute-start | bytes 368648 | tf_op jit(solution)/shard_map/ppermute | solution.py:198
  3.9 5.4 %collective-permute-start.1 = (bf16[5,6,16,128]{3,2,1,0:T(8,128)(2,1)S(1)}, bf16[5,6,16,128]{3,2,1,0:T(8,128)(2,1)S(1)}, u32[]{:S(2)}, u32[]{:S(2)}) collective-permute-start(bf16[5,6,16,128]{3,2,1,0:T(8,128)(2,1)S(1)} %pad_maximum_fusion), channel_id=1, source_target_pairs={{0,31},{1,2},{2,1},{3,4},{4,3},{5,6},{6,5},{7,8},{8,7},{9,10},{10,... | collective-permute-start | bytes 368648 | tf_op jit(solution)/shard_map/ppermute | solution.py:198
  9.4 0.0 collective-permute-start.2
  9.4 3.2 %collective-permute-start.3 = (bf16[5,6,16,128]{3,2,1,0:T(8,128)(2,1)S(1)}, bf16[5,6,16,128]{3,2,1,0:T(8,128)(2,1)S(1)}, u32[]{:S(2)}, u32[]{:S(2)}) collective-permute-start(bf16[5,6,16,128]{3,2,1,0:T(8,128)(2,1)S(1)} %pad_maximum_fusion), channel_id=1, source_target_pairs={{0,30},{1,31},{2,4},{3,5},{4,2},{5,3},{6,8},{7,9},{8,6},{9,7},{10,... | collective-permute-start | bytes 368648 | tf_op jit(solution)/shard_map/ppermute | solution.py:198
  12.6 0.0 collective-permute-start.4
  12.6 0.0 collective-permute-done.even
  12.6 1.0 %collective-permute-start.5 = (bf16[4,6,16,128]{3,2,1,0:T(8,128)(2,1)S(1)}, bf16[4,6,16,128]{3,2,1,0:T(8,128)(2,1)S(1)}, u32[]{:S(2)}, u32[]{:S(2)}) collective-permute-start(bf16[4,6,16,128]{3,2,1,0:T(8,128)(2,1)S(1)} %convert_element_type.6), channel_id=1, source_target_pairs={{0,29},{1,4},{2,31},{3,6},{4,1},{5,8},{6,3},{7,10},{8,5},{9,12},{1... | collective-permute-start | bytes 294920 | tf_op jit(solution)/shard_map/ppermute | solution.py:198
  13.6 0.0 collective-permute-done.1.odd
  13.7 2.1 %collective-permute-start.6 = (bf16[32,6,16,128]{3,2,1,0:T(8,128)(2,1)}, bf16[32,6,16,128]{3,2,1,0:T(8,128)(2,1)S(1)}, u32[]{:S(2)}, u32[]{:S(2)}) collective-permute-start(bf16[32,6,16,128]{3,2,1,0:T(8,128)(2,1)} %param.7), channel_id=1, source_target_pairs={{0,32},{32,0},{1,33},{33,1},{2,34},{34,2},{3,35},{35,3},{4,36},{36... | collective-permute-start | bytes 2359304 | tf_op jit(solution)/shard_map/ppermute | solution.py:198
  15.7 0.0 copy-done.2
  15.7 0.0 copy-done
  15.7 0.0 copy-done.3
  15.7 0.5 near_terms.1.near
  16.3 4.6 %collective-permute-done.4.even3 = bf16[4,6,16,128]{3,2,1,0:T(8,128)(2,1)S(1)} collective-permute-done((bf16[4,6,16,128]{3,2,1,0:T(8,128)(2,1)S(1)}, bf16[4,6,16,128]{3,2,1,0:T(8,128)(2,1)S(1)}, u32[]{:S(2)}, u32[]{:S(2)}) %collective-permute-start.4) | collective-permute-done | bytes 98336 | tf_op jit(solution)/shard_map/ppermute | solution.py:198
  20.8 0.0 collective-permute-done.5.odd3
  20.8 0.0 collective-permute-done.2.even2
  20.8 0.0 collective-permute-done.3.odd2
  20.8 1.6 %filter_own.1 = bf16[8,6,16,128]{3,2,1,0:T(8,128)(2,1)S(1)} custom-call(bf16[5,6,16,128]{3,2,1,0:T(8,128)(2,1)S(1)} %collective-permute-done.even, bf16[5,6,16,128]{3,2,1,0:T(8,128)(2,1)S(1)} %collective-permute-done.1.odd, bf16[5,6,16,128]{3,2,1,0:T(8,128)(2,1)S(1)} %collective-permute-done.2.even2, ...), custom_call_target="tpu_custom_call" | custom-call | flops 5000000000 | bytes 1500000 | tf_op jit(solution)/shard_map/filter_own/pallas_call | solution.py:244
  22.4 0.0 copy-start.4
  22.4 21.6 %all_gather.3 = bf16[32,6,16,128]{3,2,1,0:T(8,128)(2,1)S(1)} all-gather(bf16[8,6,16,128]{3,2,1,0:T(8,128)(2,1)S(1)} %filter_own.1), channel_id=1, replica_groups=mesh['z_hi'=4,'core'=2,'z_lo'=2,'x'=4,'y'=4] {'z_hi'}, dimensions={0}, use_global_device_ids=true | all-gather | bytes 983040 | tf_op jit(solution)/shard_map/all_gather | solution.py:265
  44.0 0.0 copy-done.4
  44.0 0.5 convolution_bitcast_fusion.1
  44.5 0.0 collective-permute-done.6
  44.5 0.5 convolution_bitcast_fusion
  45.1 2.4 %collective-permute-start.7 = (f32[32,32]{1,0:T(8,128)S(1)}, f32[32,32]{1,0:T(8,128)S(1)}, u32[]{:S(2)}, u32[]{:S(2)}) collective-permute-start(f32[32,32]{1,0:T(8,128)S(1)} %convolution_bitcast_fusion), channel_id=1, source_target_pairs={{0,32},{32,0},{1,33},{33,1},{2,34},{34,2},{3,35},{35,3},{4,36},{36... | collective-permute-start | bytes 12296 | tf_op jit(solution)/shard_map/ppermute | solution.py:198
  47.5 0.8 %collective-permute-done.7 = f32[32,32]{1,0:T(8,128)S(1)} collective-permute-done((f32[32,32]{1,0:T(8,128)S(1)}, f32[32,32]{1,0:T(8,128)S(1)}, u32[]{:S(2)}, u32[]{:S(2)}) %collective-permute-start.7) | collective-permute-done | bytes 4128 | tf_op jit(solution)/shard_map/ppermute | solution.py:198
  48.4 0.1 all_to_all.6
  48.5 12.3 %all_to_all.9 = f32[32,1,64]{2,1,0:T(1,128)S(1)} all-to-all(f32[32,1,64]{2,1,0:T(1,128)S(1)} %bitcast.16), channel_id=1, replica_groups=mesh['z_hi'=4,'core'=2,'z_lo'=2,'x'=4,'y'=4] {'z_lo','x','y'}, dimensions={0} | all-to-all | bytes 16384 | tf_op jit(solution)/shard_map/all_to_all | solution.py:281
  60.8 0.1 reduce_sum.9
  60.8 0.6 fusion.4
  (5 shorter events, 0.1 us)
Async XLA Ops:
  0.6 1.0 %copy-start.1 = (f32[6,16,128]{2,1,0:T(8,128)S(1)}, f32[6,16,128]{2,1,0:T(8,128)}, u32[]{:S(2)}) copy-start(f32[6,16,128]{2,1,0:T(8,128)} %pot.3) | copy-start | bytes 147460
  0.6 15.1 %copy-start.2 = (bf16[96,864]{1,0:T(8,128)(2,1)S(1)}, bf16[96,864]{1,0:T(8,128)(2,1)}, u32[]{:S(2)}) copy-start(bf16[96,864]{1,0:T(8,128)(2,1)} %constant.17.clone.left_ref) | copy-start | bytes 497668
  1.6 14.1 %copy-start = (f32[4,6,16,128]{3,2,1,0:T(8,128)S(1)}, f32[4,6,16,128]{3,2,1,0:T(8,128)}, u32[]{:S(2)}) copy-start(f32[4,6,16,128]{3,2,1,0:T(8,128)} %s.3) | copy-start | bytes 589828
  1.7 14.1 %copy-start.3 = (bf16[256,256]{1,0:T(8,128)(2,1)S(1)}, bf16[256,256]{1,0:T(8,128)(2,1)}, u32[]{:S(2)}) copy-start(bf16[256,256]{1,0:T(8,128)(2,1)} %constant.16.clone.z3_ref) | copy-start | bytes 393220
  1.7 10.9 %collective-permute-start = (bf16[5,6,16,128]{3,2,1,0:T(8,128)(2,1)S(1)}, bf16[5,6,16,128]{3,2,1,0:T(8,128)(2,1)S(1)}, u32[]{:S(2)}, u32[]{:S(2)}) collective-permute-start(bf16[5,6,16,128]{3,2,1,0:T(8,128)(2,1)S(1)} %pad_maximum_fusion), channel_id=1, source_target_pairs={{0,1},{1,0},{2,3},{3,2},{4,5},{5,4},{6,7},{7,6},{8,9},{9,8},{10,11... | collective-permute-start | bytes 368648 | tf_op jit(solution)/shard_map/ppermute | solution.py:198
  3.9 9.7 %collective-permute-start.1 = (bf16[5,6,16,128]{3,2,1,0:T(8,128)(2,1)S(1)}, bf16[5,6,16,128]{3,2,1,0:T(8,128)(2,1)S(1)}, u32[]{:S(2)}, u32[]{:S(2)}) collective-permute-start(bf16[5,6,16,128]{3,2,1,0:T(8,128)(2,1)S(1)} %pad_maximum_fusion), channel_id=1, source_target_pairs={{0,31},{1,2},{2,1},{3,4},{4,3},{5,6},{6,5},{7,8},{8,7},{9,10},{10,... | collective-permute-start | bytes 368648 | tf_op jit(solution)/shard_map/ppermute | solution.py:198
  9.4 11.4 %collective-permute-start.2 = (bf16[5,6,16,128]{3,2,1,0:T(8,128)(2,1)S(1)}, bf16[5,6,16,128]{3,2,1,0:T(8,128)(2,1)S(1)}, u32[]{:S(2)}, u32[]{:S(2)}) collective-permute-start(bf16[5,6,16,128]{3,2,1,0:T(8,128)(2,1)S(1)} %pad_maximum_fusion), channel_id=1, source_target_pairs={{0,2},{1,3},{2,0},{3,1},{4,6},{5,7},{6,4},{7,5},{8,10},{9,11},{10,... | collective-permute-start | bytes 368648 | tf_op jit(solution)/shard_map/ppermute | solution.py:198
  9.4 11.4 %collective-permute-start.3 = (bf16[5,6,16,128]{3,2,1,0:T(8,128)(2,1)S(1)}, bf16[5,6,16,128]{3,2,1,0:T(8,128)(2,1)S(1)}, u32[]{:S(2)}, u32[]{:S(2)}) collective-permute-start(bf16[5,6,16,128]{3,2,1,0:T(8,128)(2,1)S(1)} %pad_maximum_fusion), channel_id=1, source_target_pairs={{0,30},{1,31},{2,4},{3,5},{4,2},{5,3},{6,8},{7,9},{8,6},{9,7},{10,... | collective-permute-start | bytes 368648 | tf_op jit(solution)/shard_map/ppermute | solution.py:198
  12.6 8.2 %collective-permute-start.4 = (bf16[4,6,16,128]{3,2,1,0:T(8,128)(2,1)S(1)}, bf16[4,6,16,128]{3,2,1,0:T(8,128)(2,1)S(1)}, u32[]{:S(2)}, u32[]{:S(2)}) collective-permute-start(bf16[4,6,16,128]{3,2,1,0:T(8,128)(2,1)S(1)} %convert_element_type.6), channel_id=1, source_target_pairs={{0,3},{1,30},{2,5},{3,0},{4,7},{5,2},{6,9},{7,4},{8,11},{9,6},{10,... | collective-permute-start | bytes 294920 | tf_op jit(solution)/shard_map/ppermute | solution.py:198
  12.6 8.2 %collective-permute-start.5 = (bf16[4,6,16,128]{3,2,1,0:T(8,128)(2,1)S(1)}, bf16[4,6,16,128]{3,2,1,0:T(8,128)(2,1)S(1)}, u32[]{:S(2)}, u32[]{:S(2)}) collective-permute-start(bf16[4,6,16,128]{3,2,1,0:T(8,128)(2,1)S(1)} %convert_element_type.6), channel_id=1, source_target_pairs={{0,29},{1,4},{2,31},{3,6},{4,1},{5,8},{6,3},{7,10},{8,5},{9,12},{1... | collective-permute-start | bytes 294920 | tf_op jit(solution)/shard_map/ppermute | solution.py:198
  13.7 30.9 %collective-permute-start.6 = (bf16[32,6,16,128]{3,2,1,0:T(8,128)(2,1)}, bf16[32,6,16,128]{3,2,1,0:T(8,128)(2,1)S(1)}, u32[]{:S(2)}, u32[]{:S(2)}) collective-permute-start(bf16[32,6,16,128]{3,2,1,0:T(8,128)(2,1)} %param.7), channel_id=1, source_target_pairs={{0,32},{32,0},{1,33},{33,1},{2,34},{34,2},{3,35},{35,3},{4,36},{36... | collective-permute-start | bytes 2359304 | tf_op jit(solution)/shard_map/ppermute | solution.py:198
  22.4 21.6 %copy-start.4 = (bf16[32,6,16,128]{3,2,1,0:T(8,128)(2,1)S(1)}, bf16[32,6,16,128]{3,2,1,0:T(8,128)(2,1)}, u32[]{:S(2)}) copy-start(bf16[32,6,16,128]{3,2,1,0:T(8,128)(2,1)} %param.7) | copy-start | bytes 2359300
  45.1 3.3 %collective-permute-start.7 = (f32[32,32]{1,0:T(8,128)S(1)}, f32[32,32]{1,0:T(8,128)S(1)}, u32[]{:S(2)}, u32[]{:S(2)}) collective-permute-start(f32[32,32]{1,0:T(8,128)S(1)} %convolution_bitcast_fusion), channel_id=1, source_target_pairs={{0,32},{32,0},{1,33},{33,1},{2,34},{34,2},{3,35},{35,3},{4,36},{36... | collective-permute-start | bytes 12296 | tf_op jit(solution)/shard_map/ppermute | solution.py:198

commit v7 on v6

--- a/solution.py
+++ b/solution.py
@@ -260,21 +260,20 @@
     twos = even_twos(near), odd_twos(near)
     threes = even_threes(low), odd_threes(low)
     near = near_terms(pairs, states, potential)
-    other_slab = lax.optimization_barrier(exchange(slab, "core", 2, lambda i: i ^ 1))
+    other_slab = exchange(slab, "core", 2, lambda i: i ^ 1)
+    slabs = jnp.concatenate([slab, other_slab], axis=0)
     both = filter_own(pairs, twos, threes, states, potential, near)
     mine = lax.all_gather(both, "z_hi", axis=0, tiled=True)
     n = slab.shape[0]
 
-    def products(block):
-        out = lax.dot_general(
-            mine.reshape(mine.shape[0], -1),
-            block.reshape(n, -1),
-            (((1,), (1,)), ((), ())),
-            preferred_element_type=F32,
-        )
-        return lax.optimization_barrier(out)
-
-    out = products(slab), exchange(products(other_slab), "core", 2, lambda i: i ^ 1)
+    out = lax.dot_general(
+        mine.reshape(mine.shape[0], -1),
+        slabs.reshape(2 * n, -1),
+        (((1,), (1,)), ((), ())),
+        preferred_element_type=F32,
+    )
+    out = lax.optimization_barrier(out)
+    out = out[:, :n], exchange(out[:, n:], "core", 2, lambda i: i ^ 1)
     pair = jnp.stack(out).reshape(2, 4, 2, count, n) * (1.0 / np.sqrt(np.float32(CELLS)))
     pair = jnp.where(lax.axis_index("core") == 1, jnp.flip(pair, 0), pair)
     term = jnp.transpose(pair, (1, 0, 3, 2, 4)).reshape(32, 2 * n)

time: 61.5 us -> 61.6 us (level)
  blocking collectives: 33.8 us -> 31.4 us
  starting transfers between devices: 16.4 us -> 18.6 us
  local copies, waits for them, and re-layouts: 0.73 us -> 2.29 us
  waiting for transfers between devices: 5.39 us -> 3.83 us
  other arithmetic: 1.08 us -> 1.83 us
    ppermute x8, starting transfers between devices: 16.4 us -> 18.6 us  [exchange(): lax.ppermute(array, axes, [(i, partner(i) % size) for i in range(size)])]
    ppermute x8, waiting for transfers between devices: 5.39 us -> 3.83 us  [exchange(): lax.ppermute(array, axes, [(i, partner(i) % size) for i in range(size)])]
    unnamed x11 -> x10, local copies, waits for them, and re-layouts: 0.04 us -> 1.52 us
    all_to_all x1, blocking collectives: 12.3 us -> 11 us  [body(): parts = lax.all_to_all(term, DOMAIN, 0, 0, tiled=True)]
    all_gather x1, blocking collectives: 21.6 us -> 20.4 us  [body(): mine = lax.all_gather(both, 'z_hi', axis=0, tiled=True)]
    broadcast_in_dim x1, other arithmetic: 0.01 us -> 0.81 us  [body(): near = jnp.concatenate([low, potential.astype(BF16)[None]], axis=0)]
  transfers between devices with their start and end apart: 8 -> 8, of which waited for: 2 -> 2; matrix products, arithmetic and copies ran while one was open for 1% -> 2% of each run, Pallas kernels for 3% -> 3%
where the time goes in v7:
time: 61.6 us; the launch traced here: 61.4 us
  blocking collectives  31.4 us (51%)
  starting transfers between devices  18.6 us (30%)
  waiting for transfers between devices  3.83 us (6%)
  local copies, waits for them, and re-layouts  2.29 us (4%)
  Pallas kernels  2.1 us (3%)
  other arithmetic  1.83 us (3%)
  between operations  0.7 us (1%)
    all_gather x1, blocking collectives, body(): mine = lax.all_gather(both, 'z_hi', axis=0, tiled=True)  20.4 us
    ppermute x8, starting transfers between devices, exchange(): lax.ppermute(array, axes, [(i, partner(i) % size) for i in range(size)])  18.6 us
    all_to_all x1, blocking collectives, body(): parts = lax.all_to_all(term, DOMAIN, 0, 0, tiled=True)  11 us
    ppermute x8, waiting for transfers between devices, exchange(): lax.ppermute(array, axes, [(i, partner(i) % size) for i in range(size)])  3.83 us
    pallas_call x1, Pallas kernels, filter_own(): pl.pallas_call(filter_kernel, out_shape=jax.ShapeDtypeStruct((2 * s.shape...  1.6 us
    unnamed x10, local copies, waits for them, and re-layouts  1.52 us
  transfers between devices with their start and end apart: 8, of which 2 were waited for; matrix products, arithmetic and copies ran while one was open for 2% of the time, Pallas kernels for 3%

profile of v7, /device:TPU:1, one launch (start us, length us, event | category | flops | bytes accessed | tf_op | source)
XLA Modules:
  0.0 61.4 jit_solution(18111748320606447565)
XLA Ops:
  0.6 0.9 %convert_element_type.6 = bf16[4,6,16,128]{3,2,1,0:T(8,128)(2,1)S(1)} convert(f32[4,6,16,128]{3,2,1,0:T(8,128)} %s.3) | non-fusion elementwise | flops 49152 | bytes 294912 | tf_op jit(solution)/shard_map/convert_element_type | solution.py:257
  1.6 0.8 %convert_bitcast_fusion = bf16[1,6,16,128]{3,2,1,0:T(8,128)(2,1)S(1)} fusion(f32[6,16,128]{2,1,0:T(8,128)} %pot.3), kind=kLoop, calls=%fused_computation.8 | loop fusion | flops 12288 | bytes 73728 | tf_op jit(solution)/shard_map/broadcast_in_dim | solution.py:258
  2.4 2.2 %collective-permute-start = (bf16[5,6,16,128]{3,2,1,0:T(8,128)(2,1)S(1)}, bf16[5,6,16,128]{3,2,1,0:T(8,128)(2,1)S(1)}, u32[]{:S(2)}, u32[]{:S(2)}) collective-permute-start(bf16[5,6,16,128]{3,2,1,0:T(8,128)(2,1)S(1)} %pad_maximum_fusion), channel_id=1, source_target_pairs={{0,1},{1,0},{2,3},{3,2},{4,5},{5,4},{6,7},{7,6},{8,9},{9,8},{10,11... | collective-permute-start | bytes 368648 | tf_op jit(solution)/shard_map/ppermute | solution.py:198
  4.6 5.4 %collective-permute-start.1 = (bf16[5,6,16,128]{3,2,1,0:T(8,128)(2,1)S(1)}, bf16[5,6,16,128]{3,2,1,0:T(8,128)(2,1)S(1)}, u32[]{:S(2)}, u32[]{:S(2)}) collective-permute-start(bf16[5,6,16,128]{3,2,1,0:T(8,128)(2,1)S(1)} %pad_maximum_fusion), channel_id=1, source_target_pairs={{0,31},{1,2},{2,1},{3,4},{4,3},{5,6},{6,5},{7,8},{8,7},{9,10},{10,... | collective-permute-start | bytes 368648 | tf_op jit(solution)/shard_map/ppermute | solution.py:198
  10.1 0.0 collective-permute-start.2
  10.1 3.2 %collective-permute-start.3 = (bf16[5,6,16,128]{3,2,1,0:T(8,128)(2,1)S(1)}, bf16[5,6,16,128]{3,2,1,0:T(8,128)(2,1)S(1)}, u32[]{:S(2)}, u32[]{:S(2)}) collective-permute-start(bf16[5,6,16,128]{3,2,1,0:T(8,128)(2,1)S(1)} %pad_maximum_fusion), channel_id=1, source_target_pairs={{0,30},{1,31},{2,4},{3,5},{4,2},{5,3},{6,8},{7,9},{8,6},{9,7},{10,... | collective-permute-start | bytes 368648 | tf_op jit(solution)/shard_map/ppermute | solution.py:198
  13.3 0.0 collective-permute-start.4
  13.3 0.0 copy-start
  13.3 0.0 copy-start.1
  13.3 0.0 copy-start.2
  13.3 0.0 copy-start.3
  13.3 1.5 %copy.16 = bf16[32,6,16,128]{3,0,2,1:T(8,128)(2,1)S(1)} copy(bf16[32,6,16,128]{3,2,1,0:T(8,128)(2,1)} %param.7) | data formatting | bytes 1572864 | tf_op args[2]
  14.8 0.0 collective-permute-done.even
  14.8 1.1 %collective-permute-start.5 = (bf16[4,6,16,128]{3,2,1,0:T(8,128)(2,1)S(1)}, bf16[4,6,16,128]{3,2,1,0:T(8,128)(2,1)S(1)}, u32[]{:S(2)}, u32[]{:S(2)}) collective-permute-start(bf16[4,6,16,128]{3,2,1,0:T(8,128)(2,1)S(1)} %convert_element_type.6), channel_id=1, source_target_pairs={{0,29},{1,4},{2,31},{3,6},{4,1},{5,8},{6,3},{7,10},{8,5},{9,12},{1... | collective-permute-start | bytes 294920 | tf_op jit(solution)/shard_map/ppermute | solution.py:198
  15.9 0.0 collective-permute-done.1.odd
  15.9 2.1 %collective-permute-start.6 = (bf16[32,6,16,128]{3,0,2,1:T(8,128)(2,1)S(1)}, bf16[32,6,16,128]{3,0,2,1:T(8,128)(2,1)S(1)}, u32[]{:S(2)}, u32[]{:S(2)}) collective-permute-start(bf16[32,6,16,128]{3,0,2,1:T(8,128)(2,1)S(1)} %copy.16), channel_id=1, source_target_pairs={{0,32},{32,0},{1,33},{33,1},{2,34},{34,2},{3,35},{35,3},{4,36},{36... | collective-permute-start | bytes 2359304 | tf_op jit(solution)/shard_map/ppermute | solution.py:198
  18.0 0.0 copy-done
  18.0 0.0 copy-done.1
  18.0 0.0 copy-done.2
  18.0 0.0 copy-done.3
  18.0 0.5 near_terms.1.near
  18.5 3.0 %collective-permute-done.4.even3 = bf16[4,6,16,128]{3,2,1,0:T(8,128)(2,1)S(1)} collective-permute-done((bf16[4,6,16,128]{3,2,1,0:T(8,128)(2,1)S(1)}, bf16[4,6,16,128]{3,2,1,0:T(8,128)(2,1)S(1)}, u32[]{:S(2)}, u32[]{:S(2)}) %collective-permute-start.4) | collective-permute-done | bytes 98336 | tf_op jit(solution)/shard_map/ppermute | solution.py:198
  21.5 0.0 collective-permute-done.5.odd3
  21.5 0.0 collective-permute-done.2.even2
  21.5 0.0 collective-permute-done.3.odd2
  21.5 1.6 %filter_own.1 = bf16[8,6,16,128]{3,2,1,0:T(8,128)(2,1)S(1)} custom-call(bf16[5,6,16,128]{3,2,1,0:T(8,128)(2,1)S(1)} %collective-permute-done.even, bf16[5,6,16,128]{3,2,1,0:T(8,128)(2,1)S(1)} %collective-permute-done.1.odd, bf16[5,6,16,128]{3,2,1,0:T(8,128)(2,1)S(1)} %collective-permute-done.2.even2, ...), custom_call_target="tpu_custom_call" | custom-call | flops 5000000000 | bytes 1500000 | tf_op jit(solution)/shard_map/filter_own/pallas_call | solution.py:244
  23.2 20.4 %all_gather.3 = bf16[32,6,16,128]{3,2,1,0:T(8,128)(2,1)S(1)} all-gather(bf16[8,6,16,128]{3,2,1,0:T(8,128)(2,1)S(1)} %filter_own.1), channel_id=1, replica_groups=mesh['z_hi'=4,'core'=2,'z_lo'=2,'x'=4,'y'=4] {'z_hi'}, dimensions={0}, use_global_device_ids=true | all-gather | bytes 983040 | tf_op jit(solution)/shard_map/all_gather | solution.py:266
  43.5 0.0 collective-permute-done.6
  43.6 0.6 fusion.4
  44.1 0.1 fusion.9
  44.2 4.6 %collective-permute-start.7 = (f32[32,32]{1,0:T(8,128)S(1)}, f32[32,32]{1,0:T(8,128)S(1)}, u32[]{:S(2)}, u32[]{:S(2)}) collective-permute-start(f32[32,32]{1,0:T(8,128)S(1)} %get-tuple-element.2), channel_id=1, source_target_pairs={{0,32},{32,0},{1,33},{33,1},{2,34},{34,2},{3,35},{35,3},{4,36},{36... | collective-permute-start | bytes 12296 | tf_op jit(solution)/shard_map/ppermute | solution.py:198
  48.8 0.8 %collective-permute-done.7 = f32[32,32]{1,0:T(8,128)S(1)} collective-permute-done((f32[32,32]{1,0:T(8,128)S(1)}, f32[32,32]{1,0:T(8,128)S(1)}, u32[]{:S(2)}, u32[]{:S(2)}) %collective-permute-start.7) | collective-permute-done | bytes 4128 | tf_op jit(solution)/shard_map/ppermute | solution.py:198
  49.7 0.1 all_to_all.6
  49.8 11.0 %all_to_all.9 = f32[32,1,64]{2,1,0:T(1,128)S(1)} all-to-all(f32[32,1,64]{2,1,0:T(1,128)S(1)} %bitcast.12), channel_id=1, replica_groups=mesh['z_hi'=4,'core'=2,'z_lo'=2,'x'=4,'y'=4] {'z_lo','x','y'}, dimensions={0} | all-to-all | bytes 16384 | tf_op jit(solution)/shard_map/all_to_all | solution.py:280
  60.7 0.1 reduce_sum.9
  60.8 0.6 fusion.10
  (4 shorter events, 0.1 us)
Async XLA Ops:
  2.4 12.4 %collective-permute-start = (bf16[5,6,16,128]{3,2,1,0:T(8,128)(2,1)S(1)}, bf16[5,6,16,128]{3,2,1,0:T(8,128)(2,1)S(1)}, u32[]{:S(2)}, u32[]{:S(2)}) collective-permute-start(bf16[5,6,16,128]{3,2,1,0:T(8,128)(2,1)S(1)} %pad_maximum_fusion), channel_id=1, source_target_pairs={{0,1},{1,0},{2,3},{3,2},{4,5},{5,4},{6,7},{7,6},{8,9},{9,8},{10,11... | collective-permute-start | bytes 368648 | tf_op jit(solution)/shard_map/ppermute | solution.py:198
  4.6 11.3 %collective-permute-start.1 = (bf16[5,6,16,128]{3,2,1,0:T(8,128)(2,1)S(1)}, bf16[5,6,16,128]{3,2,1,0:T(8,128)(2,1)S(1)}, u32[]{:S(2)}, u32[]{:S(2)}) collective-permute-start(bf16[5,6,16,128]{3,2,1,0:T(8,128)(2,1)S(1)} %pad_maximum_fusion), channel_id=1, source_target_pairs={{0,31},{1,2},{2,1},{3,4},{4,3},{5,6},{6,5},{7,8},{8,7},{9,10},{10,... | collective-permute-start | bytes 368648 | tf_op jit(solution)/shard_map/ppermute | solution.py:198
  10.1 11.5 %collective-permute-start.2 = (bf16[5,6,16,128]{3,2,1,0:T(8,128)(2,1)S(1)}, bf16[5,6,16,128]{3,2,1,0:T(8,128)(2,1)S(1)}, u32[]{:S(2)}, u32[]{:S(2)}) collective-permute-start(bf16[5,6,16,128]{3,2,1,0:T(8,128)(2,1)S(1)} %pad_maximum_fusion), channel_id=1, source_target_pairs={{0,2},{1,3},{2,0},{3,1},{4,6},{5,7},{6,4},{7,5},{8,10},{9,11},{10,... | collective-permute-start | bytes 368648 | tf_op jit(solution)/shard_map/ppermute | solution.py:198
  10.1 11.5 %collective-permute-start.3 = (bf16[5,6,16,128]{3,2,1,0:T(8,128)(2,1)S(1)}, bf16[5,6,16,128]{3,2,1,0:T(8,128)(2,1)S(1)}, u32[]{:S(2)}, u32[]{:S(2)}) collective-permute-start(bf16[5,6,16,128]{3,2,1,0:T(8,128)(2,1)S(1)} %pad_maximum_fusion), channel_id=1, source_target_pairs={{0,30},{1,31},{2,4},{3,5},{4,2},{5,3},{6,8},{7,9},{8,6},{9,7},{10,... | collective-permute-start | bytes 368648 | tf_op jit(solution)/shard_map/ppermute | solution.py:198
  13.3 8.2 %collective-permute-start.4 = (bf16[4,6,16,128]{3,2,1,0:T(8,128)(2,1)S(1)}, bf16[4,6,16,128]{3,2,1,0:T(8,128)(2,1)S(1)}, u32[]{:S(2)}, u32[]{:S(2)}) collective-permute-start(bf16[4,6,16,128]{3,2,1,0:T(8,128)(2,1)S(1)} %convert_element_type.6), channel_id=1, source_target_pairs={{0,3},{1,30},{2,5},{3,0},{4,7},{5,2},{6,9},{7,4},{8,11},{9,6},{10,... | collective-permute-start | bytes 294920 | tf_op jit(solution)/shard_map/ppermute | solution.py:198
  13.3 4.7 %copy-start = (f32[4,6,16,128]{3,2,1,0:T(8,128)S(1)}, f32[4,6,16,128]{3,2,1,0:T(8,128)}, u32[]{:S(2)}) copy-start(f32[4,6,16,128]{3,2,1,0:T(8,128)} %s.3) | copy-start | bytes 589828
  13.3 4.7 %copy-start.1 = (f32[6,16,128]{2,1,0:T(8,128)S(1)}, f32[6,16,128]{2,1,0:T(8,128)}, u32[]{:S(2)}) copy-start(f32[6,16,128]{2,1,0:T(8,128)} %pot.3) | copy-start | bytes 147460
  13.3 4.7 %copy-start.2 = (bf16[96,864]{1,0:T(8,128)(2,1)S(1)}, bf16[96,864]{1,0:T(8,128)(2,1)}, u32[]{:S(2)}) copy-start(bf16[96,864]{1,0:T(8,128)(2,1)} %constant.17.clone.left_ref) | copy-start | bytes 497668
  13.3 4.7 %copy-start.3 = (bf16[256,256]{1,0:T(8,128)(2,1)S(1)}, bf16[256,256]{1,0:T(8,128)(2,1)}, u32[]{:S(2)}) copy-start(bf16[256,256]{1,0:T(8,128)(2,1)} %constant.16.clone.z3_ref) | copy-start | bytes 393220
  14.8 6.7 %collective-permute-start.5 = (bf16[4,6,16,128]{3,2,1,0:T(8,128)(2,1)S(1)}, bf16[4,6,16,128]{3,2,1,0:T(8,128)(2,1)S(1)}, u32[]{:S(2)}, u32[]{:S(2)}) collective-permute-start(bf16[4,6,16,128]{3,2,1,0:T(8,128)(2,1)S(1)} %convert_element_type.6), channel_id=1, source_target_pairs={{0,29},{1,4},{2,31},{3,6},{4,1},{5,8},{6,3},{7,10},{8,5},{9,12},{1... | collective-permute-start | bytes 294920 | tf_op jit(solution)/shard_map/ppermute | solution.py:198
  15.9 27.6 %collective-permute-start.6 = (bf16[32,6,16,128]{3,0,2,1:T(8,128)(2,1)S(1)}, bf16[32,6,16,128]{3,0,2,1:T(8,128)(2,1)S(1)}, u32[]{:S(2)}, u32[]{:S(2)}) collective-permute-start(bf16[32,6,16,128]{3,0,2,1:T(8,128)(2,1)S(1)} %copy.16), channel_id=1, source_target_pairs={{0,32},{32,0},{1,33},{33,1},{2,34},{34,2},{3,35},{35,3},{4,36},{36... | collective-permute-start | bytes 2359304 | tf_op jit(solution)/shard_map/ppermute | solution.py:198
  44.2 5.4 %collective-permute-start.7 = (f32[32,32]{1,0:T(8,128)S(1)}, f32[32,32]{1,0:T(8,128)S(1)}, u32[]{:S(2)}, u32[]{:S(2)}) collective-permute-start(f32[32,32]{1,0:T(8,128)S(1)} %get-tuple-element.2), channel_id=1, source_target_pairs={{0,32},{32,0},{1,33},{33,1},{2,34},{34,2},{3,35},{35,3},{4,36},{36... | collective-permute-start | bytes 12296 | tf_op jit(solution)/shard_map/ppermute | solution.py:198

commit v8 on v6

--- a/solution.py
+++ b/solution.py
@@ -172,7 +172,7 @@
             planes.append(total)
         first.append(planes)
     inner = [planes[W:-W] for planes in first]
-    yz = along_yz(inner, z3, left, lambda block: False)
+    yz = along_yz(inner, z3, left, lambda block: block != 1)
     rounded = []
     for i in range(count):
         x_terms = along_x(first[i], 3 * PLANES)

time: 61.5 us -> 61.6 us (level)
  no operation moved by 1% of the time
where the time goes in v8:
time: 61.6 us; the launch traced here: 61.4 us
  blocking collectives  34.3 us (56%)
  starting transfers between devices  16.1 us (26%)
  waiting for transfers between devices  5.39 us (9%)
  Pallas kernels  2.04 us (3%)
  other arithmetic  1.08 us (2%)
  matrix products  1.06 us (2%)
  local copies, waits for them, and re-layouts  0.73 us (1%)
  between operations  0.73 us (1%)
    all_gather x1, blocking collectives, body(): mine = lax.all_gather(both, 'z_hi', axis=0, tiled=True)  21.6 us
    ppermute x8, starting transfers between devices, exchange(): lax.ppermute(array, axes, [(i, partner(i) % size) for i in range(size)])  16.1 us
    all_to_all x1, blocking collectives, body(): parts = lax.all_to_all(term, DOMAIN, 0, 0, tiled=True)  12.6 us
    ppermute x8, waiting for transfers between devices, exchange(): lax.ppermute(array, axes, [(i, partner(i) % size) for i in range(size)])  5.39 us
    pallas_call x1, Pallas kernels, filter_own(): pl.pallas_call(filter_kernel, out_shape=jax.ShapeDtypeStruct((2 * s.shape...  1.53 us
  transfers between devices with their start and end apart: 8, of which 2 were waited for; matrix products, arithmetic and copies ran while one was open for 1% of the time, Pallas kernels for 3%

profile of v8, /device:TPU:1, one launch (start us, length us, event | category | flops | bytes accessed | tf_op | source)
XLA Modules:
  0.0 61.4 jit_solution(11487241536619037044)
XLA Ops:
  0.6 0.0 copy-start.1
  0.6 0.0 copy-start.2
  0.7 1.0 %convert_element_type.6 = bf16[4,6,16,128]{3,2,1,0:T(8,128)(2,1)S(1)} convert(f32[4,6,16,128]{3,2,1,0:T(8,128)} %s.3) | non-fusion elementwise | flops 49152 | bytes 294912 | tf_op jit(solution)/shard_map/convert_element_type | solution.py:257
  1.6 0.0 copy-done.1
  1.6 0.0 copy-start
  1.7 0.0 copy-start.3
  1.7 2.2 %collective-permute-start = (bf16[5,6,16,128]{3,2,1,0:T(8,128)(2,1)S(1)}, bf16[5,6,16,128]{3,2,1,0:T(8,128)(2,1)S(1)}, u32[]{:S(2)}, u32[]{:S(2)}) collective-permute-start(bf16[5,6,16,128]{3,2,1,0:T(8,128)(2,1)S(1)} %pad_maximum_fusion), channel_id=1, source_target_pairs={{0,1},{1,0},{2,3},{3,2},{4,5},{5,4},{6,7},{7,6},{8,9},{9,8},{10,11... | collective-permute-start | bytes 368648 | tf_op jit(solution)/shard_map/ppermute | solution.py:198
  3.9 5.4 %collective-permute-start.1 = (bf16[5,6,16,128]{3,2,1,0:T(8,128)(2,1)S(1)}, bf16[5,6,16,128]{3,2,1,0:T(8,128)(2,1)S(1)}, u32[]{:S(2)}, u32[]{:S(2)}) collective-permute-start(bf16[5,6,16,128]{3,2,1,0:T(8,128)(2,1)S(1)} %pad_maximum_fusion), channel_id=1, source_target_pairs={{0,31},{1,2},{2,1},{3,4},{4,3},{5,6},{6,5},{7,8},{8,7},{9,10},{10,... | collective-permute-start | bytes 368648 | tf_op jit(solution)/shard_map/ppermute | solution.py:198
  9.4 0.0 collective-permute-start.2
  9.4 3.2 %collective-permute-start.3 = (bf16[5,6,16,128]{3,2,1,0:T(8,128)(2,1)S(1)}, bf16[5,6,16,128]{3,2,1,0:T(8,128)(2,1)S(1)}, u32[]{:S(2)}, u32[]{:S(2)}) collective-permute-start(bf16[5,6,16,128]{3,2,1,0:T(8,128)(2,1)S(1)} %pad_maximum_fusion), channel_id=1, source_target_pairs={{0,30},{1,31},{2,4},{3,5},{4,2},{5,3},{6,8},{7,9},{8,6},{9,7},{10,... | collective-permute-start | bytes 368648 | tf_op jit(solution)/shard_map/ppermute | solution.py:198
  12.6 0.0 collective-permute-start.4
  12.6 0.0 collective-permute-done.even
  12.6 1.0 %collective-permute-start.5 = (bf16[4,6,16,128]{3,2,1,0:T(8,128)(2,1)S(1)}, bf16[4,6,16,128]{3,2,1,0:T(8,128)(2,1)S(1)}, u32[]{:S(2)}, u32[]{:S(2)}) collective-permute-start(bf16[4,6,16,128]{3,2,1,0:T(8,128)(2,1)S(1)} %convert_element_type.6), channel_id=1, source_target_pairs={{0,29},{1,4},{2,31},{3,6},{4,1},{5,8},{6,3},{7,10},{8,5},{9,12},{1... | collective-permute-start | bytes 294920 | tf_op jit(solution)/shard_map/ppermute | solution.py:198
  13.6 0.0 collective-permute-done.1.odd
  13.7 2.1 %collective-permute-start.6 = (bf16[32,6,16,128]{3,2,1,0:T(8,128)(2,1)}, bf16[32,6,16,128]{3,2,1,0:T(8,128)(2,1)S(1)}, u32[]{:S(2)}, u32[]{:S(2)}) collective-permute-start(bf16[32,6,16,128]{3,2,1,0:T(8,128)(2,1)} %param.7), channel_id=1, source_target_pairs={{0,32},{32,0},{1,33},{33,1},{2,34},{34,2},{3,35},{35,3},{4,36},{36... | collective-permute-start | bytes 2359304 | tf_op jit(solution)/shard_map/ppermute | solution.py:198
  15.7 0.0 copy-done.2
  15.7 0.0 copy-done
  15.7 0.0 copy-done.3
  15.7 0.5 near_terms.1.near
  16.3 4.6 %collective-permute-done.4.even3 = bf16[4,6,16,128]{3,2,1,0:T(8,128)(2,1)S(1)} collective-permute-done((bf16[4,6,16,128]{3,2,1,0:T(8,128)(2,1)S(1)}, bf16[4,6,16,128]{3,2,1,0:T(8,128)(2,1)S(1)}, u32[]{:S(2)}, u32[]{:S(2)}) %collective-permute-start.4) | collective-permute-done | bytes 98336 | tf_op jit(solution)/shard_map/ppermute | solution.py:198
  20.8 0.0 collective-permute-done.5.odd3
  20.8 0.0 collective-permute-done.2.even2
  20.8 0.0 collective-permute-done.3.odd2
  20.8 1.5 %filter_own.1 = bf16[8,6,16,128]{3,2,1,0:T(8,128)(2,1)S(1)} custom-call(bf16[5,6,16,128]{3,2,1,0:T(8,128)(2,1)S(1)} %collective-permute-done.even, bf16[5,6,16,128]{3,2,1,0:T(8,128)(2,1)S(1)} %collective-permute-done.1.odd, bf16[5,6,16,128]{3,2,1,0:T(8,128)(2,1)S(1)} %collective-permute-done.2.even2, ...), custom_call_target="tpu_custom_call" | custom-call | flops 5000000000 | bytes 1500000 | tf_op jit(solution)/shard_map/filter_own/pallas_call | solution.py:244
  22.3 0.0 copy-start.4
  22.4 21.6 %all_gather.3 = bf16[32,6,16,128]{3,2,1,0:T(8,128)(2,1)S(1)} all-gather(bf16[8,6,16,128]{3,2,1,0:T(8,128)(2,1)S(1)} %filter_own.1), channel_id=1, replica_groups=mesh['z_hi'=4,'core'=2,'z_lo'=2,'x'=4,'y'=4] {'z_hi'}, dimensions={0}, use_global_device_ids=true | all-gather | bytes 983040 | tf_op jit(solution)/shard_map/all_gather | solution.py:265
  44.0 0.0 copy-done.4
  44.0 0.5 convolution_bitcast_fusion.1
  44.5 0.0 collective-permute-done.6
  44.5 0.5 convolution_bitcast_fusion
  45.1 2.1 %collective-permute-start.7 = (f32[32,32]{1,0:T(8,128)S(1)}, f32[32,32]{1,0:T(8,128)S(1)}, u32[]{:S(2)}, u32[]{:S(2)}) collective-permute-start(f32[32,32]{1,0:T(8,128)S(1)} %convolution_bitcast_fusion), channel_id=1, source_target_pairs={{0,32},{32,0},{1,33},{33,1},{2,34},{34,2},{3,35},{35,3},{4,36},{36... | collective-permute-start | bytes 12296 | tf_op jit(solution)/shard_map/ppermute | solution.py:198
  47.2 0.8 %collective-permute-done.7 = f32[32,32]{1,0:T(8,128)S(1)} collective-permute-done((f32[32,32]{1,0:T(8,128)S(1)}, f32[32,32]{1,0:T(8,128)S(1)}, u32[]{:S(2)}, u32[]{:S(2)}) %collective-permute-start.7) | collective-permute-done | bytes 4128 | tf_op jit(solution)/shard_map/ppermute | solution.py:198
  48.1 0.1 all_to_all.6
  48.2 12.6 %all_to_all.9 = f32[32,1,64]{2,1,0:T(1,128)S(1)} all-to-all(f32[32,1,64]{2,1,0:T(1,128)S(1)} %bitcast.16), channel_id=1, replica_groups=mesh['z_hi'=4,'core'=2,'z_lo'=2,'x'=4,'y'=4] {'z_lo','x','y'}, dimensions={0} | all-to-all | bytes 16384 | tf_op jit(solution)/shard_map/all_to_all | solution.py:281
  60.8 0.1 reduce_sum.9
  60.8 0.6 fusion.4
  (5 shorter events, 0.1 us)
Async XLA Ops:
  0.6 1.0 %copy-start.1 = (f32[6,16,128]{2,1,0:T(8,128)S(1)}, f32[6,16,128]{2,1,0:T(8,128)}, u32[]{:S(2)}) copy-start(f32[6,16,128]{2,1,0:T(8,128)} %pot.3) | copy-start | bytes 147460
  0.6 15.1 %copy-start.2 = (bf16[96,864]{1,0:T(8,128)(2,1)S(1)}, bf16[96,864]{1,0:T(8,128)(2,1)}, u32[]{:S(2)}) copy-start(bf16[96,864]{1,0:T(8,128)(2,1)} %constant.17.clone.left_ref) | copy-start | bytes 497668
  1.6 14.1 %copy-start = (f32[4,6,16,128]{3,2,1,0:T(8,128)S(1)}, f32[4,6,16,128]{3,2,1,0:T(8,128)}, u32[]{:S(2)}) copy-start(f32[4,6,16,128]{3,2,1,0:T(8,128)} %s.3) | copy-start | bytes 589828
  1.7 14.1 %copy-start.3 = (bf16[256,256]{1,0:T(8,128)(2,1)S(1)}, bf16[256,256]{1,0:T(8,128)(2,1)}, u32[]{:S(2)}) copy-start(bf16[256,256]{1,0:T(8,128)(2,1)} %constant.16.clone.z3_ref) | copy-start | bytes 393220
  1.7 10.9 %collective-permute-start = (bf16[5,6,16,128]{3,2,1,0:T(8,128)(2,1)S(1)}, bf16[5,6,16,128]{3,2,1,0:T(8,128)(2,1)S(1)}, u32[]{:S(2)}, u32[]{:S(2)}) collective-permute-start(bf16[5,6,16,128]{3,2,1,0:T(8,128)(2,1)S(1)} %pad_maximum_fusion), channel_id=1, source_target_pairs={{0,1},{1,0},{2,3},{3,2},{4,5},{5,4},{6,7},{7,6},{8,9},{9,8},{10,11... | collective-permute-start | bytes 368648 | tf_op jit(solution)/shard_map/ppermute | solution.py:198
  3.9 9.7 %collective-permute-start.1 = (bf16[5,6,16,128]{3,2,1,0:T(8,128)(2,1)S(1)}, bf16[5,6,16,128]{3,2,1,0:T(8,128)(2,1)S(1)}, u32[]{:S(2)}, u32[]{:S(2)}) collective-permute-start(bf16[5,6,16,128]{3,2,1,0:T(8,128)(2,1)S(1)} %pad_maximum_fusion), channel_id=1, source_target_pairs={{0,31},{1,2},{2,1},{3,4},{4,3},{5,6},{6,5},{7,8},{8,7},{9,10},{10,... | collective-permute-start | bytes 368648 | tf_op jit(solution)/shard_map/ppermute | solution.py:198
  9.4 11.4 %collective-permute-start.2 = (bf16[5,6,16,128]{3,2,1,0:T(8,128)(2,1)S(1)}, bf16[5,6,16,128]{3,2,1,0:T(8,128)(2,1)S(1)}, u32[]{:S(2)}, u32[]{:S(2)}) collective-permute-start(bf16[5,6,16,128]{3,2,1,0:T(8,128)(2,1)S(1)} %pad_maximum_fusion), channel_id=1, source_target_pairs={{0,2},{1,3},{2,0},{3,1},{4,6},{5,7},{6,4},{7,5},{8,10},{9,11},{10,... | collective-permute-start | bytes 368648 | tf_op jit(solution)/shard_map/ppermute | solution.py:198
  9.4 11.4 %collective-permute-start.3 = (bf16[5,6,16,128]{3,2,1,0:T(8,128)(2,1)S(1)}, bf16[5,6,16,128]{3,2,1,0:T(8,128)(2,1)S(1)}, u32[]{:S(2)}, u32[]{:S(2)}) collective-permute-start(bf16[5,6,16,128]{3,2,1,0:T(8,128)(2,1)S(1)} %pad_maximum_fusion), channel_id=1, source_target_pairs={{0,30},{1,31},{2,4},{3,5},{4,2},{5,3},{6,8},{7,9},{8,6},{9,7},{10,... | collective-permute-start | bytes 368648 | tf_op jit(solution)/shard_map/ppermute | solution.py:198
  12.6 8.2 %collective-permute-start.4 = (bf16[4,6,16,128]{3,2,1,0:T(8,128)(2,1)S(1)}, bf16[4,6,16,128]{3,2,1,0:T(8,128)(2,1)S(1)}, u32[]{:S(2)}, u32[]{:S(2)}) collective-permute-start(bf16[4,6,16,128]{3,2,1,0:T(8,128)(2,1)S(1)} %convert_element_type.6), channel_id=1, source_target_pairs={{0,3},{1,30},{2,5},{3,0},{4,7},{5,2},{6,9},{7,4},{8,11},{9,6},{10,... | collective-permute-start | bytes 294920 | tf_op jit(solution)/shard_map/ppermute | solution.py:198
  12.6 8.2 %collective-permute-start.5 = (bf16[4,6,16,128]{3,2,1,0:T(8,128)(2,1)S(1)}, bf16[4,6,16,128]{3,2,1,0:T(8,128)(2,1)S(1)}, u32[]{:S(2)}, u32[]{:S(2)}) collective-permute-start(bf16[4,6,16,128]{3,2,1,0:T(8,128)(2,1)S(1)} %convert_element_type.6), channel_id=1, source_target_pairs={{0,29},{1,4},{2,31},{3,6},{4,1},{5,8},{6,3},{7,10},{8,5},{9,12},{1... | collective-permute-start | bytes 294920 | tf_op jit(solution)/shard_map/ppermute | solution.py:198
  13.7 30.9 %collective-permute-start.6 = (bf16[32,6,16,128]{3,2,1,0:T(8,128)(2,1)}, bf16[32,6,16,128]{3,2,1,0:T(8,128)(2,1)S(1)}, u32[]{:S(2)}, u32[]{:S(2)}) collective-permute-start(bf16[32,6,16,128]{3,2,1,0:T(8,128)(2,1)} %param.7), channel_id=1, source_target_pairs={{0,32},{32,0},{1,33},{33,1},{2,34},{34,2},{3,35},{35,3},{4,36},{36... | collective-permute-start | bytes 2359304 | tf_op jit(solution)/shard_map/ppermute | solution.py:198
  22.3 21.7 %copy-start.4 = (bf16[32,6,16,128]{3,2,1,0:T(8,128)(2,1)S(1)}, bf16[32,6,16,128]{3,2,1,0:T(8,128)(2,1)}, u32[]{:S(2)}) copy-start(bf16[32,6,16,128]{3,2,1,0:T(8,128)(2,1)} %param.7) | copy-start | bytes 2359300
  45.1 3.0 %collective-permute-start.7 = (f32[32,32]{1,0:T(8,128)S(1)}, f32[32,32]{1,0:T(8,128)S(1)}, u32[]{:S(2)}, u32[]{:S(2)}) collective-permute-start(f32[32,32]{1,0:T(8,128)S(1)} %convolution_bitcast_fusion), channel_id=1, source_target_pairs={{0,32},{32,0},{1,33},{33,1},{2,34},{34,2},{3,35},{35,3},{4,36},{36... | collective-permute-start | bytes 12296 | tf_op jit(solution)/shard_map/ppermute | solution.py:198
